TPU v7x, 32 devices: a whole 2x2x4 slice. The times are simulated.
32 devices in a mesh: row: 4 (over y, x), col: 8 (over z, core).
Axes of the slice: x: 2, y: 2, z: 4, core: 2. Of those that a mesh axis runs over, the one named last changes fastest.
Arguments:
- view_a: bfloat16 [64, 8192], P('col', 'row'), may hold values from -30 to 30
- view_b: bfloat16 [64, 8192], P('row', 'col'), may hold values from -30 to 30
Outputs:
- loss: float32 [], replicated
- grad_a: bfloat16 [64, 8192], P('col', 'row')
- grad_b: bfloat16 [64, 8192], P('row', 'col')
All inputs are finite; a program needn't handle non-finite values.
Results may differ from a plain program's by a relative error of at most 0.0062.
Values may be sent and summed in bfloat16 or wider, within the bound.
No kernel may reach another device: no remote copies, remote signals or barrier semaphores. Data moves between devices by JAX's collectives and lax.ppermute only.
A program may use at most 64 MiB of HBM per device.

v0:
```python
import jax
import jax.numpy as jnp
from jax import lax
from jax.sharding import PartitionSpec as P

off_weight = 0.0051
epsilon = 1e-05


def normalize(values):
    values = values.astype(jnp.float32)
    center = jnp.mean(values, 0)
    spread = jnp.mean(jnp.square(values - center), 0)
    scaled = lax.rsqrt(spread + epsilon)
    return (((values - center) * scaled).astype(jnp.bfloat16), scaled)


def body(view_a, view_b):
    whole_a = lax.all_gather(view_a, "col", axis=0, tiled=True)
    whole_b = lax.all_gather(view_b, "row", axis=0, tiled=True)
    normed_a, scaled_a = normalize(whole_a)
    normed_b, scaled_b = normalize(whole_b)
    count = whole_a.shape[0]
    width_a = whole_a.shape[1]
    width_b = whole_b.shape[1]
    corr = (
        lax.dot_general(
            normed_a, normed_b, (((0,), (0,)), ((), ())), preferred_element_type=jnp.float32
        )
        / count
    )
    rows = lax.axis_index("row") * width_a + lax.iota(jnp.int32, width_a)
    columns = lax.axis_index("col") * width_b + lax.iota(jnp.int32, width_b)
    diag = rows[:, None] == columns[None, :]
    partial_loss = jnp.sum(jnp.where(diag, jnp.square(1.0 - corr), off_weight * jnp.square(corr)))
    weights = jnp.where(diag, 2.0 * (corr - 1.0), 2.0 * off_weight * corr).astype(jnp.bfloat16)
    term_a = lax.dot_general(
        normed_b, weights, (((1,), (1,)), ((), ())), preferred_element_type=jnp.float32
    )
    term_b = jnp.dot(normed_a, weights, preferred_element_type=jnp.float32)
    summed_a = lax.psum_scatter(term_a, "col", scatter_dimension=0, tiled=True)
    summed_b = lax.psum_scatter(term_b, "row", scatter_dimension=0, tiled=True)
    share_a = summed_a.shape[0]
    share_b = summed_b.shape[0]
    mine_a = lax.dynamic_slice_in_dim(normed_a, lax.axis_index("col") * share_a, share_a, 0).astype(
        jnp.float32
    )
    mine_b = lax.dynamic_slice_in_dim(normed_b, lax.axis_index("row") * share_b, share_b, 0).astype(
        jnp.float32
    )
    first_a, second_a = lax.psum((jnp.sum(summed_a, 0), jnp.sum(summed_a * mine_a, 0)), "col")
    first_b, second_b = lax.psum((jnp.sum(summed_b, 0), jnp.sum(summed_b * mine_b, 0)), "row")
    grad_a = (scaled_a * (summed_a - first_a / count - mine_a * (second_a / count))).astype(
        jnp.bfloat16
    )
    grad_b = (scaled_b * (summed_b - first_b / count - mine_b * (second_b / count))).astype(
        jnp.bfloat16
    )
    total = lax.psum(partial_loss, ("row", "col"))
    loss = total / (width_a * lax.axis_size("row"))
    return (loss, grad_a, grad_b)


def solution(mesh):
    in_specs = (P("col", "row"), P("row", "col"))
    out_specs = (P(), P("col", "row"), P("row", "col"))
    return jax.shard_map(body, mesh=mesh, in_specs=in_specs, out_specs=out_specs, check_vma=False)
```

profile of v0, /device:TPU:0, one launch (start us, length us, event | category | flops | bytes accessed | tf_op | source)
XLA Modules:
  0.0 135.4 jit_solution(3026154325210010621)
XLA Ops:
  7.2 0.0 reduce-scatter.5.cloned.1.call-start
  7.2 10.1 %all_gather.7 = bf16[64,1024]{1,0:T(8,128)(2,1)S(1)} all-gather(bf16[16,1024]{1,0:T(8,128)(2,1)} %param.3), channel_id=1, replica_groups=mesh['row'=4,'col'=8] {'row'}, dimensions={0}, use_global_device_ids=true | all-gather | bytes 163840 | tf_op jit(solution)/shard_map/all_gather | solution.py:20
  17.5 14.7 %all_gather.6 = bf16[64,2048]{1,0:T(8,128)(2,1)S(1)} all-gather(bf16[8,2048]{1,0:T(8,128)(2,1)} %param.2), channel_id=1, replica_groups=mesh['row'=4,'col'=8] {'col'}, dimensions={0}, use_global_device_ids=true | all-gather | bytes 294912 | tf_op jit(solution)/shard_map/all_gather | solution.py:19
  32.1 0.1 convert_reduce_fusion
  32.2 0.1 fusion.4
  32.3 0.1 fusion.5
  32.4 5.3 %fusion.1 = (bf16[2048,1024]{1,0:T(8,128)(2,1)S(1)}, f32[]{:T(128)}) fusion(s32[1024]{0:T(1024)S(1)} %iota_add_fusion.1, s32[2048]{0:T(1024)S(1)} %iota_add_fusion, bf16[64,2048]{1,0:T(8,128)(2,1)S(1)} %fusion.5, bf16[64,1024]{1,0:T(8,128)(2,1)S(1)} %fusion.9), kind=kOutput, calls=%fused_computation.3 | convolution fusion | flops 295698432 | bytes 4599812 | tf_op jit(solution)/shard_map/dot_general | solution.py:27
  37.7 0.0 copy-start
  37.7 1.9 %copy-done = bf16[2048,1024]{1,0:T(8,128)(2,1)} copy-done((bf16[2048,1024]{1,0:T(8,128)(2,1)}, bf16[2048,1024]{1,0:T(8,128)(2,1)S(1)}, u32[]{:S(2)}) %copy-start) | copy-done | bytes 4194328
  39.6 1.6 %fusion.21 = f32[64,1024]{1,0:T(8,128)} fusion(bf16[64,2048]{1,0:T(8,128)(2,1)S(1)} %fusion.5, bf16[2048,1024]{1,0:T(8,128)(2,1)S(1)} %get-tuple-element.11), kind=kOutput, calls=%fused_computation.41 | convolution fusion | flops 268435456 | bytes 4718592 | tf_op jit(solution)/shard_map/dot_general | solution.py:40
  41.2 0.0 reduce-scatter.5.cloned.1.call-update
  41.2 0.0 reduce-scatter.3.cloned.1.call-start
  41.3 4.4 %fusion.20 = f32[64,2048]{1,0:T(8,128)} fusion(bf16[64,1024]{1,0:T(8,128)(2,1)S(1)} %fusion.9, bf16[2048,1024]{1,0:T(8,128)(2,1)} %copy-done), kind=kOutput, calls=%fused_computation.40 | convolution fusion | flops 268435456 | bytes 4849664 | tf_op jit(solution)/shard_map/dot_general | solution.py:37
  45.7 0.0 reduce-scatter.3.cloned.1.call-update
  45.7 39.6 %psum.35 = f32[]{:T(128)} all-reduce(f32[]{:T(128)} %get-tuple-element.12), channel_id=1, replica_groups=mesh['row'=4,'col'=8] {'row','col'}, use_global_device_ids=true, to_apply=%region_5.6 | all-reduce | flops 1 | bytes 8 | tf_op jit(solution)/shard_map/psum | solution.py:59
  86.0 0.0 reduce-scatter.5.cloned.1.call-done
  86.0 0.9 fusion.18
  86.9 10.7 %all-reduce.1 = (f32[1024]{0:T(1024)S(1)}, f32[1024]{0:T(1024)S(1)}) all-reduce(f32[1024]{0:T(1024)S(1)} %get-tuple-element.4, f32[1024]{0:T(1024)S(1)} %get-tuple-element.3), channel_id=1, replica_groups=mesh['row'=4,'col'=8] {'row'}, use_global_device_ids=true, to_apply=%region_15.16 | all-reduce | flops 2048 | bytes 16384 | tf_op jit(solution)/shard_map/psum | solution.py:52
  97.6 1.5 %fusion.17 = bf16[16,1024]{1,0:T(8,128)(2,1)} fusion(f32[16,1024]{1,0:T(8,128)} %reduce-scatter.5.cloned.1.call-done, f32[1024]{0:T(1024)S(1)} %get-tuple-element.15, f32[1024]{0:T(1024)S(1)} %get-tuple-element.16, f32[1024]{0:T(1024)S(1)} %add_rsqrt_fusion.1, bf16[64,1024]{1,0:T(8,128)(2,1)S(1)} %fusion.9, s32[]{:T(128)S(6)} %select_n.16), kind=kLoop, calls=%fused_computation.27 | loop fusion | flops 98304 | bytes 143364 | tf_op jit(solution)/shard_map/convert_element_type | solution.py:56
  99.1 0.0 reduce-scatter.3.cloned.1.call-done
  99.1 0.9 fusion.19
  100.0 25.9 %all-reduce = (f32[2048]{0:T(1024)S(1)}, f32[2048]{0:T(1024)S(1)}) all-reduce(f32[2048]{0:T(1024)S(1)} %get-tuple-element.6, f32[2048]{0:T(1024)S(1)} %get-tuple-element.5), channel_id=1, replica_groups=mesh['row'=4,'col'=8] {'col'}, use_global_device_ids=true, to_apply=%region_10.11 | all-reduce | flops 4096 | bytes 32768 | tf_op jit(solution)/shard_map/psum | solution.py:51
  125.9 1.5 %fusion.13 = bf16[8,2048]{1,0:T(8,128)(2,1)} fusion(f32[8,2048]{1,0:T(8,128)} %reduce-scatter.3.cloned.1.call-done, f32[2048]{0:T(1024)S(1)} %get-tuple-element.13, f32[2048]{0:T(1024)S(1)} %get-tuple-element.14, f32[2048]{0:T(1024)S(1)} %add_rsqrt_fusion, bf16[64,2048]{1,0:T(8,128)(2,1)S(1)} %fusion.5, s32[]{:T(128)S(6)} %select_n.15), kind=kLoop, calls=%fused_computation.23 | loop fusion | flops 98304 | bytes 155652 | tf_op jit(solution)/shard_map/convert_element_type | solution.py:53
  (11 shorter events, 0.2 us)
Async XLA Ops:
  7.2 78.8 %reduce-scatter.5.cloned.1.call-start = ((), (), s32[]{:S(2)}) async-start(), calls=%async_computation.3 | async-start | bytes 327680 | tf_op jit(solution)/shard_map/reduce_scatter | solution.py:42
  37.7 1.9 %copy-start = (bf16[2048,1024]{1,0:T(8,128)(2,1)}, bf16[2048,1024]{1,0:T(8,128)(2,1)S(1)}, u32[]{:S(2)}) copy-start(bf16[2048,1024]{1,0:T(8,128)(2,1)S(1)} %get-tuple-element.11) | copy-start | bytes 12582916
  41.2 57.9 %reduce-scatter.3.cloned.1.call-start = ((), (), s32[]{:S(2)}) async-start(), calls=%async_computation.2 | async-start | bytes 589824 | tf_op jit(solution)/shard_map/reduce_scatter | solution.py:41
Sparse Core Ops, SparseCore 0:
  41.4 24.1 reduce-scatter.4
  67.9 30.8 reduce-scatter.2
where the time goes:
time: 136 us; the launch traced here: 135 us
  blocking collectives  101 us (74%)
  between operations  15.9 us (12%)
  matrix products  11.2 us (8%)
  other arithmetic  5.07 us (4%)
  local copies, waits for them, and re-layouts  1.92 us (1%)
    psum x1, blocking collectives, body(): total = lax.psum(partial_loss, ('row', 'col'))  39.6 us
    psum x1, blocking collectives, body(): lax.psum((jnp.sum(summed_a, 0), jnp.sum(summed_a * mine_a, 0)), 'col')  25.9 us
    all_gather x1, blocking collectives, body(): whole_a = lax.all_gather(view_a, 'col', axis=0, tiled=True)  14.7 us
    psum x1, blocking collectives, body(): lax.psum((jnp.sum(summed_b, 0), jnp.sum(summed_b * mine_b, 0)), 'row')  10.7 us
    all_gather x1, blocking collectives, body(): whole_b = lax.all_gather(view_b, 'row', axis=0, tiled=True)  10.1 us
    dot_general x1, matrix products, body(): lax.dot_general(normed_a, normed_b, (((0,), (0,)), ((), ())), preferred_e...  5.3 us
    dot_general x1, matrix products, body(): lax.dot_general(normed_b, weights, (((1,), (1,)), ((), ())), preferred_el...  4.38 us
  transfers between devices with their start and end apart: 2, of which 0 were waited for; matrix products, arithmetic and copies ran while one was open for 5% of the time, Pallas kernels for 0%

commit v1 on v0

--- a/solution.py
+++ b/solution.py
@@ -5,6 +5,8 @@
 
 off_weight = 0.0051
 epsilon = 1e-05
+
+BOTH = ("row", "col")
 
 
 def normalize(values):
@@ -15,7 +17,7 @@
     return (((values - center) * scaled).astype(jnp.bfloat16), scaled)
 
 
-def body(view_a, view_b):
+def tiled_body(view_a, view_b):
     whole_a = lax.all_gather(view_a, "col", axis=0, tiled=True)
     whole_b = lax.all_gather(view_b, "row", axis=0, tiled=True)
     normed_a, scaled_a = normalize(whole_a)
@@ -61,7 +63,228 @@
     return (loss, grad_a, grad_b)
 
 
+def sibling(value, n_col):
+    return lax.ppermute(value, "col", [(c, c ^ 1) for c in range(n_col)])
+
+
+def flip(value, side, step):
+    pairs = []
+    for row in range(side):
+        for z in range(side):
+            pairs.append(((row * side + z) * 2, (row * side + (z ^ step)) * 2))
+            pairs.append(((row * side + z) * 2 + 1, ((row ^ step) * side + z) * 2 + 1))
+    return lax.ppermute(value, BOTH, pairs)
+
+
+def across(value, side, step):
+    pairs = []
+    for row in range(side):
+        for z in range(side):
+            pairs.append(((row * side + z) * 2, ((row ^ step) * side + z) * 2))
+            pairs.append(((row * side + z) * 2 + 1, (row * side + (z ^ step)) * 2 + 1))
+    return lax.ppermute(value, BOTH, pairs)
+
+
+def in_order(pieces, position):
+    bit = 1
+    while bit < len(pieces):
+        on = (position & bit) != 0
+        pieces = [jnp.where(on, pieces[i ^ bit], pieces[i]) for i in range(len(pieces))]
+        bit *= 2
+    return pieces
+
+
+def rounded(value):
+    return lax.reduce_precision(value, exponent_bits=8, mantissa_bits=7)
+
+
+def split(value):
+    high = rounded(value)
+    return high.astype(jnp.bfloat16), rounded(value - high).astype(jnp.bfloat16)
+
+
+def standardize(values):
+    values = values.astype(jnp.float32)
+    center = jnp.mean(values, 0)
+    spread = jnp.mean(jnp.square(values - center), 0)
+    scaled = lax.rsqrt(spread + epsilon)
+    return (rounded((values - center) * scaled).astype(jnp.bfloat16), scaled)
+
+
+def meetings(side):
+    chips = [(row, z) for row in range(side) for z in range(side)]
+
+    def hops(p, q):
+        return bin(p[0] ^ q[0]).count("1") + abs(p[1] - q[1])
+
+    def search(choices, order, used, chosen):
+        if len(chosen) == len(order):
+            return dict(chosen)
+        chip = order[len(chosen)]
+        for pair in choices[chip]:
+            if all(used[q] < 2 for q in pair):
+                for q in pair:
+                    used[q] += 1
+                found = search(choices, order, used, chosen + [(chip, pair)])
+                if found:
+                    return found
+                for q in pair:
+                    used[q] -= 1
+        return None
+
+    if side > 6:
+        return None
+    for limit in range(1, 3 * side):
+        choices = {
+            p: [
+                (q, t)
+                for i, q in enumerate(chips)
+                for t in chips[i + 1 :]
+                if max(hops(p, q), hops(p, t)) <= limit and len({*p, *q, *t}) == side
+            ]
+            for p in chips
+        }
+        if all(choices.values()):
+            order = sorted(chips, key=lambda p: len(choices[p]))
+            found = search(choices, order, dict.fromkeys(chips, 0), [])
+            if found:
+                return found
+    return None
+
+
+def spread_sums(known, side):
+    n_col = 2 * side
+    plan = meetings(side)
+    if plan is None:
+        step = 1
+        while step < side:
+            known = known + lax.ppermute(known, "col", [(c, c ^ (2 * step)) for c in range(n_col)])
+            step *= 2
+        return known
+    used, pairs = {}, []
+    for (row, z), pair in plan.items():
+        for core, (from_row, from_z) in enumerate(pair):
+            from_core = used.get((from_row, from_z), 0)
+            used[from_row, from_z] = from_core + 1
+            pairs.append(((from_row * side + from_z) * 2 + from_core, (row * side + z) * 2 + core))
+    known = known + lax.ppermute(known, BOTH, pairs)
+    return known + sibling(known, n_col)
+
+
+def gram_body(side, view_a, view_b):
+    n_col = 2 * side
+    share, width = view_a.shape
+    pair, half = view_b.shape
+    count = share * n_col
+    row = lax.axis_index("row")
+    col = lax.axis_index("col")
+    z = lax.shift_right_logical(col, 1)
+    is_a = (col & 1) == 0
+    diagonal = row == z
+
+    give = jnp.where(is_a, jnp.concatenate([view_b[:share], view_b[share:]], 1), view_a)
+    got = sibling(give, n_col)
+    both_a = jnp.concatenate([view_a, got], 0)
+    both_b = jnp.concatenate(
+        [jnp.concatenate([got[:, :half], got[:, half:]], 0), view_b], 1
+    )
+    own = jnp.where(is_a, both_a, both_b)
+
+    pieces = [own] + [flip(own, side, step) for step in range(1, side)]
+    mine = jnp.concatenate(in_order(pieces, jnp.where(is_a, z, row)), 0)
+    other = sibling(mine, n_col)
+
+    normed, scaled = standardize(mine)
+    gram = lax.dot_general(
+        normed, normed, (((1,), (1,)), ((), ())), preferred_element_type=jnp.float32
+    )
+    other_normed, other_scaled = standardize(other)
+
+    normed_f = normed.astype(jnp.float32)
+    other_f = other_normed.astype(jnp.float32)
+    corr = jnp.mean(normed_f * other_f, 0)
+    slope = jnp.where(diagonal, rounded(2.0 * (corr - 1.0)) - 2.0 * off_weight * corr, 0.0)
+    extra = (slope * (normed_f - jnp.mean(normed_f, 0) - other_f * corr)).astype(jnp.bfloat16)
+    part = jnp.square(1.0 - corr) - off_weight * jnp.square(corr)
+    part = jnp.sum(jnp.where(diagonal, part, 0.0).reshape(-1, 128), 0, keepdims=True)
+
+    flat = jnp.concatenate([gram[i * pair : (i + 1) * pair] for i in range(side)], 1)
+    block = side * count
+
+    def payload(images, flat, part):
+        part = jnp.broadcast_to(part, (pair, 128))
+        return jnp.concatenate([images, *split(flat), *split(part)], 1)
+
+    def parts(value):
+        value = value.astype(jnp.float32)
+        flat = value[:, width : width + block] + value[:, width + block : width + 2 * block]
+        part = value[:1, width + 2 * block :]
+        return value[:, :width].astype(jnp.bfloat16), flat, part[:, :128] + part[:, 128:]
+
+    def images_of(step):
+        return lax.dynamic_slice_in_dim(extra, (row ^ step) * pair, pair, 0)
+
+    landed = [payload(images_of(0), flat, part)]
+    landed += [across(payload(images_of(step), flat, part), side, step) for step in range(1, side)]
+    sent = payload(*parts(sum(x.astype(jnp.float32) for x in landed)))
+
+    came = sibling(sent, n_col)
+    for_a = jnp.where(is_a, came, sent)
+    for_b = jnp.where(is_a, sent, came)
+
+    slots = lax.broadcasted_iota(jnp.int32, (2 * side, 128), 0)
+    by_z = (slots & (side - 1)) == z
+    by_row = (slots & (side - 1)) == row
+    counts = slots >= side
+    known = jnp.where(by_z, jnp.where(counts, 1.0, parts(for_b)[2]), 0.0)
+    known = known + jnp.where(by_row, jnp.where(counts, 1.0, parts(for_a)[2]), 0.0)
+    known = spread_sums(known, side)
+
+    all_a = jnp.where(is_a, normed, other_normed)
+    all_b = jnp.where(is_a, other_normed[:, :half], normed[:, half:])
+    scaled_a = jnp.where(is_a, scaled, other_scaled)
+    scaled_b = jnp.where(is_a, other_scaled[:half], scaled[half:])
+    extra_a = jnp.where(is_a, for_a[:share, :width], for_a[share:, :width])
+    extra_b = jnp.where(is_a, for_b[:, :half], for_b[:, half:width])
+
+    def gradient(sums, normed, scaled, extra, start, images):
+        halves = sums[:, width : width + 2 * block]
+        halves = jnp.concatenate(
+            [halves[:, i * count : (i + 1) * count] for i in range(2 * side)], 0
+        )
+        term = jnp.dot(halves, normed, preferred_element_type=jnp.float32)
+        term = (term[:count] + term[count:]) * (2.0 * off_weight / count)
+        normed_f = normed.astype(jnp.float32)
+        first = jnp.mean(term, 0)
+        second = jnp.mean(term * normed_f, 0)
+        term = lax.dynamic_slice_in_dim(term, start, images, 0)
+        normed_f = lax.dynamic_slice_in_dim(normed_f, start, images, 0)
+        return (scaled * (term - first - normed_f * second + extra.astype(jnp.float32))).astype(
+            jnp.bfloat16
+        )
+
+    grad_a = gradient(for_a, all_a, scaled_a, extra_a, col * share, share)
+    grad_b = gradient(for_b, all_b, scaled_b, extra_b, row * pair, pair)
+
+    on_diagonal = known[:side] / known[side:]
+    everywhere = parts(for_a)[1] * parts(for_b)[1] * (off_weight / (count * count))
+    everywhere = sum(everywhere[:, i : i + 128] for i in range(0, block, 128))
+    loss = jnp.sum(everywhere + jnp.pad(on_diagonal, ((0, pair - side), (0, 0)))) / (width * side)
+    return (loss, grad_a, grad_b)
+
+
 def solution(mesh):
     in_specs = (P("col", "row"), P("row", "col"))
     out_specs = (P(), P("col", "row"), P("row", "col"))
+    n_row, n_col = mesh.shape["row"], mesh.shape["col"]
+    square = n_col == 2 * n_row and n_row & (n_row - 1) == 0
+
+    def body(view_a, view_b):
+        share, width = view_a.shape
+        fits = view_b.shape == (2 * share, width // 2) and width % 256 == 0
+        fits = fits and share % 8 == 0 and 2 * share >= n_row and n_row * n_col * share % 128 == 0
+        if square and fits:
+            return gram_body(n_row, view_a, view_b)
+        return tiled_body(view_a, view_b)
+
     return jax.shard_map(body, mesh=mesh, in_specs=in_specs, out_specs=out_specs, check_vma=False)

time: 136 us -> 35.9 us (0.26)
  blocking collectives: 101 us -> 0 us
  waiting for transfers between devices: 0.06 us -> 17.3 us
  between operations: 15.9 us -> 2.73 us
  matrix products: 11.2 us -> 0.69 us
  starting transfers between devices: 0.08 us -> 9.89 us
  other arithmetic: 5.07 us -> 3.54 us
    psum x3 -> x0, blocking collectives: 76.3 us -> none  [the longest x1 39.6 us: body(): total = lax.psum(partial_loss, ('row', 'col'))]
    all_gather x2 -> x0, blocking collectives: 24.8 us -> none  [the longest x1 14.7 us: body(): whole_a = lax.all_gather(view_a, 'col', axis=0, tiled=True)]
    ppermute x0 -> x11, waiting for transfers between devices: none -> 17.3 us  [the longest x3 6.04 us: flip(): return lax.ppermute(value, BOTH, pairs)]
    dot_general x3, matrix products: 11.2 us -> 0.69 us  [the longest x2 0.48 us: gradient(): term = jnp.dot(halves, normed, preferred_element_type=jnp.float32)]
    ppermute x0 -> x11, starting transfers between devices: none -> 9.89 us  [the longest x3 5.58 us: flip(): return lax.ppermute(value, BOTH, pairs)]
    convert_element_type x4 -> x8, other arithmetic: 3.06 us -> 1.7 us  [the longest x2 1.29 us: gradient(): (scaled * (term - first - normed_f * second + extra.astype(jnp.float32)))...]
  transfers between devices with their start and end apart: 2 -> 11, of which waited for: 0 -> 10; matrix products, arithmetic and copies ran while one was open for 5% -> 8% of each run, Pallas kernels for 0% -> 0%
where the time goes in v1:
time: 35.9 us; the launch traced here: 35.7 us
  waiting for transfers between devices  17.3 us (48%)
  starting transfers between devices  9.89 us (28%)
  other arithmetic  3.54 us (10%)
  between operations  2.73 us (8%)
  local copies, waits for them, and re-layouts  1.55 us (4%)
  matrix products  0.69 us (2%)
    ppermute x3, waiting for transfers between devices, flip(): return lax.ppermute(value, BOTH, pairs)  6.04 us
    ppermute x3, starting transfers between devices, flip(): return lax.ppermute(value, BOTH, pairs)  5.58 us
    ppermute x3, waiting for transfers between devices, across(): return lax.ppermute(value, BOTH, pairs)  4.91 us
    ppermute x4, waiting for transfers between devices, sibling(): return lax.ppermute(value, 'col', [(c, c ^ 1) for c in range(n_col)])  4.67 us
    ppermute x3, starting transfers between devices, across(): return lax.ppermute(value, BOTH, pairs)  3.55 us
    ppermute x1, waiting for transfers between devices, spread_sums(): known = known + lax.ppermute(known, BOTH, pairs)  1.67 us
    convert_element_type x2, other arithmetic, gradient(): (scaled * (term - first - normed_f * second + extra.astype(jnp.float32)))...  1.29 us
    slice x1, local copies, waits for them, and re-layouts, gram_body(): view_b[:share]  0.74 us
  transfers between devices with their start and end apart: 11, of which 10 were waited for; matrix products, arithmetic and copies ran while one was open for 8% of the time, Pallas kernels for 0%

profile of v1, /device:TPU:0, one launch (start us, length us, event | category | flops | bytes accessed | tf_op | source)
XLA Modules:
  0.0 35.7 jit_solution(5584234990072770796)
XLA Ops:
  0.6 0.7 %fusion.47 = (bf16[8,1024]{1,0:T(8,128)(2,1)S(1)}, bf16[8,1024]{1,0:T(8,128)(2,1)S(1)}) fusion(bf16[16,1024]{1,0:T(8,128)(2,1)} %param.3), kind=kLoop, calls=%fused_computation.150 | loop fusion | bytes 65536 | tf_op jit(solution)/shard_map/slice | solution.py:185
  1.4 0.5 %collective-permute-start = (bf16[8,2048]{1,0:T(8,128)(2,1)S(1)}, bf16[8,2048]{1,0:T(8,128)(2,1)S(1)}, u32[]{:S(2)}, u32[]{:S(2)}) collective-permute-start(bf16[8,2048]{1,0:T(8,128)(2,1)S(1)} %maximum_select_fusion.1), channel_id=1, source_target_pairs={{0,1},{1,0},{2,3},{3,2},{4,5},{5,4},{6,7},{7,6},{8,9},{9,8},{10,11... | collective-permute-start | bytes 98312 | tf_op jit(solution)/shard_map/ppermute | solution.py:67
  1.9 0.9 %collective-permute-done = bf16[8,2048]{1,0:T(8,128)(2,1)S(1)} collective-permute-done((bf16[8,2048]{1,0:T(8,128)(2,1)S(1)}, bf16[8,2048]{1,0:T(8,128)(2,1)S(1)}, u32[]{:S(2)}, u32[]{:S(2)}) %collective-permute-start) | collective-permute-done | bytes 32800 | tf_op jit(solution)/shard_map/ppermute | solution.py:67
  2.8 3.0 %collective-permute-start.3 = (bf16[16,2048]{1,0:T(8,128)(2,1)S(1)}, bf16[16,2048]{1,0:T(8,128)(2,1)S(1)}, u32[]{:S(2)}, u32[]{:S(2)}) collective-permute-start(bf16[16,2048]{1,0:T(8,128)(2,1)S(1)} %maximum_select_fusion), channel_id=1, source_target_pairs={{0,2},{1,9},{2,0},{3,11},{4,6},{5,13},{6,4},{7,15},{8,10},{9,1},{1... | collective-permute-start | bytes 196616 | tf_op jit(solution)/shard_map/ppermute | solution.py:76
  5.8 2.6 %collective-permute-start.2 = (bf16[16,2048]{1,0:T(8,128)(2,1)S(1)}, bf16[16,2048]{1,0:T(8,128)(2,1)S(1)}, u32[]{:S(2)}, u32[]{:S(2)}) collective-permute-start(bf16[16,2048]{1,0:T(8,128)(2,1)S(1)} %maximum_select_fusion), channel_id=1, source_target_pairs={{0,4},{1,17},{2,6},{3,19},{4,0},{5,21},{6,2},{7,23},{8,12},{9,25},... | collective-permute-start | bytes 196616 | tf_op jit(solution)/shard_map/ppermute | solution.py:76
  8.4 3.3 %collective-permute-done.2 = bf16[16,2048]{1,0:T(8,128)(2,1)S(1)} collective-permute-done((bf16[16,2048]{1,0:T(8,128)(2,1)S(1)}, bf16[16,2048]{1,0:T(8,128)(2,1)S(1)}, u32[]{:S(2)}, u32[]{:S(2)}) %collective-permute-start.2) | collective-permute-done | bytes 65568 | tf_op jit(solution)/shard_map/ppermute | solution.py:76
  11.7 2.8 %collective-permute-done.1 = bf16[16,2048]{1,0:T(8,128)(2,1)S(1)} collective-permute-done((bf16[16,2048]{1,0:T(8,128)(2,1)S(1)}, bf16[16,2048]{1,0:T(8,128)(2,1)S(1)}, u32[]{:S(2)}, u32[]{:S(2)}) %collective-permute-start.1) | collective-permute-done | bytes 65568 | tf_op jit(solution)/shard_map/ppermute | solution.py:76
  14.6 0.1 fusion.7
  14.7 1.4 %collective-permute-done.4 = bf16[64,2048]{1,0:T(8,128)(2,1)S(1)} collective-permute-done((bf16[64,2048]{1,0:T(8,128)(2,1)S(1)}, bf16[64,2048]{1,0:T(8,128)(2,1)S(1)}, u32[]{:S(2)}, u32[]{:S(2)}) %collective-permute-start.4) | collective-permute-done | bytes 262176 | tf_op jit(solution)/shard_map/ppermute | solution.py:67
  16.2 0.1 fusion.4
  16.3 0.2 fusion.39
  16.5 0.2 fusion.48
  16.8 0.1 convert_reduce_fusion
  16.9 0.1 fusion.12
  17.1 0.1 constant_dynamic-update-slice_fusion.3
  17.3 1.6 %collective-permute-start.5 = (bf16[16,2816]{1,0:T(8,128)(2,1)S(1)}, bf16[16,2816]{1,0:T(8,128)(2,1)S(1)}, u32[]{:S(2)}, u32[]{:S(2)}) collective-permute-start(bf16[16,2816]{1,0:T(8,128)(2,1)S(1)} %get-tuple-element.59), channel_id=1, source_target_pairs={{0,8},{1,3},{2,10},{3,1},{4,12},{5,7},{6,14},{7,5},{8,0},{9,11},{1... | collective-permute-start | bytes 270344 | tf_op jit(solution)/shard_map/ppermute | solution.py:85
  18.9 1.5 %collective-permute-start.6 = (bf16[16,2816]{1,0:T(8,128)(2,1)S(1)}, bf16[16,2816]{1,0:T(8,128)(2,1)S(1)}, u32[]{:S(2)}, u32[]{:S(2)}) collective-permute-start(bf16[16,2816]{1,0:T(8,128)(2,1)S(1)} %get-tuple-element.60), channel_id=1, source_target_pairs={{0,16},{1,5},{2,18},{3,7},{4,20},{5,1},{6,22},{7,3},{8,24},{9,13},... | collective-permute-start | bytes 270344 | tf_op jit(solution)/shard_map/ppermute | solution.py:85
  20.4 0.5 %collective-permute-start.7 = (bf16[16,2816]{1,0:T(8,128)(2,1)S(1)}, bf16[16,2816]{1,0:T(8,128)(2,1)S(1)}, u32[]{:S(2)}, u32[]{:S(2)}) collective-permute-start(bf16[16,2816]{1,0:T(8,128)(2,1)S(1)} %get-tuple-element.61), channel_id=1, source_target_pairs={{0,24},{1,7},{2,26},{3,5},{4,28},{5,3},{6,30},{7,1},{8,16},{9,15},... | collective-permute-start | bytes 270344 | tf_op jit(solution)/shard_map/ppermute | solution.py:85
  20.9 1.0 %collective-permute-done.5 = bf16[16,2816]{1,0:T(8,128)(2,1)S(1)} collective-permute-done((bf16[16,2816]{1,0:T(8,128)(2,1)S(1)}, bf16[16,2816]{1,0:T(8,128)(2,1)S(1)}, u32[]{:S(2)}, u32[]{:S(2)}) %collective-permute-start.5) | collective-permute-done | bytes 90144 | tf_op jit(solution)/shard_map/ppermute | solution.py:85
  21.9 1.5 %collective-permute-done.6 = bf16[16,2816]{1,0:T(8,128)(2,1)S(1)} collective-permute-done((bf16[16,2816]{1,0:T(8,128)(2,1)S(1)}, bf16[16,2816]{1,0:T(8,128)(2,1)S(1)}, u32[]{:S(2)}, u32[]{:S(2)}) %collective-permute-start.6) | collective-permute-done | bytes 90144 | tf_op jit(solution)/shard_map/ppermute | solution.py:85
  23.4 2.4 %collective-permute-done.7 = bf16[16,2816]{1,0:T(8,128)(2,1)S(1)} collective-permute-done((bf16[16,2816]{1,0:T(8,128)(2,1)S(1)}, bf16[16,2816]{1,0:T(8,128)(2,1)S(1)}, u32[]{:S(2)}, u32[]{:S(2)}) %collective-permute-start.7) | collective-permute-done | bytes 90144 | tf_op jit(solution)/shard_map/ppermute | solution.py:85
  26.1 1.3 %collective-permute-done.8 = bf16[16,2816]{1,0:T(8,128)(2,1)S(1)} collective-permute-done((bf16[16,2816]{1,0:T(8,128)(2,1)S(1)}, bf16[16,2816]{1,0:T(8,128)(2,1)S(1)}, u32[]{:S(2)}, u32[]{:S(2)}) %collective-permute-start.8) | collective-permute-done | bytes 90144 | tf_op jit(solution)/shard_map/ppermute | solution.py:67
  27.5 0.1 collective-permute-start.9
  27.8 0.1 constant_dynamic-update-slice_fusion.25
  28.2 0.2 fusion.50
  28.6 0.3 fusion.49
  28.8 0.1 fusion.34
  29.0 0.7 %multiply_convert_fusion.1 = bf16[8,2048]{1,0:T(8,128)(2,1)} fusion(f32[64,2048]{1,0:T(8,128)S(1)} %get-tuple-element.13, s32[]{:T(128)S(6)} %select_n.201, f32[64,2048]{1,0:T(8,128)S(1)} %get-tuple-element.12, bf16[16,2816]{1,0:T(8,128)(2,1)S(1)} %get-tuple-element.18, f32[2048]{0:T(1024)S(1)} %broadcast_multiply_fusion, ...), kind=kLoop, calls=%fused_computation.78 | loop fusion | flops 131072 | bytes 253957 | tf_op jit(solution)/shard_map/convert_element_type | solution.py:262
  29.7 0.6 %multiply_convert_fusion = bf16[16,1024]{1,0:T(8,128)(2,1)} fusion(f32[64,1024]{1,0:T(8,128)S(1)} %get-tuple-element.10, s32[]{:T(128)S(6)} %select_n.185, f32[64,1024]{1,0:T(8,128)S(1)} %get-tuple-element.9, bf16[16,2816]{1,0:T(8,128)(2,1)S(1)} %get-tuple-element.36, f32[1024]{0:T(1024)S(1)} %broadcast_multiply_fusion.6, ...), kind=kLoop, calls=%fused_computation.77 | loop fusion | flops 131072 | bytes 241669 | tf_op jit(solution)/shard_map/convert_element_type | solution.py:262
  30.3 1.7 %collective-permute-done.9 = f32[8,128]{1,0:T(8,128)S(1)} collective-permute-done((f32[8,128]{1,0:T(8,128)S(1)}, f32[8,128]{1,0:T(8,128)S(1)}, u32[]{:S(2)}, u32[]{:S(2)}) %collective-permute-start.9) | collective-permute-done | bytes 4128 | tf_op jit(solution)/shard_map/ppermute | solution.py:170
  32.1 1.1 %collective-permute-done.10 = f32[8,128]{1,0:T(8,128)S(1)} collective-permute-done((f32[8,128]{1,0:T(8,128)S(1)}, f32[8,128]{1,0:T(8,128)S(1)}, u32[]{:S(2)}, u32[]{:S(2)}) %collective-permute-start.10) | collective-permute-done | bytes 4128 | tf_op jit(solution)/shard_map/ppermute | solution.py:67
  33.3 0.6 %fusion.23 = f32[]{:T(128)} fusion(f32[16,256]{1,0:T(8,128)S(1)} %fusion.21, f32[4,128]{1,0:T(4,128)S(1)} %slice_divide_fusion), kind=kLoop, calls=%fused_computation.106 | loop fusion | flops 6143 | bytes 18436 | tf_op jit(solution)/shard_map/reduce_sum | solution.py:272
  (67 shorter events, 1.7 us)
Async XLA Ops:
  0.6 0.8 %copy-start = (bf16[8,2048]{1,0:T(8,128)(2,1)S(1)}, bf16[8,2048]{1,0:T(8,128)(2,1)}, u32[]{:S(2)}) copy-start(bf16[8,2048]{1,0:T(8,128)(2,1)} %param.2) | copy-start | bytes 98308
  1.4 1.4 %collective-permute-start = (bf16[8,2048]{1,0:T(8,128)(2,1)S(1)}, bf16[8,2048]{1,0:T(8,128)(2,1)S(1)}, u32[]{:S(2)}, u32[]{:S(2)}) collective-permute-start(bf16[8,2048]{1,0:T(8,128)(2,1)S(1)} %maximum_select_fusion.1), channel_id=1, source_target_pairs={{0,1},{1,0},{2,3},{3,2},{4,5},{5,4},{6,7},{7,6},{8,9},{9,8},{10,11... | collective-permute-start | bytes 98312 | tf_op jit(solution)/shard_map/ppermute | solution.py:67
  1.9 0.9 %copy-start.1 = (bf16[16,1024]{1,0:T(8,128)(2,1)S(1)}, bf16[16,1024]{1,0:T(8,128)(2,1)}, u32[]{:S(2)}) copy-start(bf16[16,1024]{1,0:T(8,128)(2,1)} %param.3) | copy-start | bytes 98308
  2.8 5.6 %collective-permute-start.3 = (bf16[16,2048]{1,0:T(8,128)(2,1)S(1)}, bf16[16,2048]{1,0:T(8,128)(2,1)S(1)}, u32[]{:S(2)}, u32[]{:S(2)}) collective-permute-start(bf16[16,2048]{1,0:T(8,128)(2,1)S(1)} %maximum_select_fusion), channel_id=1, source_target_pairs={{0,2},{1,9},{2,0},{3,11},{4,6},{5,13},{6,4},{7,15},{8,10},{9,1},{1... | collective-permute-start | bytes 196616 | tf_op jit(solution)/shard_map/ppermute | solution.py:76
  5.8 5.9 %collective-permute-start.2 = (bf16[16,2048]{1,0:T(8,128)(2,1)S(1)}, bf16[16,2048]{1,0:T(8,128)(2,1)S(1)}, u32[]{:S(2)}, u32[]{:S(2)}) collective-permute-start(bf16[16,2048]{1,0:T(8,128)(2,1)S(1)} %maximum_select_fusion), channel_id=1, source_target_pairs={{0,4},{1,17},{2,6},{3,19},{4,0},{5,21},{6,2},{7,23},{8,12},{9,25},... | collective-permute-start | bytes 196616 | tf_op jit(solution)/shard_map/ppermute | solution.py:76
  8.4 6.1 %collective-permute-start.1 = (bf16[16,2048]{1,0:T(8,128)(2,1)S(1)}, bf16[16,2048]{1,0:T(8,128)(2,1)S(1)}, u32[]{:S(2)}, u32[]{:S(2)}) collective-permute-start(bf16[16,2048]{1,0:T(8,128)(2,1)S(1)} %maximum_select_fusion), channel_id=1, source_target_pairs={{0,6},{1,25},{2,4},{3,27},{4,2},{5,29},{6,0},{7,31},{8,14},{9,17},... | collective-permute-start | bytes 196616 | tf_op jit(solution)/shard_map/ppermute | solution.py:76
  14.5 1.6 %collective-permute-start.4 = (bf16[64,2048]{1,0:T(8,128)(2,1)S(1)}, bf16[64,2048]{1,0:T(8,128)(2,1)S(1)}, u32[]{:S(2)}, u32[]{:S(2)}) collective-permute-start(bf16[64,2048]{1,0:T(8,128)(2,1)S(1)} %get-tuple-element.26), channel_id=1, source_target_pairs={{0,1},{1,0},{2,3},{3,2},{4,5},{5,4},{6,7},{7,6},{8,9},{9,8},{10,11... | collective-permute-start | bytes 786440 | tf_op jit(solution)/shard_map/ppermute | solution.py:67
  17.3 4.6 %collective-permute-start.5 = (bf16[16,2816]{1,0:T(8,128)(2,1)S(1)}, bf16[16,2816]{1,0:T(8,128)(2,1)S(1)}, u32[]{:S(2)}, u32[]{:S(2)}) collective-permute-start(bf16[16,2816]{1,0:T(8,128)(2,1)S(1)} %get-tuple-element.59), channel_id=1, source_target_pairs={{0,8},{1,3},{2,10},{3,1},{4,12},{5,7},{6,14},{7,5},{8,0},{9,11},{1... | collective-permute-start | bytes 270344 | tf_op jit(solution)/shard_map/ppermute | solution.py:85
  18.9 4.5 %collective-permute-start.6 = (bf16[16,2816]{1,0:T(8,128)(2,1)S(1)}, bf16[16,2816]{1,0:T(8,128)(2,1)S(1)}, u32[]{:S(2)}, u32[]{:S(2)}) collective-permute-start(bf16[16,2816]{1,0:T(8,128)(2,1)S(1)} %get-tuple-element.60), channel_id=1, source_target_pairs={{0,16},{1,5},{2,18},{3,7},{4,20},{5,1},{6,22},{7,3},{8,24},{9,13},... | collective-permute-start | bytes 270344 | tf_op jit(solution)/shard_map/ppermute | solution.py:85
  20.4 5.4 %collective-permute-start.7 = (bf16[16,2816]{1,0:T(8,128)(2,1)S(1)}, bf16[16,2816]{1,0:T(8,128)(2,1)S(1)}, u32[]{:S(2)}, u32[]{:S(2)}) collective-permute-start(bf16[16,2816]{1,0:T(8,128)(2,1)S(1)} %get-tuple-element.61), channel_id=1, source_target_pairs={{0,24},{1,7},{2,26},{3,5},{4,28},{5,3},{6,30},{7,1},{8,16},{9,15},... | collective-permute-start | bytes 270344 | tf_op jit(solution)/shard_map/ppermute | solution.py:85
  26.0 1.4 %collective-permute-start.8 = (bf16[16,2816]{1,0:T(8,128)(2,1)S(1)}, bf16[16,2816]{1,0:T(8,128)(2,1)S(1)}, u32[]{:S(2)}, u32[]{:S(2)}) collective-permute-start(bf16[16,2816]{1,0:T(8,128)(2,1)S(1)} %constant_dynamic-update-slice_fusion.20), channel_id=1, source_target_pairs={{0,1},{1,0},{2,3},{3,2},{4,5},{5,4},{6,7},{7,6},{8,9},{9,8},{10,11... | collective-permute-start | bytes 270344 | tf_op jit(solution)/shard_map/ppermute | solution.py:67
  27.5 4.5 %collective-permute-start.9 = (f32[8,128]{1,0:T(8,128)S(1)}, f32[8,128]{1,0:T(8,128)S(1)}, u32[]{:S(2)}, u32[]{:S(2)}) collective-permute-start(f32[8,128]{1,0:T(8,128)S(1)} %select_add_fusion), channel_id=1, source_target_pairs={{18,0},{24,1},{6,30},{12,31},{13,8},{25,9},{4,22},{14,23},{16,2},{... | collective-permute-start | bytes 12296 | tf_op jit(solution)/shard_map/ppermute | solution.py:170
  32.0 1.2 %collective-permute-start.10 = (f32[8,128]{1,0:T(8,128)S(1)}, f32[8,128]{1,0:T(8,128)S(1)}, u32[]{:S(2)}, u32[]{:S(2)}) collective-permute-start(f32[8,128]{1,0:T(8,128)S(1)} %fusion.33), channel_id=1, source_target_pairs={{0,1},{1,0},{2,3},{3,2},{4,5},{5,4},{6,7},{7,6},{8,9},{9,8},{10,11... | collective-permute-start | bytes 12296 | tf_op jit(solution)/shard_map/ppermute | solution.py:67

commit v2 on v1

--- a/solution.py
+++ b/solution.py
@@ -113,62 +113,40 @@
 
 def meetings(side):
     chips = [(row, z) for row in range(side) for z in range(side)]
+    owners = {v: [(r, z, k) for r, z in chips for k in (0, 1) if (r, z)[1 - k] == v] for v in range(side)}
+    wanted = {(r, z): [v for v in range(side) if v not in (r, z)] for r, z in chips}
 
     def hops(p, q):
         return bin(p[0] ^ q[0]).count("1") + abs(p[1] - q[1])
 
-    def search(choices, order, used, chosen):
-        if len(chosen) == len(order):
-            return dict(chosen)
-        chip = order[len(chosen)]
-        for pair in choices[chip]:
-            if all(used[q] < 2 for q in pair):
-                for q in pair:
-                    used[q] += 1
-                found = search(choices, order, used, chosen + [(chip, pair)])
-                if found:
-                    return found
-                for q in pair:
-                    used[q] -= 1
-        return None
-
-    if side > 6:
-        return None
-    for limit in range(1, 3 * side):
-        choices = {
-            p: [
-                (q, t)
-                for i, q in enumerate(chips)
-                for t in chips[i + 1 :]
-                if max(hops(p, q), hops(p, t)) <= limit and len({*p, *q, *t}) == side
-            ]
-            for p in chips
-        }
-        if all(choices.values()):
-            order = sorted(chips, key=lambda p: len(choices[p]))
-            found = search(choices, order, dict.fromkeys(chips, 0), [])
-            if found:
-                return found
-    return None
-
-
-def spread_sums(known, side):
-    n_col = 2 * side
-    plan = meetings(side)
-    if plan is None:
-        step = 1
-        while step < side:
-            known = known + lax.ppermute(known, "col", [(c, c ^ (2 * step)) for c in range(n_col)])
-            step *= 2
-        return known
-    used, pairs = {}, []
-    for (row, z), pair in plan.items():
-        for core, (from_row, from_z) in enumerate(pair):
-            from_core = used.get((from_row, from_z), 0)
-            used[from_row, from_z] = from_core + 1
-            pairs.append(((from_row * side + from_z) * 2 + from_core, (row * side + z) * 2 + core))
-    known = known + lax.ppermute(known, BOTH, pairs)
-    return known + sibling(known, n_col)
+    rounds = []
+    while any(wanted.values()):
+        asks = []
+        for (r, z), left in wanted.items():
+            left.sort(key=lambda v: (v - r - 1) % side if r == z else v)
+            asks += [((r, z), v) for v in left[-2:]]
+
+        def place(ask, taken, limit, seen):
+            for owner in owners[ask[1]]:
+                if owner not in seen and hops(owner, ask[0]) <= limit:
+                    seen.add(owner)
+                    if owner not in taken or place(taken[owner], taken, limit, seen):
+                        taken[owner] = ask
+                        return True
+            return False
+
+        for limit in range(3 * side):
+            taken = {}
+            if all([place(ask, taken, limit, set()) for ask in asks]):
+                break
+        heard, pairs = dict.fromkeys(chips, 0), []
+        for (r, z, k), (chip, v) in taken.items():
+            receiver = (chip[0] * side + chip[1]) * 2 + heard[chip]
+            pairs.append(((r * side + z) * 2 + k, receiver))
+            heard[chip] += 1
+            wanted[chip].remove(v)
+        rounds.append(sorted(pairs))
+    return rounds
 
 
 def gram_body(side, view_a, view_b):
@@ -182,13 +160,10 @@
     is_a = (col & 1) == 0
     diagonal = row == z
 
-    give = jnp.where(is_a, jnp.concatenate([view_b[:share], view_b[share:]], 1), view_a)
-    got = sibling(give, n_col)
-    both_a = jnp.concatenate([view_a, got], 0)
-    both_b = jnp.concatenate(
-        [jnp.concatenate([got[:, :half], got[:, half:]], 0), view_b], 1
-    )
-    own = jnp.where(is_a, both_a, both_b)
+    got_a, got_b = sibling(view_a, n_col), sibling(view_b, n_col)
+    own = jnp.where(
+        is_a, jnp.concatenate([view_a, got_a], 0), jnp.concatenate([got_b, view_b], 1)
+    )
 
     pieces = [own] + [flip(own, side, step) for step in range(1, side)]
     mine = jnp.concatenate(in_order(pieces, jnp.where(is_a, z, row)), 0)
@@ -198,6 +173,7 @@
     gram = lax.dot_general(
         normed, normed, (((1,), (1,)), ((), ())), preferred_element_type=jnp.float32
     )
+    normed, gram, other = lax.optimization_barrier((normed, gram, other))
     other_normed, other_scaled = standardize(other)
 
     normed_f = normed.astype(jnp.float32)
@@ -208,53 +184,52 @@
     part = jnp.square(1.0 - corr) - off_weight * jnp.square(corr)
     part = jnp.sum(jnp.where(diagonal, part, 0.0).reshape(-1, 128), 0, keepdims=True)
 
-    flat = jnp.concatenate([gram[i * pair : (i + 1) * pair] for i in range(side)], 1)
-    block = side * count
-
-    def payload(images, flat, part):
-        part = jnp.broadcast_to(part, (pair, 128))
-        return jnp.concatenate([images, *split(flat), *split(part)], 1)
-
-    def parts(value):
-        value = value.astype(jnp.float32)
-        flat = value[:, width : width + block] + value[:, width + block : width + 2 * block]
-        part = value[:1, width + 2 * block :]
-        return value[:, :width].astype(jnp.bfloat16), flat, part[:, :128] + part[:, 128:]
+    lanes = width // side
+
+    def payload(images, gram, part):
+        images = [images[:, i * lanes : (i + 1) * lanes] for i in range(side)]
+        part = [jnp.broadcast_to(x, (count // 2, 128)) for x in split(part)]
+        return jnp.concatenate([jnp.concatenate(images, 0), *split(gram), jnp.concatenate(part, 0)], 1)
 
     def images_of(step):
         return lax.dynamic_slice_in_dim(extra, (row ^ step) * pair, pair, 0)
 
-    landed = [payload(images_of(0), flat, part)]
-    landed += [across(payload(images_of(step), flat, part), side, step) for step in range(1, side)]
-    sent = payload(*parts(sum(x.astype(jnp.float32) for x in landed)))
-
+    landed = [payload(images_of(0), gram, part)]
+    landed += [across(payload(images_of(step), gram, part), side, step) for step in range(1, side)]
+    summed = sum(x.astype(jnp.float32) for x in landed)
+    gram = summed[:, lanes : lanes + count] + summed[:, lanes + count : lanes + 2 * count]
+    part = summed[:1, lanes + 2 * count :] + summed[count // 2 : count // 2 + 1, lanes + 2 * count :]
+
+    sent = jnp.concatenate([summed[:, :lanes].astype(jnp.bfloat16), *split(gram)], 1)
     came = sibling(sent, n_col)
     for_a = jnp.where(is_a, came, sent)
     for_b = jnp.where(is_a, sent, came)
 
     slots = lax.broadcasted_iota(jnp.int32, (2 * side, 128), 0)
-    by_z = (slots & (side - 1)) == z
-    by_row = (slots & (side - 1)) == row
-    counts = slots >= side
-    known = jnp.where(by_z, jnp.where(counts, 1.0, parts(for_b)[2]), 0.0)
-    known = known + jnp.where(by_row, jnp.where(counts, 1.0, parts(for_a)[2]), 0.0)
-    known = spread_sums(known, side)
-
-    all_a = jnp.where(is_a, normed, other_normed)
-    all_b = jnp.where(is_a, other_normed[:, :half], normed[:, half:])
+    known = jnp.where((slots & (side - 1)) == jnp.where(is_a, z, row), jnp.where(slots < side, part, 1.0), 0.0)
+    known = known + sum(lax.ppermute(known, BOTH, pairs) for pairs in meetings(side))
+    known = known + sibling(known, n_col)
+
+    twice = [jnp.where(is_a, normed, other_normed)] * 2
+    all_a = jnp.concatenate(twice, 0)
+    twice = [jnp.where(is_a, other_normed[:, :half], normed[:, half:])] * 2
+    all_b = jnp.concatenate(twice, 0)
     scaled_a = jnp.where(is_a, scaled, other_scaled)
     scaled_b = jnp.where(is_a, other_scaled[:half], scaled[half:])
-    extra_a = jnp.where(is_a, for_a[:share, :width], for_a[share:, :width])
-    extra_b = jnp.where(is_a, for_b[:, :half], for_b[:, half:width])
-
-    def gradient(sums, normed, scaled, extra, start, images):
-        halves = sums[:, width : width + 2 * block]
-        halves = jnp.concatenate(
-            [halves[:, i * count : (i + 1) * count] for i in range(2 * side)], 0
-        )
-        term = jnp.dot(halves, normed, preferred_element_type=jnp.float32)
-        term = (term[:count] + term[count:]) * (2.0 * off_weight / count)
-        normed_f = normed.astype(jnp.float32)
+
+    def images_in(sums):
+        return jnp.concatenate([sums[i * pair : (i + 1) * pair, :lanes] for i in range(side)], 1)
+
+    extra_a = images_in(for_a)
+    extra_a = jnp.where(is_a, extra_a[:share], extra_a[share:])
+    extra_b = images_in(for_b)
+    extra_b = jnp.where(is_a, extra_b[:, :half], extra_b[:, half:])
+
+    def gradient(sums, twice, scaled, extra, start, images):
+        halves = sums[:, lanes : lanes + 2 * count]
+        term = jnp.dot(halves, twice, preferred_element_type=jnp.float32)
+        term = term * (2.0 * off_weight / count)
+        normed_f = twice[:count].astype(jnp.float32)
         first = jnp.mean(term, 0)
         second = jnp.mean(term * normed_f, 0)
         term = lax.dynamic_slice_in_dim(term, start, images, 0)
@@ -266,10 +241,14 @@
     grad_a = gradient(for_a, all_a, scaled_a, extra_a, col * share, share)
     grad_b = gradient(for_b, all_b, scaled_b, extra_b, row * pair, pair)
 
-    on_diagonal = known[:side] / known[side:]
-    everywhere = parts(for_a)[1] * parts(for_b)[1] * (off_weight / (count * count))
-    everywhere = sum(everywhere[:, i : i + 128] for i in range(0, block, 128))
-    loss = jnp.sum(everywhere + jnp.pad(on_diagonal, ((0, pair - side), (0, 0)))) / (width * side)
+    def whole(sums):
+        sums = sums.astype(jnp.float32)
+        return sums[:, lanes : lanes + count] + sums[:, lanes + count : lanes + 2 * count]
+
+    everywhere = whole(for_a) * whole(for_b) * (off_weight / (count * count * width * side))
+    on_diagonal = known[:side] * (1.0 / (width * side)) / known[side:]
+    everywhere = jnp.sum(jnp.pad(everywhere.reshape(side, pair, count).sum(0), ((0, 0), (0, -count % 128))), 0)
+    loss = jnp.sum(everywhere + jnp.sum(on_diagonal, 0))
     return (loss, grad_a, grad_b)
 
 
@@ -281,8 +260,9 @@
 
     def body(view_a, view_b):
         share, width = view_a.shape
-        fits = view_b.shape == (2 * share, width // 2) and width % 256 == 0
-        fits = fits and share % 8 == 0 and 2 * share >= n_row and n_row * n_col * share % 128 == 0
+        count = share * n_col
+        fits = view_b.shape == (2 * share, width // 2) and width % (128 * n_row) == 0
+        fits = fits and share % 8 == 0 and count <= 128 and 2 * count % 128 == 0
         if square and fits:
             return gram_body(n_row, view_a, view_b)
         return tiled_body(view_a, view_b)

time: 35.9 us -> 35.9 us (level)
  the two profiles are of different devices: /device:TPU:0 before, /device:TPU:9 now
where the time goes in v2:
time: 35.9 us; the launch traced here: 35.7 us
  starting transfers between devices  18.2 us (51%)
  waiting for transfers between devices  12.2 us (34%)
  other arithmetic  3.61 us (10%)
  between operations  0.94 us (3%)
  matrix products  0.67 us (2%)
    ppermute x5, starting transfers between devices, sibling(): return lax.ppermute(value, 'col', [(c, c ^ 1) for c in range(n_col)])  6.84 us
    ppermute x3, starting transfers between devices, across(): return lax.ppermute(value, BOTH, pairs)  5.38 us
    ppermute x3, waiting for transfers between devices, across(): return lax.ppermute(value, BOTH, pairs)  3.87 us
    ppermute x3, waiting for transfers between devices, flip(): return lax.ppermute(value, BOTH, pairs)  3.81 us
    ppermute x2, starting transfers between devices, gram_body(): lax.ppermute(known, BOTH, pairs)  3.29 us
    ppermute x5, waiting for transfers between devices, sibling(): return lax.ppermute(value, 'col', [(c, c ^ 1) for c in range(n_col)])  3.28 us
    ppermute x3, starting transfers between devices, flip(): return lax.ppermute(value, BOTH, pairs)  2.71 us
    convert_element_type x2, other arithmetic, gradient(): (scaled * (term - first - normed_f * second + extra.astype(jnp.float32)))...  1.29 us
  transfers between devices with their start and end apart: 13, of which 11 were waited for; matrix products, arithmetic and copies ran while one was open for 2% of the time, Pallas kernels for 0%

profile of v2, /device:TPU:9, one launch (start us, length us, event | category | flops | bytes accessed | tf_op | source)
XLA Modules:
  0.0 35.7 jit_solution(4671108989181924360)
XLA Ops:
  0.6 0.7 %collective-permute-start = (bf16[8,2048]{1,0:T(8,128)(2,1)}, bf16[8,2048]{1,0:T(8,128)(2,1)S(1)}, u32[]{:S(2)}, u32[]{:S(2)}) collective-permute-start(bf16[8,2048]{1,0:T(8,128)(2,1)} %param.2), channel_id=1, source_target_pairs={{0,1},{1,0},{2,3},{3,2},{4,5},{5,4},{6,7},{7,6},{8,9},{9,8},{10,11... | collective-permute-start | bytes 98312 | tf_op jit(solution)/shard_map/ppermute | solution.py:67
  1.5 0.9 %collective-permute-done = bf16[8,2048]{1,0:T(8,128)(2,1)S(1)} collective-permute-done((bf16[8,2048]{1,0:T(8,128)(2,1)}, bf16[8,2048]{1,0:T(8,128)(2,1)S(1)}, u32[]{:S(2)}, u32[]{:S(2)}) %collective-permute-start) | collective-permute-done | bytes 32800 | tf_op jit(solution)/shard_map/ppermute | solution.py:67
  2.4 0.3 collective-permute-done.1
  2.8 1.3 %collective-permute-start.4 = (bf16[16,2048]{1,0:T(8,128)(2,1)S(1)}, bf16[16,2048]{1,0:T(8,128)(2,1)S(1)}, u32[]{:S(2)}, u32[]{:S(2)}) collective-permute-start(bf16[16,2048]{1,0:T(8,128)(2,1)S(1)} %maximum_select_fusion), channel_id=1, source_target_pairs={{0,2},{1,9},{2,0},{3,11},{4,6},{5,13},{6,4},{7,15},{8,10},{9,1},{1... | collective-permute-start | bytes 196616 | tf_op jit(solution)/shard_map/ppermute | solution.py:76
  4.1 1.2 %collective-permute-start.3 = (bf16[16,2048]{1,0:T(8,128)(2,1)S(1)}, bf16[16,2048]{1,0:T(8,128)(2,1)S(1)}, u32[]{:S(2)}, u32[]{:S(2)}) collective-permute-start(bf16[16,2048]{1,0:T(8,128)(2,1)S(1)} %maximum_select_fusion), channel_id=1, source_target_pairs={{0,4},{1,17},{2,6},{3,19},{4,0},{5,21},{6,2},{7,23},{8,12},{9,25},... | collective-permute-start | bytes 196616 | tf_op jit(solution)/shard_map/ppermute | solution.py:76
  5.3 0.2 collective-permute-start.2
  5.5 0.8 %collective-permute-done.4 = bf16[16,2048]{1,0:T(8,128)(2,1)S(1)} collective-permute-done((bf16[16,2048]{1,0:T(8,128)(2,1)S(1)}, bf16[16,2048]{1,0:T(8,128)(2,1)S(1)}, u32[]{:S(2)}, u32[]{:S(2)}) %collective-permute-start.4) | collective-permute-done | bytes 65568 | tf_op jit(solution)/shard_map/ppermute | solution.py:76
  6.3 0.9 %collective-permute-done.3 = bf16[16,2048]{1,0:T(8,128)(2,1)S(1)} collective-permute-done((bf16[16,2048]{1,0:T(8,128)(2,1)S(1)}, bf16[16,2048]{1,0:T(8,128)(2,1)S(1)}, u32[]{:S(2)}, u32[]{:S(2)}) %collective-permute-start.3) | collective-permute-done | bytes 65568 | tf_op jit(solution)/shard_map/ppermute | solution.py:76
  7.2 2.1 %collective-permute-done.2 = bf16[16,2048]{1,0:T(8,128)(2,1)S(1)} collective-permute-done((bf16[16,2048]{1,0:T(8,128)(2,1)S(1)}, bf16[16,2048]{1,0:T(8,128)(2,1)S(1)}, u32[]{:S(2)}, u32[]{:S(2)}) %collective-permute-start.2) | collective-permute-done | bytes 65568 | tf_op jit(solution)/shard_map/ppermute | solution.py:76
  9.5 1.1 %collective-permute-start.5 = (bf16[64,2048]{1,0:T(8,128)(2,1)S(1)}, bf16[64,2048]{1,0:T(8,128)(2,1)S(1)}, u32[]{:S(2)}, u32[]{:S(2)}) collective-permute-start(bf16[64,2048]{1,0:T(8,128)(2,1)S(1)} %get-tuple-element.25), channel_id=1, source_target_pairs={{0,1},{1,0},{2,3},{3,2},{4,5},{5,4},{6,7},{7,6},{8,9},{9,8},{10,11... | collective-permute-start | bytes 786440 | tf_op jit(solution)/shard_map/ppermute | solution.py:67
  10.7 0.2 fusion.47
  10.9 0.8 %collective-permute-done.5 = bf16[64,2048]{1,0:T(8,128)(2,1)S(1)} collective-permute-done((bf16[64,2048]{1,0:T(8,128)(2,1)S(1)}, bf16[64,2048]{1,0:T(8,128)(2,1)S(1)}, u32[]{:S(2)}, u32[]{:S(2)}) %collective-permute-start.5) | collective-permute-done | bytes 262176 | tf_op jit(solution)/shard_map/ppermute | solution.py:67
  11.9 0.1 fusion.41
  12.0 0.1 convert_reduce_fusion
  12.2 0.1 fusion.12
  12.5 1.9 %collective-permute-start.8 = (bf16[64,768]{1,0:T(8,128)(2,1)S(1)}, bf16[64,768]{1,0:T(8,128)(2,1)S(1)}, u32[]{:S(2)}, u32[]{:S(2)}) collective-permute-start(bf16[64,768]{1,0:T(8,128)(2,1)S(1)} %fusion.23), channel_id=1, source_target_pairs={{0,24},{1,7},{2,26},{3,5},{4,28},{5,3},{6,30},{7,1},{8,16},{9,15},... | collective-permute-start | bytes 294920 | tf_op jit(solution)/shard_map/ppermute | solution.py:85
  14.5 1.9 %collective-permute-start.6 = (bf16[64,768]{1,0:T(8,128)(2,1)S(1)}, bf16[64,768]{1,0:T(8,128)(2,1)S(1)}, u32[]{:S(2)}, u32[]{:S(2)}) collective-permute-start(bf16[64,768]{1,0:T(8,128)(2,1)S(1)} %get-tuple-element.58), channel_id=1, source_target_pairs={{0,8},{1,3},{2,10},{3,1},{4,12},{5,7},{6,14},{7,5},{8,0},{9,11},{1... | collective-permute-start | bytes 294920 | tf_op jit(solution)/shard_map/ppermute | solution.py:85
  16.4 1.6 %collective-permute-start.7 = (bf16[64,768]{1,0:T(8,128)(2,1)S(1)}, bf16[64,768]{1,0:T(8,128)(2,1)S(1)}, u32[]{:S(2)}, u32[]{:S(2)}) collective-permute-start(bf16[64,768]{1,0:T(8,128)(2,1)S(1)} %get-tuple-element.59), channel_id=1, source_target_pairs={{0,16},{1,5},{2,18},{3,7},{4,20},{5,1},{6,22},{7,3},{8,24},{9,13},... | collective-permute-start | bytes 294920 | tf_op jit(solution)/shard_map/ppermute | solution.py:85
  18.0 1.6 %collective-permute-done.6 = bf16[64,768]{1,0:T(8,128)(2,1)S(1)} collective-permute-done((bf16[64,768]{1,0:T(8,128)(2,1)S(1)}, bf16[64,768]{1,0:T(8,128)(2,1)S(1)}, u32[]{:S(2)}, u32[]{:S(2)}) %collective-permute-start.6) | collective-permute-done | bytes 98336 | tf_op jit(solution)/shard_map/ppermute | solution.py:85
  19.6 2.3 %collective-permute-done.7 = bf16[64,768]{1,0:T(8,128)(2,1)S(1)} collective-permute-done((bf16[64,768]{1,0:T(8,128)(2,1)S(1)}, bf16[64,768]{1,0:T(8,128)(2,1)S(1)}, u32[]{:S(2)}, u32[]{:S(2)}) %collective-permute-start.7) | collective-permute-done | bytes 98336 | tf_op jit(solution)/shard_map/ppermute | solution.py:85
  21.9 0.1 convert_add_fusion
  22.0 0.7 %collective-permute-start.11 = (f32[8,128]{1,0:T(8,128)S(1)}, f32[8,128]{1,0:T(8,128)S(1)}, u32[]{:S(2)}, u32[]{:S(2)}) collective-permute-start(f32[8,128]{1,0:T(8,128)S(1)} %select_select_fusion), channel_id=1, source_target_pairs={{2,0},{4,10},{6,20},{7,30}} | collective-permute-start | bytes 12296 | tf_op jit(solution)/shard_map/ppermute | solution.py:210
  22.7 2.6 %collective-permute-start.10 = (f32[8,128]{1,0:T(8,128)S(1)}, f32[8,128]{1,0:T(8,128)S(1)}, u32[]{:S(2)}, u32[]{:S(2)}) collective-permute-start(f32[8,128]{1,0:T(8,128)S(1)} %select_select_fusion), channel_id=1, source_target_pairs={{0,20},{1,27},{2,17},{3,29},{4,30},{5,13},{6,18},{7,22},{8,14},{9,... | collective-permute-start | bytes 12296 | tf_op jit(solution)/shard_map/ppermute | solution.py:210
  25.5 1.2 %collective-permute-done.10 = f32[8,128]{1,0:T(8,128)S(1)} collective-permute-done((f32[8,128]{1,0:T(8,128)S(1)}, f32[8,128]{1,0:T(8,128)S(1)}, u32[]{:S(2)}, u32[]{:S(2)}) %collective-permute-start.10) | collective-permute-done | bytes 4128 | tf_op jit(solution)/shard_map/ppermute | solution.py:210
  26.8 4.9 %collective-permute-start.12 = (f32[8,128]{1,0:T(8,128)S(1)}, f32[8,128]{1,0:T(8,128)S(1)}, u32[]{:S(2)}, u32[]{:S(2)}) collective-permute-start(f32[8,128]{1,0:T(8,128)S(1)} %add_add_fusion), channel_id=1, source_target_pairs={{0,1},{1,0},{2,3},{3,2},{4,5},{5,4},{6,7},{7,6},{8,9},{9,8},{10,11... | collective-permute-start | bytes 12296 | tf_op jit(solution)/shard_map/ppermute | solution.py:67
  31.8 0.7 %collective-permute-done.12 = f32[8,128]{1,0:T(8,128)S(1)} collective-permute-done((f32[8,128]{1,0:T(8,128)S(1)}, f32[8,128]{1,0:T(8,128)S(1)}, u32[]{:S(2)}, u32[]{:S(2)}) %collective-permute-start.12) | collective-permute-done | bytes 4128 | tf_op jit(solution)/shard_map/ppermute | solution.py:67
  32.6 0.5 %collective-permute-done.9 = bf16[64,640]{1,0:T(8,128)(2,1)S(1)} collective-permute-done((bf16[64,640]{1,0:T(8,128)(2,1)S(1)}, bf16[64,640]{1,0:T(8,128)(2,1)S(1)}, u32[]{:S(2)}, u32[]{:S(2)}) %collective-permute-start.9) | collective-permute-done | bytes 81952 | tf_op jit(solution)/shard_map/ppermute | solution.py:67
  33.3 0.2 fusion.39
  33.5 0.3 fusion.38
  33.8 0.6 %add_reduce_fusion = f32[]{:T(128)} fusion(f32[128]{0:T(128)S(1)} %pad_reduce_fusion, f32[128]{0:T(128)S(1)} %fusion.32), kind=kLoop, calls=%fused_computation.111 | loop fusion | flops 255 | bytes 1028 | tf_op jit(solution)/shard_map/reduce_sum | solution.py:251
  34.4 0.6 %multiply_convert_fusion.1 = bf16[8,2048]{1,0:T(8,128)(2,1)} fusion(f32[64,2048]{1,0:T(8,128)S(1)} %get-tuple-element.17, s32[]{:T(128)S(6)} %select_n.188, f32[64,2048]{1,0:T(8,128)S(1)} %get-tuple-element.68, bf16[16,2048]{1,0:T(8,128)(2,1)S(1)} %pad_maximum_fusion.11, f32[2048]{0:T(1024)S(1)} %broadcast_multiply_fusion, ...), kind=kLoop, calls=%fused_computation.56 | loop fusion | flops 131072 | bytes 253957 | tf_op jit(solution)/shard_map/convert_element_type | solution.py:237
  35.1 0.6 %multiply_convert_fusion = bf16[16,1024]{1,0:T(8,128)(2,1)} fusion(f32[64,1024]{1,0:T(8,128)S(1)} %get-tuple-element.15, s32[]{:T(128)S(6)} %select_n.174, f32[64,1024]{1,0:T(8,128)S(1)} %get-tuple-element.69, bf16[16,512]{1,0:T(8,128)(2,1)S(1)} %get-tuple-element.51, bf16[16,512]{1,0:T(8,128)(2,1)S(1)} %get-tuple-element.52, ...), kind=kLoop, calls=%fused_computation.55 | loop fusion | flops 262144 | bytes 241669 | tf_op jit(solution)/shard_map/convert_element_type | solution.py:237
  (51 shorter events, 1.4 us)
Async XLA Ops:
  0.6 1.8 %collective-permute-start = (bf16[8,2048]{1,0:T(8,128)(2,1)}, bf16[8,2048]{1,0:T(8,128)(2,1)S(1)}, u32[]{:S(2)}, u32[]{:S(2)}) collective-permute-start(bf16[8,2048]{1,0:T(8,128)(2,1)} %param.2), channel_id=1, source_target_pairs={{0,1},{1,0},{2,3},{3,2},{4,5},{5,4},{6,7},{7,6},{8,9},{9,8},{10,11... | collective-permute-start | bytes 98312 | tf_op jit(solution)/shard_map/ppermute | solution.py:67
  1.4 1.4 %collective-permute-start.1 = (bf16[16,1024]{1,0:T(8,128)(2,1)}, bf16[16,1024]{1,0:T(8,128)(2,1)S(1)}, u32[]{:S(2)}, u32[]{:S(2)}) collective-permute-start(bf16[16,1024]{1,0:T(8,128)(2,1)} %param.3), channel_id=1, source_target_pairs={{0,1},{1,0},{2,3},{3,2},{4,5},{5,4},{6,7},{7,6},{8,9},{9,8},{10,11... | collective-permute-start | bytes 98312 | tf_op jit(solution)/shard_map/ppermute | solution.py:67
  1.5 1.3 %copy-start = (bf16[8,2048]{1,0:T(8,128)(2,1)S(1)}, bf16[8,2048]{1,0:T(8,128)(2,1)}, u32[]{:S(2)}) copy-start(bf16[8,2048]{1,0:T(8,128)(2,1)} %param.2) | copy-start | bytes 98308
  1.5 1.3 %copy-start.1 = (bf16[16,1024]{1,0:T(8,128)(2,1)S(1)}, bf16[16,1024]{1,0:T(8,128)(2,1)}, u32[]{:S(2)}) copy-start(bf16[16,1024]{1,0:T(8,128)(2,1)} %param.3) | copy-start | bytes 98308
  2.8 3.5 %collective-permute-start.4 = (bf16[16,2048]{1,0:T(8,128)(2,1)S(1)}, bf16[16,2048]{1,0:T(8,128)(2,1)S(1)}, u32[]{:S(2)}, u32[]{:S(2)}) collective-permute-start(bf16[16,2048]{1,0:T(8,128)(2,1)S(1)} %maximum_select_fusion), channel_id=1, source_target_pairs={{0,2},{1,9},{2,0},{3,11},{4,6},{5,13},{6,4},{7,15},{8,10},{9,1},{1... | collective-permute-start | bytes 196616 | tf_op jit(solution)/shard_map/ppermute | solution.py:76
  4.1 3.1 %collective-permute-start.3 = (bf16[16,2048]{1,0:T(8,128)(2,1)S(1)}, bf16[16,2048]{1,0:T(8,128)(2,1)S(1)}, u32[]{:S(2)}, u32[]{:S(2)}) collective-permute-start(bf16[16,2048]{1,0:T(8,128)(2,1)S(1)} %maximum_select_fusion), channel_id=1, source_target_pairs={{0,4},{1,17},{2,6},{3,19},{4,0},{5,21},{6,2},{7,23},{8,12},{9,25},... | collective-permute-start | bytes 196616 | tf_op jit(solution)/shard_map/ppermute | solution.py:76
  5.3 4.0 %collective-permute-start.2 = (bf16[16,2048]{1,0:T(8,128)(2,1)S(1)}, bf16[16,2048]{1,0:T(8,128)(2,1)S(1)}, u32[]{:S(2)}, u32[]{:S(2)}) collective-permute-start(bf16[16,2048]{1,0:T(8,128)(2,1)S(1)} %maximum_select_fusion), channel_id=1, source_target_pairs={{0,6},{1,25},{2,4},{3,27},{4,2},{5,29},{6,0},{7,31},{8,14},{9,17},... | collective-permute-start | bytes 196616 | tf_op jit(solution)/shard_map/ppermute | solution.py:76
  9.5 2.2 %collective-permute-start.5 = (bf16[64,2048]{1,0:T(8,128)(2,1)S(1)}, bf16[64,2048]{1,0:T(8,128)(2,1)S(1)}, u32[]{:S(2)}, u32[]{:S(2)}) collective-permute-start(bf16[64,2048]{1,0:T(8,128)(2,1)S(1)} %get-tuple-element.25), channel_id=1, source_target_pairs={{0,1},{1,0},{2,3},{3,2},{4,5},{5,4},{6,7},{7,6},{8,9},{9,8},{10,11... | collective-permute-start | bytes 786440 | tf_op jit(solution)/shard_map/ppermute | solution.py:67
  12.5 5.5 %collective-permute-start.8 = (bf16[64,768]{1,0:T(8,128)(2,1)S(1)}, bf16[64,768]{1,0:T(8,128)(2,1)S(1)}, u32[]{:S(2)}, u32[]{:S(2)}) collective-permute-start(bf16[64,768]{1,0:T(8,128)(2,1)S(1)} %fusion.23), channel_id=1, source_target_pairs={{0,24},{1,7},{2,26},{3,5},{4,28},{5,3},{6,30},{7,1},{8,16},{9,15},... | collective-permute-start | bytes 294920 | tf_op jit(solution)/shard_map/ppermute | solution.py:85
  14.5 5.1 %collective-permute-start.6 = (bf16[64,768]{1,0:T(8,128)(2,1)S(1)}, bf16[64,768]{1,0:T(8,128)(2,1)S(1)}, u32[]{:S(2)}, u32[]{:S(2)}) collective-permute-start(bf16[64,768]{1,0:T(8,128)(2,1)S(1)} %get-tuple-element.58), channel_id=1, source_target_pairs={{0,8},{1,3},{2,10},{3,1},{4,12},{5,7},{6,14},{7,5},{8,0},{9,11},{1... | collective-permute-start | bytes 294920 | tf_op jit(solution)/shard_map/ppermute | solution.py:85
  16.4 5.5 %collective-permute-start.7 = (bf16[64,768]{1,0:T(8,128)(2,1)S(1)}, bf16[64,768]{1,0:T(8,128)(2,1)S(1)}, u32[]{:S(2)}, u32[]{:S(2)}) collective-permute-start(bf16[64,768]{1,0:T(8,128)(2,1)S(1)} %get-tuple-element.59), channel_id=1, source_target_pairs={{0,16},{1,5},{2,18},{3,7},{4,20},{5,1},{6,22},{7,3},{8,24},{9,13},... | collective-permute-start | bytes 294920 | tf_op jit(solution)/shard_map/ppermute | solution.py:85
  22.0 3.4 %collective-permute-start.11 = (f32[8,128]{1,0:T(8,128)S(1)}, f32[8,128]{1,0:T(8,128)S(1)}, u32[]{:S(2)}, u32[]{:S(2)}) collective-permute-start(f32[8,128]{1,0:T(8,128)S(1)} %select_select_fusion), channel_id=1, source_target_pairs={{2,0},{4,10},{6,20},{7,30}} | collective-permute-start | bytes 12296 | tf_op jit(solution)/shard_map/ppermute | solution.py:210
  22.7 4.0 %collective-permute-start.10 = (f32[8,128]{1,0:T(8,128)S(1)}, f32[8,128]{1,0:T(8,128)S(1)}, u32[]{:S(2)}, u32[]{:S(2)}) collective-permute-start(f32[8,128]{1,0:T(8,128)S(1)} %select_select_fusion), channel_id=1, source_target_pairs={{0,20},{1,27},{2,17},{3,29},{4,30},{5,13},{6,18},{7,22},{8,14},{9,... | collective-permute-start | bytes 12296 | tf_op jit(solution)/shard_map/ppermute | solution.py:210
  26.8 5.8 %collective-permute-start.12 = (f32[8,128]{1,0:T(8,128)S(1)}, f32[8,128]{1,0:T(8,128)S(1)}, u32[]{:S(2)}, u32[]{:S(2)}) collective-permute-start(f32[8,128]{1,0:T(8,128)S(1)} %add_add_fusion), channel_id=1, source_target_pairs={{0,1},{1,0},{2,3},{3,2},{4,5},{5,4},{6,7},{7,6},{8,9},{9,8},{10,11... | collective-permute-start | bytes 12296 | tf_op jit(solution)/shard_map/ppermute | solution.py:67
  31.8 1.3 %collective-permute-start.9 = (bf16[64,640]{1,0:T(8,128)(2,1)S(1)}, bf16[64,640]{1,0:T(8,128)(2,1)S(1)}, u32[]{:S(2)}, u32[]{:S(2)}) collective-permute-start(bf16[64,640]{1,0:T(8,128)(2,1)S(1)} %pad_maximum_fusion.10), channel_id=1, source_target_pairs={{0,1},{1,0},{2,3},{3,2},{4,5},{5,4},{6,7},{7,6},{8,9},{9,8},{10,11... | collective-permute-start | bytes 245768 | tf_op jit(solution)/shard_map/ppermute | solution.py:67

commit v3 on v2

--- a/solution.py
+++ b/solution.py
@@ -113,40 +113,62 @@
 
 def meetings(side):
     chips = [(row, z) for row in range(side) for z in range(side)]
-    owners = {v: [(r, z, k) for r, z in chips for k in (0, 1) if (r, z)[1 - k] == v] for v in range(side)}
-    wanted = {(r, z): [v for v in range(side) if v not in (r, z)] for r, z in chips}
 
     def hops(p, q):
         return bin(p[0] ^ q[0]).count("1") + abs(p[1] - q[1])
 
-    rounds = []
-    while any(wanted.values()):
-        asks = []
-        for (r, z), left in wanted.items():
-            left.sort(key=lambda v: (v - r - 1) % side if r == z else v)
-            asks += [((r, z), v) for v in left[-2:]]
-
-        def place(ask, taken, limit, seen):
-            for owner in owners[ask[1]]:
-                if owner not in seen and hops(owner, ask[0]) <= limit:
-                    seen.add(owner)
-                    if owner not in taken or place(taken[owner], taken, limit, seen):
-                        taken[owner] = ask
-                        return True
-            return False
-
-        for limit in range(3 * side):
-            taken = {}
-            if all([place(ask, taken, limit, set()) for ask in asks]):
-                break
-        heard, pairs = dict.fromkeys(chips, 0), []
-        for (r, z, k), (chip, v) in taken.items():
-            receiver = (chip[0] * side + chip[1]) * 2 + heard[chip]
-            pairs.append(((r * side + z) * 2 + k, receiver))
-            heard[chip] += 1
-            wanted[chip].remove(v)
-        rounds.append(sorted(pairs))
-    return rounds
+    def search(choices, order, used, chosen):
+        if len(chosen) == len(order):
+            return dict(chosen)
+        chip = order[len(chosen)]
+        for pair in choices[chip]:
+            if all(used[q] < 2 for q in pair):
+                for q in pair:
+                    used[q] += 1
+                found = search(choices, order, used, chosen + [(chip, pair)])
+                if found:
+                    return found
+                for q in pair:
+                    used[q] -= 1
+        return None
+
+    if side > 6:
+        return None
+    for limit in range(1, 3 * side):
+        choices = {
+            p: [
+                (q, t)
+                for i, q in enumerate(chips)
+                for t in chips[i + 1 :]
+                if max(hops(p, q), hops(p, t)) <= limit and len({*p, *q, *t}) == side
+            ]
+            for p in chips
+        }
+        if all(choices.values()):
+            order = sorted(chips, key=lambda p: len(choices[p]))
+            found = search(choices, order, dict.fromkeys(chips, 0), [])
+            if found:
+                return found
+    return None
+
+
+def hear(known, side):
+    plan = meetings(side)
+    if plan is None:
+        step = 1
+        while step < side:
+            known = known + lax.ppermute(
+                known, "col", [(c, c ^ (2 * step)) for c in range(2 * side)]
+            )
+            step *= 2
+        return known
+    used, pairs = {}, []
+    for (row, z), pair in plan.items():
+        for core, chip in enumerate(pair):
+            from_core = used.get(chip, 0)
+            used[chip] = from_core + 1
+            pairs.append(((chip[0] * side + chip[1]) * 2 + from_core, (row * side + z) * 2 + core))
+    return known + lax.ppermute(known, BOTH, pairs)
 
 
 def gram_body(side, view_a, view_b):
@@ -200,15 +222,21 @@
     gram = summed[:, lanes : lanes + count] + summed[:, lanes + count : lanes + 2 * count]
     part = summed[:1, lanes + 2 * count :] + summed[count // 2 : count // 2 + 1, lanes + 2 * count :]
 
-    sent = jnp.concatenate([summed[:, :lanes].astype(jnp.bfloat16), *split(gram)], 1)
+    part = jnp.concatenate([jnp.broadcast_to(x, (count // 2, 128)) for x in split(part)], 0)
+    sent = jnp.concatenate([summed[:, :lanes].astype(jnp.bfloat16), *split(gram), part], 1)
     came = sibling(sent, n_col)
     for_a = jnp.where(is_a, came, sent)
     for_b = jnp.where(is_a, sent, came)
 
+    def part_of(sums):
+        sums = sums[:, lanes + 2 * count :].astype(jnp.float32)
+        return sums[:1] + sums[count // 2 : count // 2 + 1]
+
     slots = lax.broadcasted_iota(jnp.int32, (2 * side, 128), 0)
-    known = jnp.where((slots & (side - 1)) == jnp.where(is_a, z, row), jnp.where(slots < side, part, 1.0), 0.0)
-    known = known + sum(lax.ppermute(known, BOTH, pairs) for pairs in meetings(side))
-    known = known + sibling(known, n_col)
+    block, sums_in = slots & (side - 1), slots < side
+    known = jnp.where(block == z, jnp.where(sums_in, part_of(for_b), 1.0), 0.0)
+    known = known + jnp.where(block == row, jnp.where(sums_in, part_of(for_a), 1.0), 0.0)
+    known = hear(known, side)
 
     twice = [jnp.where(is_a, normed, other_normed)] * 2
     all_a = jnp.concatenate(twice, 0)
@@ -246,8 +274,10 @@
         return sums[:, lanes : lanes + count] + sums[:, lanes + count : lanes + 2 * count]
 
     everywhere = whole(for_a) * whole(for_b) * (off_weight / (count * count * width * side))
+    everywhere = jnp.pad(jnp.sum(everywhere, 0), (0, 128 - count))
+    known, grad_a, grad_b, everywhere = lax.optimization_barrier((known, grad_a, grad_b, everywhere))
+    known = known + sibling(known, n_col)
     on_diagonal = known[:side] * (1.0 / (width * side)) / known[side:]
-    everywhere = jnp.sum(jnp.pad(everywhere.reshape(side, pair, count).sum(0), ((0, 0), (0, -count % 128))), 0)
     loss = jnp.sum(everywhere + jnp.sum(on_diagonal, 0))
     return (loss, grad_a, grad_b)
 

time: 35.9 us -> 32.8 us (0.914)
  the two profiles are of different devices: /device:TPU:9 before, /device:TPU:0 now
where the time goes in v3:
time: 32.8 us; the launch traced here: 32.7 us
  waiting for transfers between devices  16.6 us (51%)
  starting transfers between devices  10.6 us (32%)
  other arithmetic  3.63 us (11%)
  between operations  1.01 us (3%)
  matrix products  0.67 us (2%)
    ppermute x3, waiting for transfers between devices, flip(): return lax.ppermute(value, BOTH, pairs)  6.04 us
    ppermute x3, starting transfers between devices, flip(): return lax.ppermute(value, BOTH, pairs)  5.39 us
    ppermute x5, waiting for transfers between devices, sibling(): return lax.ppermute(value, 'col', [(c, c ^ 1) for c in range(n_col)])  4.84 us
    ppermute x3, waiting for transfers between devices, across(): return lax.ppermute(value, BOTH, pairs)  4.08 us
    ppermute x3, starting transfers between devices, across(): return lax.ppermute(value, BOTH, pairs)  3.61 us
    ppermute x1, waiting for transfers between devices, hear(): return known + lax.ppermute(known, BOTH, pairs)  1.68 us
    convert_element_type x2, other arithmetic, gradient(): (scaled * (term - first - normed_f * second + extra.astype(jnp.float32)))...  1.3 us
    ppermute x1, starting transfers between devices, hear(): return known + lax.ppermute(known, BOTH, pairs)  0.89 us
  transfers between devices with their start and end apart: 12, of which 11 were waited for; matrix products, arithmetic and copies ran while one was open for 7% of the time, Pallas kernels for 0%

profile of v3, /device:TPU:0, one launch (start us, length us, event | category | flops | bytes accessed | tf_op | source)
XLA Modules:
  0.0 32.7 jit_solution(14592430032385833864)
XLA Ops:
  0.6 0.5 %collective-permute-start = (bf16[8,2048]{1,0:T(8,128)(2,1)}, bf16[8,2048]{1,0:T(8,128)(2,1)S(1)}, u32[]{:S(2)}, u32[]{:S(2)}) collective-permute-start(bf16[8,2048]{1,0:T(8,128)(2,1)} %param.2), channel_id=1, source_target_pairs={{0,1},{1,0},{2,3},{3,2},{4,5},{5,4},{6,7},{7,6},{8,9},{9,8},{10,11... | collective-permute-start | bytes 98312 | tf_op jit(solution)/shard_map/ppermute | solution.py:67
  1.3 0.9 %collective-permute-done = bf16[8,2048]{1,0:T(8,128)(2,1)S(1)} collective-permute-done((bf16[8,2048]{1,0:T(8,128)(2,1)}, bf16[8,2048]{1,0:T(8,128)(2,1)S(1)}, u32[]{:S(2)}, u32[]{:S(2)}) %collective-permute-start) | collective-permute-done | bytes 32800 | tf_op jit(solution)/shard_map/ppermute | solution.py:67
  2.2 0.3 %collective-permute-done.1 = bf16[16,1024]{1,0:T(8,128)(2,1)S(1)} collective-permute-done((bf16[16,1024]{1,0:T(8,128)(2,1)}, bf16[16,1024]{1,0:T(8,128)(2,1)S(1)}, u32[]{:S(2)}, u32[]{:S(2)}) %collective-permute-start.1) | collective-permute-done | bytes 32800 | tf_op jit(solution)/shard_map/ppermute | solution.py:67
  2.6 2.8 %collective-permute-start.4 = (bf16[16,2048]{1,0:T(8,128)(2,1)S(1)}, bf16[16,2048]{1,0:T(8,128)(2,1)S(1)}, u32[]{:S(2)}, u32[]{:S(2)}) collective-permute-start(bf16[16,2048]{1,0:T(8,128)(2,1)S(1)} %maximum_select_fusion), channel_id=1, source_target_pairs={{0,2},{1,9},{2,0},{3,11},{4,6},{5,13},{6,4},{7,15},{8,10},{9,1},{1... | collective-permute-start | bytes 196616 | tf_op jit(solution)/shard_map/ppermute | solution.py:76
  5.4 2.6 %collective-permute-start.3 = (bf16[16,2048]{1,0:T(8,128)(2,1)S(1)}, bf16[16,2048]{1,0:T(8,128)(2,1)S(1)}, u32[]{:S(2)}, u32[]{:S(2)}) collective-permute-start(bf16[16,2048]{1,0:T(8,128)(2,1)S(1)} %maximum_select_fusion), channel_id=1, source_target_pairs={{0,4},{1,17},{2,6},{3,19},{4,0},{5,21},{6,2},{7,23},{8,12},{9,25},... | collective-permute-start | bytes 196616 | tf_op jit(solution)/shard_map/ppermute | solution.py:76
  8.0 3.3 %collective-permute-done.3 = bf16[16,2048]{1,0:T(8,128)(2,1)S(1)} collective-permute-done((bf16[16,2048]{1,0:T(8,128)(2,1)S(1)}, bf16[16,2048]{1,0:T(8,128)(2,1)S(1)}, u32[]{:S(2)}, u32[]{:S(2)}) %collective-permute-start.3) | collective-permute-done | bytes 65568 | tf_op jit(solution)/shard_map/ppermute | solution.py:76
  11.3 2.8 %collective-permute-done.2 = bf16[16,2048]{1,0:T(8,128)(2,1)S(1)} collective-permute-done((bf16[16,2048]{1,0:T(8,128)(2,1)S(1)}, bf16[16,2048]{1,0:T(8,128)(2,1)S(1)}, u32[]{:S(2)}, u32[]{:S(2)}) %collective-permute-start.2) | collective-permute-done | bytes 65568 | tf_op jit(solution)/shard_map/ppermute | solution.py:76
  14.2 0.1 fusion.7
  14.4 0.2 fusion.56
  14.6 1.1 %collective-permute-done.5 = bf16[64,2048]{1,0:T(8,128)(2,1)S(1)} collective-permute-done((bf16[64,2048]{1,0:T(8,128)(2,1)S(1)}, bf16[64,2048]{1,0:T(8,128)(2,1)S(1)}, u32[]{:S(2)}, u32[]{:S(2)}) %collective-permute-start.5) | collective-permute-done | bytes 262176 | tf_op jit(solution)/shard_map/ppermute | solution.py:67
  15.8 0.1 fusion.4
  15.9 0.1 fusion.52
  16.1 0.1 convert_reduce_fusion
  16.3 0.1 fusion.12
  16.6 2.5 %collective-permute-start.8 = (bf16[64,768]{1,0:T(8,128)(2,1)S(1)}, bf16[64,768]{1,0:T(8,128)(2,1)S(1)}, u32[]{:S(2)}, u32[]{:S(2)}) collective-permute-start(bf16[64,768]{1,0:T(8,128)(2,1)S(1)} %fusion.23), channel_id=1, source_target_pairs={{0,24},{1,7},{2,26},{3,5},{4,28},{5,3},{6,30},{7,1},{8,16},{9,15},... | collective-permute-start | bytes 294920 | tf_op jit(solution)/shard_map/ppermute | solution.py:85
  19.1 0.6 %collective-permute-start.6 = (bf16[64,768]{1,0:T(8,128)(2,1)S(1)}, bf16[64,768]{1,0:T(8,128)(2,1)S(1)}, u32[]{:S(2)}, u32[]{:S(2)}) collective-permute-start(bf16[64,768]{1,0:T(8,128)(2,1)S(1)} %get-tuple-element.68), channel_id=1, source_target_pairs={{0,8},{1,3},{2,10},{3,1},{4,12},{5,7},{6,14},{7,5},{8,0},{9,11},{1... | collective-permute-start | bytes 294920 | tf_op jit(solution)/shard_map/ppermute | solution.py:85
  19.7 0.5 %collective-permute-start.7 = (bf16[64,768]{1,0:T(8,128)(2,1)S(1)}, bf16[64,768]{1,0:T(8,128)(2,1)S(1)}, u32[]{:S(2)}, u32[]{:S(2)}) collective-permute-start(bf16[64,768]{1,0:T(8,128)(2,1)S(1)} %get-tuple-element.69), channel_id=1, source_target_pairs={{0,16},{1,5},{2,18},{3,7},{4,20},{5,1},{6,22},{7,3},{8,24},{9,13},... | collective-permute-start | bytes 294920 | tf_op jit(solution)/shard_map/ppermute | solution.py:85
  20.3 1.8 %collective-permute-done.8 = bf16[64,768]{1,0:T(8,128)(2,1)S(1)} collective-permute-done((bf16[64,768]{1,0:T(8,128)(2,1)S(1)}, bf16[64,768]{1,0:T(8,128)(2,1)S(1)}, u32[]{:S(2)}, u32[]{:S(2)}) %collective-permute-start.8) | collective-permute-done | bytes 98336 | tf_op jit(solution)/shard_map/ppermute | solution.py:85
  22.1 1.7 %collective-permute-done.6 = bf16[64,768]{1,0:T(8,128)(2,1)S(1)} collective-permute-done((bf16[64,768]{1,0:T(8,128)(2,1)S(1)}, bf16[64,768]{1,0:T(8,128)(2,1)S(1)}, u32[]{:S(2)}, u32[]{:S(2)}) %collective-permute-start.6) | collective-permute-done | bytes 98336 | tf_op jit(solution)/shard_map/ppermute | solution.py:85
  23.8 0.5 %collective-permute-done.7 = bf16[64,768]{1,0:T(8,128)(2,1)S(1)} collective-permute-done((bf16[64,768]{1,0:T(8,128)(2,1)S(1)}, bf16[64,768]{1,0:T(8,128)(2,1)S(1)}, u32[]{:S(2)}, u32[]{:S(2)}) %collective-permute-start.7) | collective-permute-done | bytes 98336 | tf_op jit(solution)/shard_map/ppermute | solution.py:85
  24.4 0.1 convert_add_fusion
  24.8 1.3 %collective-permute-done.9 = bf16[64,768]{1,0:T(8,128)(2,1)S(1)} collective-permute-done((bf16[64,768]{1,0:T(8,128)(2,1)S(1)}, bf16[64,768]{1,0:T(8,128)(2,1)S(1)}, u32[]{:S(2)}, u32[]{:S(2)}) %collective-permute-start.9) | collective-permute-done | bytes 98336 | tf_op jit(solution)/shard_map/ppermute | solution.py:67
  26.0 0.1 fusion.50
  26.3 0.9 %collective-permute-start.10 = (f32[8,128]{1,0:T(8,128)S(1)}, f32[8,128]{1,0:T(8,128)S(1)}, u32[]{:S(2)}, u32[]{:S(2)}) collective-permute-start(f32[8,128]{1,0:T(8,128)S(1)} %select_add_fusion), channel_id=1, source_target_pairs={{18,0},{24,1},{6,30},{12,31},{13,8},{25,9},{4,22},{14,23},{16,2},{... | collective-permute-start | bytes 12296 | tf_op jit(solution)/shard_map/ppermute | solution.py:171
  27.2 0.2 fusion.48
  27.4 0.3 fusion.47
  27.7 0.7 %multiply_convert_fusion.1 = bf16[8,2048]{1,0:T(8,128)(2,1)} fusion(f32[64,2048]{1,0:T(8,128)S(1)} %get-tuple-element.29, s32[]{:T(128)S(6)} %select_n.195, f32[64,2048]{1,0:T(8,128)S(1)} %get-tuple-element.78, bf16[16,2048]{1,0:T(8,128)(2,1)S(1)} %pad_maximum_fusion.10, f32[2048]{0:T(1024)S(1)} %broadcast_multiply_fusion, ...), kind=kLoop, calls=%fused_computation.56 | loop fusion | flops 131072 | bytes 253957 | tf_op jit(solution)/shard_map/convert_element_type | solution.py:265
  28.4 0.6 %multiply_convert_fusion = bf16[16,1024]{1,0:T(8,128)(2,1)} fusion(f32[64,1024]{1,0:T(8,128)S(1)} %get-tuple-element.27, s32[]{:T(128)S(6)} %select_n.179, f32[64,1024]{1,0:T(8,128)S(1)} %get-tuple-element.79, bf16[16,512]{1,0:T(8,128)(2,1)S(1)} %get-tuple-element.62, bf16[16,512]{1,0:T(8,128)(2,1)S(1)} %get-tuple-element.63, ...), kind=kLoop, calls=%fused_computation.55 | loop fusion | flops 262144 | bytes 241669 | tf_op jit(solution)/shard_map/convert_element_type | solution.py:265
  29.0 0.1 fusion.30
  29.1 1.7 %collective-permute-done.10 = f32[8,128]{1,0:T(8,128)S(1)} collective-permute-done((f32[8,128]{1,0:T(8,128)S(1)}, f32[8,128]{1,0:T(8,128)S(1)}, u32[]{:S(2)}, u32[]{:S(2)}) %collective-permute-start.10) | collective-permute-done | bytes 4128 | tf_op jit(solution)/shard_map/ppermute | solution.py:171
  30.9 1.2 %collective-permute-done.11 = f32[8,128]{1,0:T(8,128)S(1)} collective-permute-done((f32[8,128]{1,0:T(8,128)S(1)}, f32[8,128]{1,0:T(8,128)S(1)}, u32[]{:S(2)}, u32[]{:S(2)}) %collective-permute-start.11) | collective-permute-done | bytes 4128 | tf_op jit(solution)/shard_map/ppermute | solution.py:67
  32.1 0.6 %add_reduce_fusion = f32[]{:T(128)} fusion(f32[128]{0:T(128)S(1)} %pad.4, f32[128]{0:T(128)S(1)} %fusion.33), kind=kLoop, calls=%fused_computation.121 | loop fusion | flops 255 | bytes 1028 | tf_op jit(solution)/shard_map/reduce_sum | solution.py:281
  (54 shorter events, 1.2 us)
Async XLA Ops:
  0.6 1.6 %collective-permute-start = (bf16[8,2048]{1,0:T(8,128)(2,1)}, bf16[8,2048]{1,0:T(8,128)(2,1)S(1)}, u32[]{:S(2)}, u32[]{:S(2)}) collective-permute-start(bf16[8,2048]{1,0:T(8,128)(2,1)} %param.2), channel_id=1, source_target_pairs={{0,1},{1,0},{2,3},{3,2},{4,5},{5,4},{6,7},{7,6},{8,9},{9,8},{10,11... | collective-permute-start | bytes 98312 | tf_op jit(solution)/shard_map/ppermute | solution.py:67
  1.1 1.4 %collective-permute-start.1 = (bf16[16,1024]{1,0:T(8,128)(2,1)}, bf16[16,1024]{1,0:T(8,128)(2,1)S(1)}, u32[]{:S(2)}, u32[]{:S(2)}) collective-permute-start(bf16[16,1024]{1,0:T(8,128)(2,1)} %param.3), channel_id=1, source_target_pairs={{0,1},{1,0},{2,3},{3,2},{4,5},{5,4},{6,7},{7,6},{8,9},{9,8},{10,11... | collective-permute-start | bytes 98312 | tf_op jit(solution)/shard_map/ppermute | solution.py:67
  1.2 1.3 %copy-start = (bf16[8,2048]{1,0:T(8,128)(2,1)S(1)}, bf16[8,2048]{1,0:T(8,128)(2,1)}, u32[]{:S(2)}) copy-start(bf16[8,2048]{1,0:T(8,128)(2,1)} %param.2) | copy-start | bytes 98308
  1.2 1.3 %copy-start.1 = (bf16[16,1024]{1,0:T(8,128)(2,1)S(1)}, bf16[16,1024]{1,0:T(8,128)(2,1)}, u32[]{:S(2)}) copy-start(bf16[16,1024]{1,0:T(8,128)(2,1)} %param.3) | copy-start | bytes 98308
  2.6 5.4 %collective-permute-start.4 = (bf16[16,2048]{1,0:T(8,128)(2,1)S(1)}, bf16[16,2048]{1,0:T(8,128)(2,1)S(1)}, u32[]{:S(2)}, u32[]{:S(2)}) collective-permute-start(bf16[16,2048]{1,0:T(8,128)(2,1)S(1)} %maximum_select_fusion), channel_id=1, source_target_pairs={{0,2},{1,9},{2,0},{3,11},{4,6},{5,13},{6,4},{7,15},{8,10},{9,1},{1... | collective-permute-start | bytes 196616 | tf_op jit(solution)/shard_map/ppermute | solution.py:76
  5.4 5.9 %collective-permute-start.3 = (bf16[16,2048]{1,0:T(8,128)(2,1)S(1)}, bf16[16,2048]{1,0:T(8,128)(2,1)S(1)}, u32[]{:S(2)}, u32[]{:S(2)}) collective-permute-start(bf16[16,2048]{1,0:T(8,128)(2,1)S(1)} %maximum_select_fusion), channel_id=1, source_target_pairs={{0,4},{1,17},{2,6},{3,19},{4,0},{5,21},{6,2},{7,23},{8,12},{9,25},... | collective-permute-start | bytes 196616 | tf_op jit(solution)/shard_map/ppermute | solution.py:76
  8.0 6.1 %collective-permute-start.2 = (bf16[16,2048]{1,0:T(8,128)(2,1)S(1)}, bf16[16,2048]{1,0:T(8,128)(2,1)S(1)}, u32[]{:S(2)}, u32[]{:S(2)}) collective-permute-start(bf16[16,2048]{1,0:T(8,128)(2,1)S(1)} %maximum_select_fusion), channel_id=1, source_target_pairs={{0,6},{1,25},{2,4},{3,27},{4,2},{5,29},{6,0},{7,31},{8,14},{9,17},... | collective-permute-start | bytes 196616 | tf_op jit(solution)/shard_map/ppermute | solution.py:76
  14.2 1.6 %collective-permute-start.5 = (bf16[64,2048]{1,0:T(8,128)(2,1)S(1)}, bf16[64,2048]{1,0:T(8,128)(2,1)S(1)}, u32[]{:S(2)}, u32[]{:S(2)}) collective-permute-start(bf16[64,2048]{1,0:T(8,128)(2,1)S(1)} %get-tuple-element.33), channel_id=1, source_target_pairs={{0,1},{1,0},{2,3},{3,2},{4,5},{5,4},{6,7},{7,6},{8,9},{9,8},{10,11... | collective-permute-start | bytes 786440 | tf_op jit(solution)/shard_map/ppermute | solution.py:67
  16.6 5.6 %collective-permute-start.8 = (bf16[64,768]{1,0:T(8,128)(2,1)S(1)}, bf16[64,768]{1,0:T(8,128)(2,1)S(1)}, u32[]{:S(2)}, u32[]{:S(2)}) collective-permute-start(bf16[64,768]{1,0:T(8,128)(2,1)S(1)} %fusion.23), channel_id=1, source_target_pairs={{0,24},{1,7},{2,26},{3,5},{4,28},{5,3},{6,30},{7,1},{8,16},{9,15},... | collective-permute-start | bytes 294920 | tf_op jit(solution)/shard_map/ppermute | solution.py:85
  19.1 4.7 %collective-permute-start.6 = (bf16[64,768]{1,0:T(8,128)(2,1)S(1)}, bf16[64,768]{1,0:T(8,128)(2,1)S(1)}, u32[]{:S(2)}, u32[]{:S(2)}) collective-permute-start(bf16[64,768]{1,0:T(8,128)(2,1)S(1)} %get-tuple-element.68), channel_id=1, source_target_pairs={{0,8},{1,3},{2,10},{3,1},{4,12},{5,7},{6,14},{7,5},{8,0},{9,11},{1... | collective-permute-start | bytes 294920 | tf_op jit(solution)/shard_map/ppermute | solution.py:85
  19.7 4.6 %collective-permute-start.7 = (bf16[64,768]{1,0:T(8,128)(2,1)S(1)}, bf16[64,768]{1,0:T(8,128)(2,1)S(1)}, u32[]{:S(2)}, u32[]{:S(2)}) collective-permute-start(bf16[64,768]{1,0:T(8,128)(2,1)S(1)} %get-tuple-element.69), channel_id=1, source_target_pairs={{0,16},{1,5},{2,18},{3,7},{4,20},{5,1},{6,22},{7,3},{8,24},{9,13},... | collective-permute-start | bytes 294920 | tf_op jit(solution)/shard_map/ppermute | solution.py:85
  24.7 1.4 %collective-permute-start.9 = (bf16[64,768]{1,0:T(8,128)(2,1)S(1)}, bf16[64,768]{1,0:T(8,128)(2,1)S(1)}, u32[]{:S(2)}, u32[]{:S(2)}) collective-permute-start(bf16[64,768]{1,0:T(8,128)(2,1)S(1)} %maximum_maximum_fusion), channel_id=1, source_target_pairs={{0,1},{1,0},{2,3},{3,2},{4,5},{5,4},{6,7},{7,6},{8,9},{9,8},{10,11... | collective-permute-start | bytes 294920 | tf_op jit(solution)/shard_map/ppermute | solution.py:67
  26.3 4.5 %collective-permute-start.10 = (f32[8,128]{1,0:T(8,128)S(1)}, f32[8,128]{1,0:T(8,128)S(1)}, u32[]{:S(2)}, u32[]{:S(2)}) collective-permute-start(f32[8,128]{1,0:T(8,128)S(1)} %select_add_fusion), channel_id=1, source_target_pairs={{18,0},{24,1},{6,30},{12,31},{13,8},{25,9},{4,22},{14,23},{16,2},{... | collective-permute-start | bytes 12296 | tf_op jit(solution)/shard_map/ppermute | solution.py:171
  30.9 1.2 %collective-permute-start.11 = (f32[8,128]{1,0:T(8,128)S(1)}, f32[8,128]{1,0:T(8,128)S(1)}, u32[]{:S(2)}, u32[]{:S(2)}) collective-permute-start(f32[8,128]{1,0:T(8,128)S(1)} %fusion.46), channel_id=1, source_target_pairs={{0,1},{1,0},{2,3},{3,2},{4,5},{5,4},{6,7},{7,6},{8,9},{9,8},{10,11... | collective-permute-start | bytes 12296 | tf_op jit(solution)/shard_map/ppermute | solution.py:67

commit v4 on v2

--- a/solution.py
+++ b/solution.py
@@ -111,42 +111,55 @@
     return (rounded((values - center) * scaled).astype(jnp.bfloat16), scaled)
 
 
+def early(side):
+    return [
+        (((v * side + v) * 2 + core), (((v ^ (core + 1)) * side + (v ^ (core + 1))) * 2 + core))
+        for v in range(side)
+        for core in range(2)
+    ]
+
+
 def meetings(side):
+    if side != 4:
+        return None
+    blocks = set(range(side))
     chips = [(row, z) for row in range(side) for z in range(side)]
-    owners = {v: [(r, z, k) for r, z in chips for k in (0, 1) if (r, z)[1 - k] == v] for v in range(side)}
-    wanted = {(r, z): [v for v in range(side) if v not in (r, z)] for r, z in chips}
+    knows = {
+        (row, z, core): {(z, row)[core]} | ({row ^ (core + 1)} if row == z else set())
+        for row, z in chips
+        for core in range(2)
+    }
 
     def hops(p, q):
         return bin(p[0] ^ q[0]).count("1") + abs(p[1] - q[1])
 
-    rounds = []
-    while any(wanted.values()):
-        asks = []
-        for (r, z), left in wanted.items():
-            left.sort(key=lambda v: (v - r - 1) % side if r == z else v)
-            asks += [((r, z), v) for v in left[-2:]]
-
-        def place(ask, taken, limit, seen):
-            for owner in owners[ask[1]]:
-                if owner not in seen and hops(owner, ask[0]) <= limit:
-                    seen.add(owner)
-                    if owner not in taken or place(taken[owner], taken, limit, seen):
-                        taken[owner] = ask
-                        return True
-            return False
-
-        for limit in range(3 * side):
-            taken = {}
-            if all([place(ask, taken, limit, set()) for ask in asks]):
-                break
-        heard, pairs = dict.fromkeys(chips, 0), []
-        for (r, z, k), (chip, v) in taken.items():
-            receiver = (chip[0] * side + chip[1]) * 2 + heard[chip]
-            pairs.append(((r * side + z) * 2 + k, receiver))
-            heard[chip] += 1
-            wanted[chip].remove(v)
-        rounds.append(sorted(pairs))
-    return rounds
+    def search(choices, order, used):
+        if not order:
+            return []
+        for tellers in choices[order[0]]:
+            if not used & set(tellers):
+                found = search(choices, order[1:], used | set(tellers))
+                if found is not None:
+                    return [(order[0], tellers)] + found
+        return None
+
+    for limit in range(1, 3 * side):
+        choices = {}
+        for chip in chips:
+            own = knows[*chip, 0] | knows[*chip, 1]
+            near = [d for d in knows if 0 < hops(d, chip) <= limit]
+            tellers = [(d,) for d in near] + [(d, e) for i, d in enumerate(near) for e in near[i + 1 :]]
+            choices[chip] = [t for t in tellers if own.union(*(knows[d] for d in t)) == blocks]
+        if all(choices.values()):
+            order = sorted(chips, key=lambda chip: len(choices[chip]))
+            found = search(choices, order, set())
+            if found:
+                return [
+                    ((d[0] * side + d[1]) * 2 + d[2], (chip[0] * side + chip[1]) * 2 + core)
+                    for chip, tellers in found
+                    for core, d in enumerate(tellers)
+                ]
+    return None
 
 
 def gram_body(side, view_a, view_b):
@@ -194,8 +207,17 @@
     def images_of(step):
         return lax.dynamic_slice_in_dim(extra, (row ^ step) * pair, pair, 0)
 
+    slots = lax.broadcasted_iota(jnp.int32, (2 * side, 128), 0)
+
+    def in_slot(part, block):
+        return jnp.where((slots & (side - 1)) == block, jnp.where(slots < side, part, 1.0), 0.0)
+
+    plan = meetings(side)
     landed = [payload(images_of(0), gram, part)]
     landed += [across(payload(images_of(step), gram, part), side, step) for step in range(1, side)]
+    told = 0.0
+    if plan:
+        told = lax.ppermute(jnp.where(diagonal, in_slot(part, row), 0.0), BOTH, early(side))
     summed = sum(x.astype(jnp.float32) for x in landed)
     gram = summed[:, lanes : lanes + count] + summed[:, lanes + count : lanes + 2 * count]
     part = summed[:1, lanes + 2 * count :] + summed[count // 2 : count // 2 + 1, lanes + 2 * count :]
@@ -205,10 +227,16 @@
     for_a = jnp.where(is_a, came, sent)
     for_b = jnp.where(is_a, sent, came)
 
-    slots = lax.broadcasted_iota(jnp.int32, (2 * side, 128), 0)
-    known = jnp.where((slots & (side - 1)) == jnp.where(is_a, z, row), jnp.where(slots < side, part, 1.0), 0.0)
-    known = known + sum(lax.ppermute(known, BOTH, pairs) for pairs in meetings(side))
-    known = known + sibling(known, n_col)
+    known = in_slot(part, jnp.where(is_a, z, row)) + told
+    heard = jnp.zeros_like(known)
+    if plan:
+        heard = lax.ppermute(known, BOTH, plan)
+    else:
+        known = jnp.where(is_a, known, 0.0)
+        step = 1
+        while step < side:
+            known = known + lax.ppermute(known, "col", [(c, c ^ (2 * step)) for c in range(n_col)])
+            step *= 2
 
     twice = [jnp.where(is_a, normed, other_normed)] * 2
     all_a = jnp.concatenate(twice, 0)
@@ -225,29 +253,35 @@
     extra_b = images_in(for_b)
     extra_b = jnp.where(is_a, extra_b[:, :half], extra_b[:, half:])
 
-    def gradient(sums, twice, scaled, extra, start, images):
+    def terms(sums, twice):
         halves = sums[:, lanes : lanes + 2 * count]
         term = jnp.dot(halves, twice, preferred_element_type=jnp.float32)
         term = term * (2.0 * off_weight / count)
-        normed_f = twice[:count].astype(jnp.float32)
-        first = jnp.mean(term, 0)
-        second = jnp.mean(term * normed_f, 0)
+        return (term, jnp.mean(term, 0), jnp.mean(term * twice[:count].astype(jnp.float32), 0))
+
+    def gradient(terms, twice, scaled, extra, start, images):
+        term, first, second = terms
         term = lax.dynamic_slice_in_dim(term, start, images, 0)
-        normed_f = lax.dynamic_slice_in_dim(normed_f, start, images, 0)
-        return (scaled * (term - first - normed_f * second + extra.astype(jnp.float32))).astype(
+        normed = lax.dynamic_slice_in_dim(twice, start, images, 0).astype(jnp.float32)
+        return (scaled * (term - first - normed * second + extra.astype(jnp.float32))).astype(
             jnp.bfloat16
         )
-
-    grad_a = gradient(for_a, all_a, scaled_a, extra_a, col * share, share)
-    grad_b = gradient(for_b, all_b, scaled_b, extra_b, row * pair, pair)
 
     def whole(sums):
         sums = sums.astype(jnp.float32)
         return sums[:, lanes : lanes + count] + sums[:, lanes + count : lanes + 2 * count]
 
     everywhere = whole(for_a) * whole(for_b) * (off_weight / (count * count * width * side))
+    everywhere = jnp.pad(jnp.sum(everywhere, 0), (0, 128 - count))
+    terms_a, terms_b = terms(for_a, all_a), terms(for_b, all_b)
+    heard, terms_a, terms_b, everywhere = lax.optimization_barrier(
+        (heard, terms_a, terms_b, everywhere)
+    )
+    known = known + heard
+    known = known + sibling(known, n_col)
+    grad_a = gradient(terms_a, all_a, scaled_a, extra_a, col * share, share)
+    grad_b = gradient(terms_b, all_b, scaled_b, extra_b, row * pair, pair)
     on_diagonal = known[:side] * (1.0 / (width * side)) / known[side:]
-    everywhere = jnp.sum(jnp.pad(everywhere.reshape(side, pair, count).sum(0), ((0, 0), (0, -count % 128))), 0)
     loss = jnp.sum(everywhere + jnp.sum(on_diagonal, 0))
     return (loss, grad_a, grad_b)
 

time: 35.9 us -> 34.9 us (0.972)
  the two profiles are of different devices: /device:TPU:9 before, /device:TPU:0 now
where the time goes in v4:
time: 34.9 us; the launch traced here: 34.7 us
  waiting for transfers between devices  15.7 us (45%)
  starting transfers between devices  13.5 us (39%)
  other arithmetic  3.67 us (11%)
  between operations  1.01 us (3%)
  matrix products  0.67 us (2%)
    ppermute x3, waiting for transfers between devices, flip(): return lax.ppermute(value, BOTH, pairs)  6.05 us
    ppermute x3, starting transfers between devices, flip(): return lax.ppermute(value, BOTH, pairs)  5.39 us
    ppermute x3, starting transfers between devices, across(): return lax.ppermute(value, BOTH, pairs)  3.61 us
    ppermute x1, waiting for transfers between devices, gram_body(): heard = lax.ppermute(known, BOTH, plan)  3.13 us
    ppermute x5, waiting for transfers between devices, sibling(): return lax.ppermute(value, 'col', [(c, c ^ 1) for c in range(n_col)])  2.39 us
    ppermute x3, waiting for transfers between devices, across(): return lax.ppermute(value, BOTH, pairs)  2.11 us
    ppermute x1, waiting for transfers between devices, gram_body(): lax.ppermute(jnp.where(diagonal, in_slot(part, row), 0.0), BOTH, early(si...  2.04 us
    ppermute x1, starting transfers between devices, gram_body(): heard = lax.ppermute(known, BOTH, plan)  1.91 us
  transfers between devices with their start and end apart: 13, of which 9 were waited for; matrix products, arithmetic and copies ran while one was open for 8% of the time, Pallas kernels for 0%

profile of v4, /device:TPU:0, one launch (start us, length us, event | category | flops | bytes accessed | tf_op | source)
XLA Modules:
  0.0 34.7 jit_solution(10553481079619399082)
XLA Ops:
  0.6 0.5 %collective-permute-start = (bf16[8,2048]{1,0:T(8,128)(2,1)}, bf16[8,2048]{1,0:T(8,128)(2,1)S(1)}, u32[]{:S(2)}, u32[]{:S(2)}) collective-permute-start(bf16[8,2048]{1,0:T(8,128)(2,1)} %param.2), channel_id=1, source_target_pairs={{0,1},{1,0},{2,3},{3,2},{4,5},{5,4},{6,7},{7,6},{8,9},{9,8},{10,11... | collective-permute-start | bytes 98312 | tf_op jit(solution)/shard_map/ppermute | solution.py:67
  1.3 0.9 %collective-permute-done = bf16[8,2048]{1,0:T(8,128)(2,1)S(1)} collective-permute-done((bf16[8,2048]{1,0:T(8,128)(2,1)}, bf16[8,2048]{1,0:T(8,128)(2,1)S(1)}, u32[]{:S(2)}, u32[]{:S(2)}) %collective-permute-start) | collective-permute-done | bytes 32800 | tf_op jit(solution)/shard_map/ppermute | solution.py:67
  2.2 0.3 %collective-permute-done.1 = bf16[16,1024]{1,0:T(8,128)(2,1)S(1)} collective-permute-done((bf16[16,1024]{1,0:T(8,128)(2,1)}, bf16[16,1024]{1,0:T(8,128)(2,1)S(1)}, u32[]{:S(2)}, u32[]{:S(2)}) %collective-permute-start.1) | collective-permute-done | bytes 32800 | tf_op jit(solution)/shard_map/ppermute | solution.py:67
  2.6 2.8 %collective-permute-start.4 = (bf16[16,2048]{1,0:T(8,128)(2,1)S(1)}, bf16[16,2048]{1,0:T(8,128)(2,1)S(1)}, u32[]{:S(2)}, u32[]{:S(2)}) collective-permute-start(bf16[16,2048]{1,0:T(8,128)(2,1)S(1)} %maximum_select_fusion), channel_id=1, source_target_pairs={{0,2},{1,9},{2,0},{3,11},{4,6},{5,13},{6,4},{7,15},{8,10},{9,1},{1... | collective-permute-start | bytes 196616 | tf_op jit(solution)/shard_map/ppermute | solution.py:76
  5.4 2.6 %collective-permute-start.3 = (bf16[16,2048]{1,0:T(8,128)(2,1)S(1)}, bf16[16,2048]{1,0:T(8,128)(2,1)S(1)}, u32[]{:S(2)}, u32[]{:S(2)}) collective-permute-start(bf16[16,2048]{1,0:T(8,128)(2,1)S(1)} %maximum_select_fusion), channel_id=1, source_target_pairs={{0,4},{1,17},{2,6},{3,19},{4,0},{5,21},{6,2},{7,23},{8,12},{9,25},... | collective-permute-start | bytes 196616 | tf_op jit(solution)/shard_map/ppermute | solution.py:76
  8.0 3.3 %collective-permute-done.3 = bf16[16,2048]{1,0:T(8,128)(2,1)S(1)} collective-permute-done((bf16[16,2048]{1,0:T(8,128)(2,1)S(1)}, bf16[16,2048]{1,0:T(8,128)(2,1)S(1)}, u32[]{:S(2)}, u32[]{:S(2)}) %collective-permute-start.3) | collective-permute-done | bytes 65568 | tf_op jit(solution)/shard_map/ppermute | solution.py:76
  11.3 2.8 %collective-permute-done.2 = bf16[16,2048]{1,0:T(8,128)(2,1)S(1)} collective-permute-done((bf16[16,2048]{1,0:T(8,128)(2,1)S(1)}, bf16[16,2048]{1,0:T(8,128)(2,1)S(1)}, u32[]{:S(2)}, u32[]{:S(2)}) %collective-permute-start.2) | collective-permute-done | bytes 65568 | tf_op jit(solution)/shard_map/ppermute | solution.py:76
  14.2 0.1 fusion.7
  14.4 0.2 fusion.42
  14.6 1.1 %collective-permute-done.5 = bf16[64,2048]{1,0:T(8,128)(2,1)S(1)} collective-permute-done((bf16[64,2048]{1,0:T(8,128)(2,1)S(1)}, bf16[64,2048]{1,0:T(8,128)(2,1)S(1)}, u32[]{:S(2)}, u32[]{:S(2)}) %collective-permute-start.5) | collective-permute-done | bytes 262176 | tf_op jit(solution)/shard_map/ppermute | solution.py:67
  15.8 0.1 fusion.4
  15.9 0.1 broadcast_select_fusion
  16.1 0.1 convert_reduce_fusion
  16.3 0.1 fusion.12
  16.5 0.1 fusion.17
  16.6 2.5 %collective-permute-start.8 = (bf16[64,768]{1,0:T(8,128)(2,1)S(1)}, bf16[64,768]{1,0:T(8,128)(2,1)S(1)}, u32[]{:S(2)}, u32[]{:S(2)}) collective-permute-start(bf16[64,768]{1,0:T(8,128)(2,1)S(1)} %fusion.17), channel_id=1, source_target_pairs={{0,24},{1,7},{2,26},{3,5},{4,28},{5,3},{6,30},{7,1},{8,16},{9,15},... | collective-permute-start | bytes 294920 | tf_op jit(solution)/shard_map/ppermute | solution.py:85
  19.2 0.6 %collective-permute-start.6 = (bf16[64,768]{1,0:T(8,128)(2,1)S(1)}, bf16[64,768]{1,0:T(8,128)(2,1)S(1)}, u32[]{:S(2)}, u32[]{:S(2)}) collective-permute-start(bf16[64,768]{1,0:T(8,128)(2,1)S(1)} %get-tuple-element.71), channel_id=1, source_target_pairs={{0,8},{1,3},{2,10},{3,1},{4,12},{5,7},{6,14},{7,5},{8,0},{9,11},{1... | collective-permute-start | bytes 294920 | tf_op jit(solution)/shard_map/ppermute | solution.py:85
  19.8 0.5 %collective-permute-start.7 = (bf16[64,768]{1,0:T(8,128)(2,1)S(1)}, bf16[64,768]{1,0:T(8,128)(2,1)S(1)}, u32[]{:S(2)}, u32[]{:S(2)}) collective-permute-start(bf16[64,768]{1,0:T(8,128)(2,1)S(1)} %get-tuple-element.72), channel_id=1, source_target_pairs={{0,16},{1,5},{2,18},{3,7},{4,20},{5,1},{6,22},{7,3},{8,24},{9,13},... | collective-permute-start | bytes 294920 | tf_op jit(solution)/shard_map/ppermute | solution.py:85
  20.3 1.9 %collective-permute-start.9 = (f32[8,128]{1,0:T(8,128)S(1)}, f32[8,128]{1,0:T(8,128)S(1)}, u32[]{:S(2)}, u32[]{:S(2)}) collective-permute-start(f32[8,128]{1,0:T(8,128)S(1)} %select_select_fusion), channel_id=1, source_target_pairs={{0,10},{1,21},{10,0},{11,31},{20,30},{21,1},{30,20},{31,11}} | collective-permute-start | bytes 12296 | tf_op jit(solution)/shard_map/ppermute | solution.py:220
  22.3 1.6 %collective-permute-done.6 = bf16[64,768]{1,0:T(8,128)(2,1)S(1)} collective-permute-done((bf16[64,768]{1,0:T(8,128)(2,1)S(1)}, bf16[64,768]{1,0:T(8,128)(2,1)S(1)}, u32[]{:S(2)}, u32[]{:S(2)}) %collective-permute-start.6) | collective-permute-done | bytes 98336 | tf_op jit(solution)/shard_map/ppermute | solution.py:85
  23.8 0.5 %collective-permute-done.7 = bf16[64,768]{1,0:T(8,128)(2,1)S(1)} collective-permute-done((bf16[64,768]{1,0:T(8,128)(2,1)S(1)}, bf16[64,768]{1,0:T(8,128)(2,1)S(1)}, u32[]{:S(2)}, u32[]{:S(2)}) %collective-permute-start.7) | collective-permute-done | bytes 98336 | tf_op jit(solution)/shard_map/ppermute | solution.py:85
  24.4 0.1 convert_add_fusion
  24.7 2.0 %collective-permute-done.9 = f32[8,128]{1,0:T(8,128)S(1)} collective-permute-done((f32[8,128]{1,0:T(8,128)S(1)}, f32[8,128]{1,0:T(8,128)S(1)}, u32[]{:S(2)}, u32[]{:S(2)}) %collective-permute-start.9) | collective-permute-done | bytes 4128 | tf_op jit(solution)/shard_map/ppermute | solution.py:220
  26.8 1.9 %collective-permute-start.10 = (f32[8,128]{1,0:T(8,128)S(1)}, f32[8,128]{1,0:T(8,128)S(1)}, u32[]{:S(2)}, u32[]{:S(2)}) collective-permute-start(f32[8,128]{1,0:T(8,128)S(1)} %select_add_fusion), channel_id=1, source_target_pairs={{1,8},{11,9},{5,22},{15,23},{4,14},{7,15},{0,16},{20,17},{2,6},{12... | collective-permute-start | bytes 12296 | tf_op jit(solution)/shard_map/ppermute | solution.py:233
  28.7 0.1 fusion.38
  28.9 0.2 multiply_reduce_fusion.1
  29.1 0.3 multiply_reduce_fusion
  29.4 0.1 fusion.26
  29.5 3.1 %collective-permute-done.10 = f32[8,128]{1,0:T(8,128)S(1)} collective-permute-done((f32[8,128]{1,0:T(8,128)S(1)}, f32[8,128]{1,0:T(8,128)S(1)}, u32[]{:S(2)}, u32[]{:S(2)}) %collective-permute-start.10) | collective-permute-done | bytes 4128 | tf_op jit(solution)/shard_map/ppermute | solution.py:233
  32.7 0.7 %multiply_convert_fusion.1 = bf16[8,2048]{1,0:T(8,128)(2,1)} fusion(f32[64,2048]{1,0:T(8,128)S(1)} %get-tuple-element.19, s32[]{:T(128)S(6)} %select_n.212, s32[]{:T(128)S(6)} %select_n.213, bf16[64,2048]{1,0:T(8,128)(2,1)S(1)} %get-tuple-element.35, bf16[16,2048]{1,0:T(8,128)(2,1)S(1)} %pad_maximum_fusion.15, f32[2048]{0:T(1024)S(1)} %broadcast_multiply_fusion, ...), kind=kLoop, calls=%fused_computation.56 | loop fusion | flops 196608 | bytes 450569 | tf_op jit(solution)/shard_map/convert_element_type | solution.py:266
  33.4 0.7 %multiply_convert_fusion = bf16[16,1024]{1,0:T(8,128)(2,1)} fusion(f32[64,1024]{1,0:T(8,128)S(1)} %get-tuple-element.22, s32[]{:T(128)S(6)} %select_n.191, s32[]{:T(128)S(6)} %select_n.218, bf16[64,1024]{1,0:T(8,128)(2,1)S(1)} %slice_select_fusion, bf16[16,512]{1,0:T(8,128)(2,1)S(1)} %get-tuple-element.64, bf16[16,512]{1,0:T(8,128)(2,1)S(1)} %get-tuple-element.65, ...), kind=kLoop, calls=%fused_computation.55 | loop fusion | flops 327680 | bytes 307209 | tf_op jit(solution)/shard_map/convert_element_type | solution.py:266
  34.1 0.6 %add_reduce_fusion = f32[]{:T(128)} fusion(f32[128]{0:T(128)S(1)} %pad.4, f32[128]{0:T(128)S(1)} %fusion.29), kind=kLoop, calls=%fused_computation.113 | loop fusion | flops 255 | bytes 1028 | tf_op jit(solution)/shard_map/reduce_sum | solution.py:285
  (52 shorter events, 1.1 us)
Async XLA Ops:
  0.6 1.6 %collective-permute-start = (bf16[8,2048]{1,0:T(8,128)(2,1)}, bf16[8,2048]{1,0:T(8,128)(2,1)S(1)}, u32[]{:S(2)}, u32[]{:S(2)}) collective-permute-start(bf16[8,2048]{1,0:T(8,128)(2,1)} %param.2), channel_id=1, source_target_pairs={{0,1},{1,0},{2,3},{3,2},{4,5},{5,4},{6,7},{7,6},{8,9},{9,8},{10,11... | collective-permute-start | bytes 98312 | tf_op jit(solution)/shard_map/ppermute | solution.py:67
  1.1 1.4 %collective-permute-start.1 = (bf16[16,1024]{1,0:T(8,128)(2,1)}, bf16[16,1024]{1,0:T(8,128)(2,1)S(1)}, u32[]{:S(2)}, u32[]{:S(2)}) collective-permute-start(bf16[16,1024]{1,0:T(8,128)(2,1)} %param.3), channel_id=1, source_target_pairs={{0,1},{1,0},{2,3},{3,2},{4,5},{5,4},{6,7},{7,6},{8,9},{9,8},{10,11... | collective-permute-start | bytes 98312 | tf_op jit(solution)/shard_map/ppermute | solution.py:67
  1.2 1.3 %copy-start.1 = (bf16[16,1024]{1,0:T(8,128)(2,1)S(1)}, bf16[16,1024]{1,0:T(8,128)(2,1)}, u32[]{:S(2)}) copy-start(bf16[16,1024]{1,0:T(8,128)(2,1)} %param.3) | copy-start | bytes 98308
  1.3 1.3 %copy-start = (bf16[8,2048]{1,0:T(8,128)(2,1)S(1)}, bf16[8,2048]{1,0:T(8,128)(2,1)}, u32[]{:S(2)}) copy-start(bf16[8,2048]{1,0:T(8,128)(2,1)} %param.2) | copy-start | bytes 98308
  2.6 5.4 %collective-permute-start.4 = (bf16[16,2048]{1,0:T(8,128)(2,1)S(1)}, bf16[16,2048]{1,0:T(8,128)(2,1)S(1)}, u32[]{:S(2)}, u32[]{:S(2)}) collective-permute-start(bf16[16,2048]{1,0:T(8,128)(2,1)S(1)} %maximum_select_fusion), channel_id=1, source_target_pairs={{0,2},{1,9},{2,0},{3,11},{4,6},{5,13},{6,4},{7,15},{8,10},{9,1},{1... | collective-permute-start | bytes 196616 | tf_op jit(solution)/shard_map/ppermute | solution.py:76
  5.4 5.9 %collective-permute-start.3 = (bf16[16,2048]{1,0:T(8,128)(2,1)S(1)}, bf16[16,2048]{1,0:T(8,128)(2,1)S(1)}, u32[]{:S(2)}, u32[]{:S(2)}) collective-permute-start(bf16[16,2048]{1,0:T(8,128)(2,1)S(1)} %maximum_select_fusion), channel_id=1, source_target_pairs={{0,4},{1,17},{2,6},{3,19},{4,0},{5,21},{6,2},{7,23},{8,12},{9,25},... | collective-permute-start | bytes 196616 | tf_op jit(solution)/shard_map/ppermute | solution.py:76
  8.0 6.1 %collective-permute-start.2 = (bf16[16,2048]{1,0:T(8,128)(2,1)S(1)}, bf16[16,2048]{1,0:T(8,128)(2,1)S(1)}, u32[]{:S(2)}, u32[]{:S(2)}) collective-permute-start(bf16[16,2048]{1,0:T(8,128)(2,1)S(1)} %maximum_select_fusion), channel_id=1, source_target_pairs={{0,6},{1,25},{2,4},{3,27},{4,2},{5,29},{6,0},{7,31},{8,14},{9,17},... | collective-permute-start | bytes 196616 | tf_op jit(solution)/shard_map/ppermute | solution.py:76
  14.2 1.6 %collective-permute-start.5 = (bf16[64,2048]{1,0:T(8,128)(2,1)S(1)}, bf16[64,2048]{1,0:T(8,128)(2,1)S(1)}, u32[]{:S(2)}, u32[]{:S(2)}) collective-permute-start(bf16[64,2048]{1,0:T(8,128)(2,1)S(1)} %get-tuple-element.38), channel_id=1, source_target_pairs={{0,1},{1,0},{2,3},{3,2},{4,5},{5,4},{6,7},{7,6},{8,9},{9,8},{10,11... | collective-permute-start | bytes 786440 | tf_op jit(solution)/shard_map/ppermute | solution.py:67
  16.6 5.7 %collective-permute-start.8 = (bf16[64,768]{1,0:T(8,128)(2,1)S(1)}, bf16[64,768]{1,0:T(8,128)(2,1)S(1)}, u32[]{:S(2)}, u32[]{:S(2)}) collective-permute-start(bf16[64,768]{1,0:T(8,128)(2,1)S(1)} %fusion.17), channel_id=1, source_target_pairs={{0,24},{1,7},{2,26},{3,5},{4,28},{5,3},{6,30},{7,1},{8,16},{9,15},... | collective-permute-start | bytes 294920 | tf_op jit(solution)/shard_map/ppermute | solution.py:85
  19.2 4.7 %collective-permute-start.6 = (bf16[64,768]{1,0:T(8,128)(2,1)S(1)}, bf16[64,768]{1,0:T(8,128)(2,1)S(1)}, u32[]{:S(2)}, u32[]{:S(2)}) collective-permute-start(bf16[64,768]{1,0:T(8,128)(2,1)S(1)} %get-tuple-element.71), channel_id=1, source_target_pairs={{0,8},{1,3},{2,10},{3,1},{4,12},{5,7},{6,14},{7,5},{8,0},{9,11},{1... | collective-permute-start | bytes 294920 | tf_op jit(solution)/shard_map/ppermute | solution.py:85
  19.8 4.6 %collective-permute-start.7 = (bf16[64,768]{1,0:T(8,128)(2,1)S(1)}, bf16[64,768]{1,0:T(8,128)(2,1)S(1)}, u32[]{:S(2)}, u32[]{:S(2)}) collective-permute-start(bf16[64,768]{1,0:T(8,128)(2,1)S(1)} %get-tuple-element.72), channel_id=1, source_target_pairs={{0,16},{1,5},{2,18},{3,7},{4,20},{5,1},{6,22},{7,3},{8,24},{9,13},... | collective-permute-start | bytes 294920 | tf_op jit(solution)/shard_map/ppermute | solution.py:85
  20.3 6.4 %collective-permute-start.9 = (f32[8,128]{1,0:T(8,128)S(1)}, f32[8,128]{1,0:T(8,128)S(1)}, u32[]{:S(2)}, u32[]{:S(2)}) collective-permute-start(f32[8,128]{1,0:T(8,128)S(1)} %select_select_fusion), channel_id=1, source_target_pairs={{0,10},{1,21},{10,0},{11,31},{20,30},{21,1},{30,20},{31,11}} | collective-permute-start | bytes 12296 | tf_op jit(solution)/shard_map/ppermute | solution.py:220
  24.7 4.1 %collective-permute-start.11 = (bf16[64,640]{1,0:T(8,128)(2,1)S(1)}, bf16[64,640]{1,0:T(8,128)(2,1)S(1)}, u32[]{:S(2)}, u32[]{:S(2)}) collective-permute-start(bf16[64,640]{1,0:T(8,128)(2,1)S(1)} %pad_maximum_fusion.14), channel_id=1, source_target_pairs={{0,1},{1,0},{2,3},{3,2},{4,5},{5,4},{6,7},{7,6},{8,9},{9,8},{10,11... | collective-permute-start | bytes 245768 | tf_op jit(solution)/shard_map/ppermute | solution.py:67
  26.8 5.8 %collective-permute-start.10 = (f32[8,128]{1,0:T(8,128)S(1)}, f32[8,128]{1,0:T(8,128)S(1)}, u32[]{:S(2)}, u32[]{:S(2)}) collective-permute-start(f32[8,128]{1,0:T(8,128)S(1)} %select_add_fusion), channel_id=1, source_target_pairs={{1,8},{11,9},{5,22},{15,23},{4,14},{7,15},{0,16},{20,17},{2,6},{12... | collective-permute-start | bytes 12296 | tf_op jit(solution)/shard_map/ppermute | solution.py:233
  32.7 1.4 %collective-permute-start.12 = (f32[8,128]{1,0:T(8,128)S(1)}, f32[8,128]{1,0:T(8,128)S(1)}, u32[]{:S(2)}, u32[]{:S(2)}) collective-permute-start(f32[8,128]{1,0:T(8,128)S(1)} %fusion.45), channel_id=1, source_target_pairs={{0,1},{1,0},{2,3},{3,2},{4,5},{5,4},{6,7},{7,6},{8,9},{9,8},{10,11... | collective-permute-start | bytes 12296 | tf_op jit(solution)/shard_map/ppermute | solution.py:67

commit v5 on v4

--- a/solution.py
+++ b/solution.py
@@ -112,11 +112,7 @@
 
 
 def early(side):
-    return [
-        (((v * side + v) * 2 + core), (((v ^ (core + 1)) * side + (v ^ (core + 1))) * 2 + core))
-        for v in range(side)
-        for core in range(2)
-    ]
+    return [((v * side + v) * 2, ((v ^ 1) * side + (v ^ 1)) * 2) for v in range(side)]
 
 
 def meetings(side):
@@ -125,7 +121,7 @@
     blocks = set(range(side))
     chips = [(row, z) for row in range(side) for z in range(side)]
     knows = {
-        (row, z, core): {(z, row)[core]} | ({row ^ (core + 1)} if row == z else set())
+        (row, z, core): {(z, row)[core]} | ({row ^ 1} if row == z and core == 0 else set())
         for row, z in chips
         for core in range(2)
     }

time: 34.9 us -> 33.6 us (0.963)
  starting transfers between devices: 13.5 us -> 11.6 us
  waiting for transfers between devices: 15.7 us -> 16.3 us
    ppermute x1, starting transfers between devices: 1.91 us -> 0.01 us  [gram_body(): heard = lax.ppermute(known, BOTH, plan)]
    ppermute x1, waiting for transfers between devices: 3.13 us -> 3.73 us  [gram_body(): heard = lax.ppermute(known, BOTH, plan)]
  transfers between devices with their start and end apart: 13 -> 13, of which waited for: 9 -> 9; matrix products, arithmetic and copies ran while one was open for 8% -> 9% of each run, Pallas kernels for 0% -> 0%
where the time goes in v5:
time: 33.6 us; the launch traced here: 33.4 us
  waiting for transfers between devices  16.3 us (49%)
  starting transfers between devices  11.6 us (35%)
  other arithmetic  3.67 us (11%)
  between operations  1.01 us (3%)
  matrix products  0.67 us (2%)
    ppermute x3, waiting for transfers between devices, flip(): return lax.ppermute(value, BOTH, pairs)  6.05 us
    ppermute x3, starting transfers between devices, flip(): return lax.ppermute(value, BOTH, pairs)  5.39 us
    ppermute x1, waiting for transfers between devices, gram_body(): heard = lax.ppermute(known, BOTH, plan)  3.73 us
    ppermute x3, starting transfers between devices, across(): return lax.ppermute(value, BOTH, pairs)  3.61 us
    ppermute x5, waiting for transfers between devices, sibling(): return lax.ppermute(value, 'col', [(c, c ^ 1) for c in range(n_col)])  2.39 us
    ppermute x3, waiting for transfers between devices, across(): return lax.ppermute(value, BOTH, pairs)  2.11 us
    ppermute x1, waiting for transfers between devices, gram_body(): lax.ppermute(jnp.where(diagonal, in_slot(part, row), 0.0), BOTH, early(si...  2.04 us
    ppermute x1, starting transfers between devices, gram_body(): lax.ppermute(jnp.where(diagonal, in_slot(part, row), 0.0), BOTH, early(si...  1.91 us
  transfers between devices with their start and end apart: 13, of which 9 were waited for; matrix products, arithmetic and copies ran while one was open for 9% of the time, Pallas kernels for 0%

profile of v5, /device:TPU:0, one launch (start us, length us, event | category | flops | bytes accessed | tf_op | source)
XLA Modules:
  0.0 33.4 jit_solution(1999139623781253122)
XLA Ops:
  0.6 0.5 %collective-permute-start = (bf16[8,2048]{1,0:T(8,128)(2,1)}, bf16[8,2048]{1,0:T(8,128)(2,1)S(1)}, u32[]{:S(2)}, u32[]{:S(2)}) collective-permute-start(bf16[8,2048]{1,0:T(8,128)(2,1)} %param.2), channel_id=1, source_target_pairs={{0,1},{1,0},{2,3},{3,2},{4,5},{5,4},{6,7},{7,6},{8,9},{9,8},{10,11... | collective-permute-start | bytes 98312 | tf_op jit(solution)/shard_map/ppermute | solution.py:67
  1.3 0.9 %collective-permute-done = bf16[8,2048]{1,0:T(8,128)(2,1)S(1)} collective-permute-done((bf16[8,2048]{1,0:T(8,128)(2,1)}, bf16[8,2048]{1,0:T(8,128)(2,1)S(1)}, u32[]{:S(2)}, u32[]{:S(2)}) %collective-permute-start) | collective-permute-done | bytes 32800 | tf_op jit(solution)/shard_map/ppermute | solution.py:67
  2.2 0.3 %collective-permute-done.1 = bf16[16,1024]{1,0:T(8,128)(2,1)S(1)} collective-permute-done((bf16[16,1024]{1,0:T(8,128)(2,1)}, bf16[16,1024]{1,0:T(8,128)(2,1)S(1)}, u32[]{:S(2)}, u32[]{:S(2)}) %collective-permute-start.1) | collective-permute-done | bytes 32800 | tf_op jit(solution)/shard_map/ppermute | solution.py:67
  2.6 2.8 %collective-permute-start.4 = (bf16[16,2048]{1,0:T(8,128)(2,1)S(1)}, bf16[16,2048]{1,0:T(8,128)(2,1)S(1)}, u32[]{:S(2)}, u32[]{:S(2)}) collective-permute-start(bf16[16,2048]{1,0:T(8,128)(2,1)S(1)} %maximum_select_fusion), channel_id=1, source_target_pairs={{0,2},{1,9},{2,0},{3,11},{4,6},{5,13},{6,4},{7,15},{8,10},{9,1},{1... | collective-permute-start | bytes 196616 | tf_op jit(solution)/shard_map/ppermute | solution.py:76
  5.4 2.6 %collective-permute-start.3 = (bf16[16,2048]{1,0:T(8,128)(2,1)S(1)}, bf16[16,2048]{1,0:T(8,128)(2,1)S(1)}, u32[]{:S(2)}, u32[]{:S(2)}) collective-permute-start(bf16[16,2048]{1,0:T(8,128)(2,1)S(1)} %maximum_select_fusion), channel_id=1, source_target_pairs={{0,4},{1,17},{2,6},{3,19},{4,0},{5,21},{6,2},{7,23},{8,12},{9,25},... | collective-permute-start | bytes 196616 | tf_op jit(solution)/shard_map/ppermute | solution.py:76
  8.0 3.3 %collective-permute-done.3 = bf16[16,2048]{1,0:T(8,128)(2,1)S(1)} collective-permute-done((bf16[16,2048]{1,0:T(8,128)(2,1)S(1)}, bf16[16,2048]{1,0:T(8,128)(2,1)S(1)}, u32[]{:S(2)}, u32[]{:S(2)}) %collective-permute-start.3) | collective-permute-done | bytes 65568 | tf_op jit(solution)/shard_map/ppermute | solution.py:76
  11.3 2.8 %collective-permute-done.2 = bf16[16,2048]{1,0:T(8,128)(2,1)S(1)} collective-permute-done((bf16[16,2048]{1,0:T(8,128)(2,1)S(1)}, bf16[16,2048]{1,0:T(8,128)(2,1)S(1)}, u32[]{:S(2)}, u32[]{:S(2)}) %collective-permute-start.2) | collective-permute-done | bytes 65568 | tf_op jit(solution)/shard_map/ppermute | solution.py:76
  14.2 0.1 fusion.7
  14.4 0.2 fusion.42
  14.6 1.1 %collective-permute-done.5 = bf16[64,2048]{1,0:T(8,128)(2,1)S(1)} collective-permute-done((bf16[64,2048]{1,0:T(8,128)(2,1)S(1)}, bf16[64,2048]{1,0:T(8,128)(2,1)S(1)}, u32[]{:S(2)}, u32[]{:S(2)}) %collective-permute-start.5) | collective-permute-done | bytes 262176 | tf_op jit(solution)/shard_map/ppermute | solution.py:67
  15.8 0.1 fusion.4
  15.9 0.1 broadcast_select_fusion
  16.1 0.1 convert_reduce_fusion
  16.3 0.1 fusion.12
  16.5 0.1 fusion.17
  16.6 2.5 %collective-permute-start.8 = (bf16[64,768]{1,0:T(8,128)(2,1)S(1)}, bf16[64,768]{1,0:T(8,128)(2,1)S(1)}, u32[]{:S(2)}, u32[]{:S(2)}) collective-permute-start(bf16[64,768]{1,0:T(8,128)(2,1)S(1)} %fusion.17), channel_id=1, source_target_pairs={{0,24},{1,7},{2,26},{3,5},{4,28},{5,3},{6,30},{7,1},{8,16},{9,15},... | collective-permute-start | bytes 294920 | tf_op jit(solution)/shard_map/ppermute | solution.py:85
  19.1 0.1 fusion.15
  19.2 0.6 %collective-permute-start.6 = (bf16[64,768]{1,0:T(8,128)(2,1)S(1)}, bf16[64,768]{1,0:T(8,128)(2,1)S(1)}, u32[]{:S(2)}, u32[]{:S(2)}) collective-permute-start(bf16[64,768]{1,0:T(8,128)(2,1)S(1)} %get-tuple-element.71), channel_id=1, source_target_pairs={{0,8},{1,3},{2,10},{3,1},{4,12},{5,7},{6,14},{7,5},{8,0},{9,11},{1... | collective-permute-start | bytes 294920 | tf_op jit(solution)/shard_map/ppermute | solution.py:85
  19.8 0.5 %collective-permute-start.7 = (bf16[64,768]{1,0:T(8,128)(2,1)S(1)}, bf16[64,768]{1,0:T(8,128)(2,1)S(1)}, u32[]{:S(2)}, u32[]{:S(2)}) collective-permute-start(bf16[64,768]{1,0:T(8,128)(2,1)S(1)} %get-tuple-element.72), channel_id=1, source_target_pairs={{0,16},{1,5},{2,18},{3,7},{4,20},{5,1},{6,22},{7,3},{8,24},{9,13},... | collective-permute-start | bytes 294920 | tf_op jit(solution)/shard_map/ppermute | solution.py:85
  20.3 1.9 %collective-permute-start.9 = (f32[8,128]{1,0:T(8,128)S(1)}, f32[8,128]{1,0:T(8,128)S(1)}, u32[]{:S(2)}, u32[]{:S(2)}) collective-permute-start(f32[8,128]{1,0:T(8,128)S(1)} %select_select_fusion), channel_id=1, source_target_pairs={{0,10},{10,0},{20,30},{30,20}} | collective-permute-start | bytes 12296 | tf_op jit(solution)/shard_map/ppermute | solution.py:216
  22.3 1.6 %collective-permute-done.6 = bf16[64,768]{1,0:T(8,128)(2,1)S(1)} collective-permute-done((bf16[64,768]{1,0:T(8,128)(2,1)S(1)}, bf16[64,768]{1,0:T(8,128)(2,1)S(1)}, u32[]{:S(2)}, u32[]{:S(2)}) %collective-permute-start.6) | collective-permute-done | bytes 98336 | tf_op jit(solution)/shard_map/ppermute | solution.py:85
  23.8 0.5 %collective-permute-done.7 = bf16[64,768]{1,0:T(8,128)(2,1)S(1)} collective-permute-done((bf16[64,768]{1,0:T(8,128)(2,1)S(1)}, bf16[64,768]{1,0:T(8,128)(2,1)S(1)}, u32[]{:S(2)}, u32[]{:S(2)}) %collective-permute-start.7) | collective-permute-done | bytes 98336 | tf_op jit(solution)/shard_map/ppermute | solution.py:85
  24.4 0.1 convert_add_fusion
  24.7 2.0 %collective-permute-done.9 = f32[8,128]{1,0:T(8,128)S(1)} collective-permute-done((f32[8,128]{1,0:T(8,128)S(1)}, f32[8,128]{1,0:T(8,128)S(1)}, u32[]{:S(2)}, u32[]{:S(2)}) %collective-permute-start.9) | collective-permute-done | bytes 4128 | tf_op jit(solution)/shard_map/ppermute | solution.py:216
  26.8 0.1 fusion.38
  26.9 0.2 multiply_reduce_fusion.1
  27.2 0.3 multiply_reduce_fusion
  27.5 0.1 fusion.26
  27.6 3.7 %collective-permute-done.10 = f32[8,128]{1,0:T(8,128)S(1)} collective-permute-done((f32[8,128]{1,0:T(8,128)S(1)}, f32[8,128]{1,0:T(8,128)S(1)}, u32[]{:S(2)}, u32[]{:S(2)}) %collective-permute-start.10) | collective-permute-done | bytes 4128 | tf_op jit(solution)/shard_map/ppermute | solution.py:229
  31.4 0.7 %multiply_convert_fusion.1 = bf16[8,2048]{1,0:T(8,128)(2,1)} fusion(f32[64,2048]{1,0:T(8,128)S(1)} %get-tuple-element.19, s32[]{:T(128)S(6)} %select_n.212, s32[]{:T(128)S(6)} %select_n.213, bf16[64,2048]{1,0:T(8,128)(2,1)S(1)} %get-tuple-element.35, bf16[16,2048]{1,0:T(8,128)(2,1)S(1)} %pad_maximum_fusion.15, f32[2048]{0:T(1024)S(1)} %broadcast_multiply_fusion, ...), kind=kLoop, calls=%fused_computation.56 | loop fusion | flops 196608 | bytes 450569 | tf_op jit(solution)/shard_map/convert_element_type | solution.py:262
  32.1 0.7 %multiply_convert_fusion = bf16[16,1024]{1,0:T(8,128)(2,1)} fusion(f32[64,1024]{1,0:T(8,128)S(1)} %get-tuple-element.22, s32[]{:T(128)S(6)} %select_n.191, s32[]{:T(128)S(6)} %select_n.218, bf16[64,1024]{1,0:T(8,128)(2,1)S(1)} %slice_select_fusion, bf16[16,512]{1,0:T(8,128)(2,1)S(1)} %get-tuple-element.64, bf16[16,512]{1,0:T(8,128)(2,1)S(1)} %get-tuple-element.65, ...), kind=kLoop, calls=%fused_computation.55 | loop fusion | flops 327680 | bytes 307209 | tf_op jit(solution)/shard_map/convert_element_type | solution.py:262
  32.8 0.6 %add_reduce_fusion = f32[]{:T(128)} fusion(f32[128]{0:T(128)S(1)} %pad.4, f32[128]{0:T(128)S(1)} %fusion.29), kind=kLoop, calls=%fused_computation.113 | loop fusion | flops 255 | bytes 1028 | tf_op jit(solution)/shard_map/reduce_sum | solution.py:281
  (52 shorter events, 1.1 us)
Async XLA Ops:
  0.6 1.6 %collective-permute-start = (bf16[8,2048]{1,0:T(8,128)(2,1)}, bf16[8,2048]{1,0:T(8,128)(2,1)S(1)}, u32[]{:S(2)}, u32[]{:S(2)}) collective-permute-start(bf16[8,2048]{1,0:T(8,128)(2,1)} %param.2), channel_id=1, source_target_pairs={{0,1},{1,0},{2,3},{3,2},{4,5},{5,4},{6,7},{7,6},{8,9},{9,8},{10,11... | collective-permute-start | bytes 98312 | tf_op jit(solution)/shard_map/ppermute | solution.py:67
  1.1 1.4 %collective-permute-start.1 = (bf16[16,1024]{1,0:T(8,128)(2,1)}, bf16[16,1024]{1,0:T(8,128)(2,1)S(1)}, u32[]{:S(2)}, u32[]{:S(2)}) collective-permute-start(bf16[16,1024]{1,0:T(8,128)(2,1)} %param.3), channel_id=1, source_target_pairs={{0,1},{1,0},{2,3},{3,2},{4,5},{5,4},{6,7},{7,6},{8,9},{9,8},{10,11... | collective-permute-start | bytes 98312 | tf_op jit(solution)/shard_map/ppermute | solution.py:67
  1.2 1.3 %copy-start.1 = (bf16[16,1024]{1,0:T(8,128)(2,1)S(1)}, bf16[16,1024]{1,0:T(8,128)(2,1)}, u32[]{:S(2)}) copy-start(bf16[16,1024]{1,0:T(8,128)(2,1)} %param.3) | copy-start | bytes 98308
  1.3 1.3 %copy-start = (bf16[8,2048]{1,0:T(8,128)(2,1)S(1)}, bf16[8,2048]{1,0:T(8,128)(2,1)}, u32[]{:S(2)}) copy-start(bf16[8,2048]{1,0:T(8,128)(2,1)} %param.2) | copy-start | bytes 98308
  2.6 5.4 %collective-permute-start.4 = (bf16[16,2048]{1,0:T(8,128)(2,1)S(1)}, bf16[16,2048]{1,0:T(8,128)(2,1)S(1)}, u32[]{:S(2)}, u32[]{:S(2)}) collective-permute-start(bf16[16,2048]{1,0:T(8,128)(2,1)S(1)} %maximum_select_fusion), channel_id=1, source_target_pairs={{0,2},{1,9},{2,0},{3,11},{4,6},{5,13},{6,4},{7,15},{8,10},{9,1},{1... | collective-permute-start | bytes 196616 | tf_op jit(solution)/shard_map/ppermute | solution.py:76
  5.4 5.9 %collective-permute-start.3 = (bf16[16,2048]{1,0:T(8,128)(2,1)S(1)}, bf16[16,2048]{1,0:T(8,128)(2,1)S(1)}, u32[]{:S(2)}, u32[]{:S(2)}) collective-permute-start(bf16[16,2048]{1,0:T(8,128)(2,1)S(1)} %maximum_select_fusion), channel_id=1, source_target_pairs={{0,4},{1,17},{2,6},{3,19},{4,0},{5,21},{6,2},{7,23},{8,12},{9,25},... | collective-permute-start | bytes 196616 | tf_op jit(solution)/shard_map/ppermute | solution.py:76
  8.0 6.1 %collective-permute-start.2 = (bf16[16,2048]{1,0:T(8,128)(2,1)S(1)}, bf16[16,2048]{1,0:T(8,128)(2,1)S(1)}, u32[]{:S(2)}, u32[]{:S(2)}) collective-permute-start(bf16[16,2048]{1,0:T(8,128)(2,1)S(1)} %maximum_select_fusion), channel_id=1, source_target_pairs={{0,6},{1,25},{2,4},{3,27},{4,2},{5,29},{6,0},{7,31},{8,14},{9,17},... | collective-permute-start | bytes 196616 | tf_op jit(solution)/shard_map/ppermute | solution.py:76
  14.2 1.6 %collective-permute-start.5 = (bf16[64,2048]{1,0:T(8,128)(2,1)S(1)}, bf16[64,2048]{1,0:T(8,128)(2,1)S(1)}, u32[]{:S(2)}, u32[]{:S(2)}) collective-permute-start(bf16[64,2048]{1,0:T(8,128)(2,1)S(1)} %get-tuple-element.38), channel_id=1, source_target_pairs={{0,1},{1,0},{2,3},{3,2},{4,5},{5,4},{6,7},{7,6},{8,9},{9,8},{10,11... | collective-permute-start | bytes 786440 | tf_op jit(solution)/shard_map/ppermute | solution.py:67
  16.6 5.7 %collective-permute-start.8 = (bf16[64,768]{1,0:T(8,128)(2,1)S(1)}, bf16[64,768]{1,0:T(8,128)(2,1)S(1)}, u32[]{:S(2)}, u32[]{:S(2)}) collective-permute-start(bf16[64,768]{1,0:T(8,128)(2,1)S(1)} %fusion.17), channel_id=1, source_target_pairs={{0,24},{1,7},{2,26},{3,5},{4,28},{5,3},{6,30},{7,1},{8,16},{9,15},... | collective-permute-start | bytes 294920 | tf_op jit(solution)/shard_map/ppermute | solution.py:85
  19.2 4.7 %collective-permute-start.6 = (bf16[64,768]{1,0:T(8,128)(2,1)S(1)}, bf16[64,768]{1,0:T(8,128)(2,1)S(1)}, u32[]{:S(2)}, u32[]{:S(2)}) collective-permute-start(bf16[64,768]{1,0:T(8,128)(2,1)S(1)} %get-tuple-element.71), channel_id=1, source_target_pairs={{0,8},{1,3},{2,10},{3,1},{4,12},{5,7},{6,14},{7,5},{8,0},{9,11},{1... | collective-permute-start | bytes 294920 | tf_op jit(solution)/shard_map/ppermute | solution.py:85
  19.8 4.6 %collective-permute-start.7 = (bf16[64,768]{1,0:T(8,128)(2,1)S(1)}, bf16[64,768]{1,0:T(8,128)(2,1)S(1)}, u32[]{:S(2)}, u32[]{:S(2)}) collective-permute-start(bf16[64,768]{1,0:T(8,128)(2,1)S(1)} %get-tuple-element.72), channel_id=1, source_target_pairs={{0,16},{1,5},{2,18},{3,7},{4,20},{5,1},{6,22},{7,3},{8,24},{9,13},... | collective-permute-start | bytes 294920 | tf_op jit(solution)/shard_map/ppermute | solution.py:85
  20.3 6.4 %collective-permute-start.9 = (f32[8,128]{1,0:T(8,128)S(1)}, f32[8,128]{1,0:T(8,128)S(1)}, u32[]{:S(2)}, u32[]{:S(2)}) collective-permute-start(f32[8,128]{1,0:T(8,128)S(1)} %select_select_fusion), channel_id=1, source_target_pairs={{0,10},{10,0},{20,30},{30,20}} | collective-permute-start | bytes 12296 | tf_op jit(solution)/shard_map/ppermute | solution.py:216
  24.7 2.1 %collective-permute-start.11 = (bf16[64,640]{1,0:T(8,128)(2,1)S(1)}, bf16[64,640]{1,0:T(8,128)(2,1)S(1)}, u32[]{:S(2)}, u32[]{:S(2)}) collective-permute-start(bf16[64,640]{1,0:T(8,128)(2,1)S(1)} %pad_maximum_fusion.14), channel_id=1, source_target_pairs={{0,1},{1,0},{2,3},{3,2},{4,5},{5,4},{6,7},{7,6},{8,9},{9,8},{10,11... | collective-permute-start | bytes 245768 | tf_op jit(solution)/shard_map/ppermute | solution.py:67
  26.8 4.5 %collective-permute-start.10 = (f32[8,128]{1,0:T(8,128)S(1)}, f32[8,128]{1,0:T(8,128)S(1)}, u32[]{:S(2)}, u32[]{:S(2)}) collective-permute-start(f32[8,128]{1,0:T(8,128)S(1)} %select_add_fusion), channel_id=1, source_target_pairs={{4,0},{25,1},{7,30},{13,31},{12,8},{27,9},{5,22},{15,23},{10,14},{... | collective-permute-start | bytes 12296 | tf_op jit(solution)/shard_map/ppermute | solution.py:229
  31.4 1.4 %collective-permute-start.12 = (f32[8,128]{1,0:T(8,128)S(1)}, f32[8,128]{1,0:T(8,128)S(1)}, u32[]{:S(2)}, u32[]{:S(2)}) collective-permute-start(f32[8,128]{1,0:T(8,128)S(1)} %fusion.45), channel_id=1, source_target_pairs={{0,1},{1,0},{2,3},{3,2},{4,5},{5,4},{6,7},{7,6},{8,9},{9,8},{10,11... | collective-permute-start | bytes 12296 | tf_op jit(solution)/shard_map/ppermute | solution.py:67

commit v6 on v3

--- a/solution.py
+++ b/solution.py
@@ -152,23 +152,29 @@
     return None
 
 
+def joined(known, heard):
+    side = known.shape[0] // 2
+    here = known[side:] > 0.0
+    return jnp.concatenate(
+        [jnp.where(here, known[:side], heard[:side]), jnp.maximum(known[side:], heard[side:])], 0
+    )
+
+
+def total(values):
+    while len(values) > 1:
+        values = [x + y for x, y in zip(values[::2], values[1::2])]
+    return values[0]
+
+
 def hear(known, side):
     plan = meetings(side)
-    if plan is None:
-        step = 1
-        while step < side:
-            known = known + lax.ppermute(
-                known, "col", [(c, c ^ (2 * step)) for c in range(2 * side)]
-            )
-            step *= 2
-        return known
     used, pairs = {}, []
     for (row, z), pair in plan.items():
         for core, chip in enumerate(pair):
             from_core = used.get(chip, 0)
             used[chip] = from_core + 1
             pairs.append(((chip[0] * side + chip[1]) * 2 + from_core, (row * side + z) * 2 + core))
-    return known + lax.ppermute(known, BOTH, pairs)
+    return lax.ppermute(known, BOTH, pairs)
 
 
 def gram_body(side, view_a, view_b):
@@ -187,7 +193,8 @@
         is_a, jnp.concatenate([view_a, got_a], 0), jnp.concatenate([got_b, view_b], 1)
     )
 
-    pieces = [own] + [flip(own, side, step) for step in range(1, side)]
+    pieces = {step: flip(own, side, step) for step in range(1, side)}
+    pieces = [own] + [pieces[step] for step in range(1, side)]
     mine = jnp.concatenate(in_order(pieces, jnp.where(is_a, z, row)), 0)
     other = sibling(mine, n_col)
 
@@ -216,27 +223,22 @@
     def images_of(step):
         return lax.dynamic_slice_in_dim(extra, (row ^ step) * pair, pair, 0)
 
-    landed = [payload(images_of(0), gram, part)]
-    landed += [across(payload(images_of(step), gram, part), side, step) for step in range(1, side)]
-    summed = sum(x.astype(jnp.float32) for x in landed)
+    landed = {step: across(payload(images_of(step), gram, part), side, step) for step in range(1, side)}
+    landed[0] = payload(images_of(0), gram, part)
+    summed = total([landed[step].astype(jnp.float32) for step in range(side)])
     gram = summed[:, lanes : lanes + count] + summed[:, lanes + count : lanes + 2 * count]
     part = summed[:1, lanes + 2 * count :] + summed[count // 2 : count // 2 + 1, lanes + 2 * count :]
 
-    part = jnp.concatenate([jnp.broadcast_to(x, (count // 2, 128)) for x in split(part)], 0)
-    sent = jnp.concatenate([summed[:, :lanes].astype(jnp.bfloat16), *split(gram), part], 1)
+    sent = jnp.concatenate([summed[:, :lanes].astype(jnp.bfloat16), *split(gram)], 1)
     came = sibling(sent, n_col)
     for_a = jnp.where(is_a, came, sent)
     for_b = jnp.where(is_a, sent, came)
 
-    def part_of(sums):
-        sums = sums[:, lanes + 2 * count :].astype(jnp.float32)
-        return sums[:1] + sums[count // 2 : count // 2 + 1]
-
     slots = lax.broadcasted_iota(jnp.int32, (2 * side, 128), 0)
-    block, sums_in = slots & (side - 1), slots < side
-    known = jnp.where(block == z, jnp.where(sums_in, part_of(for_b), 1.0), 0.0)
-    known = known + jnp.where(block == row, jnp.where(sums_in, part_of(for_a), 1.0), 0.0)
-    known = hear(known, side)
+    known = jnp.where(slots < side, part, 1.0)
+    known = jnp.where((slots & (side - 1)) == jnp.where(is_a, z, row), known, 0.0)
+    known = joined(known, sibling(known, n_col))
+    heard = hear(known, side)
 
     twice = [jnp.where(is_a, normed, other_normed)] * 2
     all_a = jnp.concatenate(twice, 0)
@@ -253,21 +255,19 @@
     extra_b = images_in(for_b)
     extra_b = jnp.where(is_a, extra_b[:, :half], extra_b[:, half:])
 
-    def gradient(sums, twice, scaled, extra, start, images):
+    def terms(sums, twice):
         halves = sums[:, lanes : lanes + 2 * count]
         term = jnp.dot(halves, twice, preferred_element_type=jnp.float32)
         term = term * (2.0 * off_weight / count)
-        normed_f = twice[:count].astype(jnp.float32)
-        first = jnp.mean(term, 0)
-        second = jnp.mean(term * normed_f, 0)
+        return (term, jnp.mean(term, 0), jnp.mean(term * twice[:count].astype(jnp.float32), 0))
+
+    def gradient(terms, twice, scaled, extra, start, images):
+        term, first, second = terms
         term = lax.dynamic_slice_in_dim(term, start, images, 0)
-        normed_f = lax.dynamic_slice_in_dim(normed_f, start, images, 0)
-        return (scaled * (term - first - normed_f * second + extra.astype(jnp.float32))).astype(
+        normed = lax.dynamic_slice_in_dim(twice, start, images, 0).astype(jnp.float32)
+        return (scaled * (term - first - normed * second + extra.astype(jnp.float32))).astype(
             jnp.bfloat16
         )
-
-    grad_a = gradient(for_a, all_a, scaled_a, extra_a, col * share, share)
-    grad_b = gradient(for_b, all_b, scaled_b, extra_b, row * pair, pair)
 
     def whole(sums):
         sums = sums.astype(jnp.float32)
@@ -275,10 +275,13 @@
 
     everywhere = whole(for_a) * whole(for_b) * (off_weight / (count * count * width * side))
     everywhere = jnp.pad(jnp.sum(everywhere, 0), (0, 128 - count))
-    known, grad_a, grad_b, everywhere = lax.optimization_barrier((known, grad_a, grad_b, everywhere))
-    known = known + sibling(known, n_col)
-    on_diagonal = known[:side] * (1.0 / (width * side)) / known[side:]
-    loss = jnp.sum(everywhere + jnp.sum(on_diagonal, 0))
+    grad_a = gradient(terms(for_a, all_a), all_a, scaled_a, extra_a, col * share, share)
+    grad_b = gradient(terms(for_b, all_b), all_b, scaled_b, extra_b, row * pair, pair)
+
+    heard, grad_a, grad_b, everywhere = lax.optimization_barrier((heard, grad_a, grad_b, everywhere))
+    known = joined(known, heard)
+    known = joined(known, sibling(known, n_col))
+    loss = jnp.sum(everywhere + jnp.sum(known[:side], 0) * (1.0 / (width * side)))
     return (loss, grad_a, grad_b)
 
 
@@ -293,7 +296,7 @@
         count = share * n_col
         fits = view_b.shape == (2 * share, width // 2) and width % (128 * n_row) == 0
         fits = fits and share % 8 == 0 and count <= 128 and 2 * count % 128 == 0
-        if square and fits:
+        if square and fits and meetings(n_row):
             return gram_body(n_row, view_a, view_b)
         return tiled_body(view_a, view_b)
 

time: 32.8 us -> 32.4 us (0.988)
  waiting for transfers between devices: 16.6 us -> 15.8 us
  starting transfers between devices: 10.6 us -> 11.2 us
    ppermute x5 -> x6, waiting for transfers between devices: 4.84 us -> 4.14 us  [sibling(): return lax.ppermute(value, 'col', [(c, c ^ 1) for c in range(n_col)])]
    ppermute x5 -> x6, starting transfers between devices: 0.75 us -> 1.25 us  [sibling(): return lax.ppermute(value, 'col', [(c, c ^ 1) for c in range(n_col)])]
    convert_element_type x6 -> x2, other arithmetic: 1.47 us -> 1.32 us  [gradient(): (scaled * (term - first - normed * second + extra.astype(jnp.float32))).a...]
  transfers between devices with their start and end apart: 12 -> 13, of which waited for: 11 -> 11; matrix products, arithmetic and copies ran while one was open for 7% -> 8% of each run, Pallas kernels for 0% -> 0%
where the time goes in v6:
time: 32.4 us; the launch traced here: 32.3 us
  waiting for transfers between devices  15.8 us (49%)
  starting transfers between devices  11.2 us (35%)
  other arithmetic  3.52 us (11%)
  between operations  0.95 us (3%)
  matrix products  0.67 us (2%)
    ppermute x3, waiting for transfers between devices, flip(): return lax.ppermute(value, BOTH, pairs)  6.05 us
    ppermute x3, starting transfers between devices, flip(): return lax.ppermute(value, BOTH, pairs)  5.39 us
    ppermute x6, waiting for transfers between devices, sibling(): return lax.ppermute(value, 'col', [(c, c ^ 1) for c in range(n_col)])  4.14 us
    ppermute x3, waiting for transfers between devices, across(): return lax.ppermute(value, BOTH, pairs)  4.1 us
    ppermute x3, starting transfers between devices, across(): return lax.ppermute(value, BOTH, pairs)  3.61 us
    ppermute x1, waiting for transfers between devices, hear(): return lax.ppermute(known, BOTH, pairs)  1.52 us
    convert_element_type x2, other arithmetic, gradient(): (scaled * (term - first - normed * second + extra.astype(jnp.float32))).a...  1.32 us
    ppermute x6, starting transfers between devices, sibling(): return lax.ppermute(value, 'col', [(c, c ^ 1) for c in range(n_col)])  1.25 us
  transfers between devices with their start and end apart: 13, of which 11 were waited for; matrix products, arithmetic and copies ran while one was open for 8% of the time, Pallas kernels for 0%

profile of v6, /device:TPU:0, one launch (start us, length us, event | category | flops | bytes accessed | tf_op | source)
XLA Modules:
  0.0 32.3 jit_solution(10457463488576294608)
XLA Ops:
  0.6 0.5 %collective-permute-start = (bf16[8,2048]{1,0:T(8,128)(2,1)}, bf16[8,2048]{1,0:T(8,128)(2,1)S(1)}, u32[]{:S(2)}, u32[]{:S(2)}) collective-permute-start(bf16[8,2048]{1,0:T(8,128)(2,1)} %param.2), channel_id=1, source_target_pairs={{0,1},{1,0},{2,3},{3,2},{4,5},{5,4},{6,7},{7,6},{8,9},{9,8},{10,11... | collective-permute-start | bytes 98312 | tf_op jit(solution)/shard_map/ppermute | solution.py:67
  1.3 0.9 %collective-permute-done = bf16[8,2048]{1,0:T(8,128)(2,1)S(1)} collective-permute-done((bf16[8,2048]{1,0:T(8,128)(2,1)}, bf16[8,2048]{1,0:T(8,128)(2,1)S(1)}, u32[]{:S(2)}, u32[]{:S(2)}) %collective-permute-start) | collective-permute-done | bytes 32800 | tf_op jit(solution)/shard_map/ppermute | solution.py:67
  2.2 0.3 %collective-permute-done.1 = bf16[16,1024]{1,0:T(8,128)(2,1)S(1)} collective-permute-done((bf16[16,1024]{1,0:T(8,128)(2,1)}, bf16[16,1024]{1,0:T(8,128)(2,1)S(1)}, u32[]{:S(2)}, u32[]{:S(2)}) %collective-permute-start.1) | collective-permute-done | bytes 32800 | tf_op jit(solution)/shard_map/ppermute | solution.py:67
  2.6 2.8 %collective-permute-start.4 = (bf16[16,2048]{1,0:T(8,128)(2,1)S(1)}, bf16[16,2048]{1,0:T(8,128)(2,1)S(1)}, u32[]{:S(2)}, u32[]{:S(2)}) collective-permute-start(bf16[16,2048]{1,0:T(8,128)(2,1)S(1)} %maximum_select_fusion), channel_id=1, source_target_pairs={{0,2},{1,9},{2,0},{3,11},{4,6},{5,13},{6,4},{7,15},{8,10},{9,1},{1... | collective-permute-start | bytes 196616 | tf_op jit(solution)/shard_map/ppermute | solution.py:76
  5.4 2.6 %collective-permute-start.3 = (bf16[16,2048]{1,0:T(8,128)(2,1)S(1)}, bf16[16,2048]{1,0:T(8,128)(2,1)S(1)}, u32[]{:S(2)}, u32[]{:S(2)}) collective-permute-start(bf16[16,2048]{1,0:T(8,128)(2,1)S(1)} %maximum_select_fusion), channel_id=1, source_target_pairs={{0,4},{1,17},{2,6},{3,19},{4,0},{5,21},{6,2},{7,23},{8,12},{9,25},... | collective-permute-start | bytes 196616 | tf_op jit(solution)/shard_map/ppermute | solution.py:76
  8.0 3.3 %collective-permute-done.3 = bf16[16,2048]{1,0:T(8,128)(2,1)S(1)} collective-permute-done((bf16[16,2048]{1,0:T(8,128)(2,1)S(1)}, bf16[16,2048]{1,0:T(8,128)(2,1)S(1)}, u32[]{:S(2)}, u32[]{:S(2)}) %collective-permute-start.3) | collective-permute-done | bytes 65568 | tf_op jit(solution)/shard_map/ppermute | solution.py:76
  11.3 2.8 %collective-permute-done.2 = bf16[16,2048]{1,0:T(8,128)(2,1)S(1)} collective-permute-done((bf16[16,2048]{1,0:T(8,128)(2,1)S(1)}, bf16[16,2048]{1,0:T(8,128)(2,1)S(1)}, u32[]{:S(2)}, u32[]{:S(2)}) %collective-permute-start.2) | collective-permute-done | bytes 65568 | tf_op jit(solution)/shard_map/ppermute | solution.py:76
  14.2 0.1 fusion.7
  14.4 0.2 fusion.41
  14.6 1.1 %collective-permute-done.5 = bf16[64,2048]{1,0:T(8,128)(2,1)S(1)} collective-permute-done((bf16[64,2048]{1,0:T(8,128)(2,1)S(1)}, bf16[64,2048]{1,0:T(8,128)(2,1)S(1)}, u32[]{:S(2)}, u32[]{:S(2)}) %collective-permute-start.5) | collective-permute-done | bytes 262176 | tf_op jit(solution)/shard_map/ppermute | solution.py:67
  15.8 0.1 fusion.4
  15.9 0.1 broadcast_select_fusion
  16.1 0.1 convert_reduce_fusion
  16.3 0.1 fusion.12
  16.5 0.1 fusion.17
  16.6 2.5 %collective-permute-start.8 = (bf16[64,768]{1,0:T(8,128)(2,1)S(1)}, bf16[64,768]{1,0:T(8,128)(2,1)S(1)}, u32[]{:S(2)}, u32[]{:S(2)}) collective-permute-start(bf16[64,768]{1,0:T(8,128)(2,1)S(1)} %fusion.17), channel_id=1, source_target_pairs={{0,24},{1,7},{2,26},{3,5},{4,28},{5,3},{6,30},{7,1},{8,16},{9,15},... | collective-permute-start | bytes 294920 | tf_op jit(solution)/shard_map/ppermute | solution.py:85
  19.2 0.6 %collective-permute-start.6 = (bf16[64,768]{1,0:T(8,128)(2,1)S(1)}, bf16[64,768]{1,0:T(8,128)(2,1)S(1)}, u32[]{:S(2)}, u32[]{:S(2)}) collective-permute-start(bf16[64,768]{1,0:T(8,128)(2,1)S(1)} %get-tuple-element.63), channel_id=1, source_target_pairs={{0,8},{1,3},{2,10},{3,1},{4,12},{5,7},{6,14},{7,5},{8,0},{9,11},{1... | collective-permute-start | bytes 294920 | tf_op jit(solution)/shard_map/ppermute | solution.py:85
  19.8 0.5 %collective-permute-start.7 = (bf16[64,768]{1,0:T(8,128)(2,1)S(1)}, bf16[64,768]{1,0:T(8,128)(2,1)S(1)}, u32[]{:S(2)}, u32[]{:S(2)}) collective-permute-start(bf16[64,768]{1,0:T(8,128)(2,1)S(1)} %get-tuple-element.64), channel_id=1, source_target_pairs={{0,16},{1,5},{2,18},{3,7},{4,20},{5,1},{6,22},{7,3},{8,24},{9,13},... | collective-permute-start | bytes 294920 | tf_op jit(solution)/shard_map/ppermute | solution.py:85
  20.3 1.9 %collective-permute-done.8 = bf16[64,768]{1,0:T(8,128)(2,1)S(1)} collective-permute-done((bf16[64,768]{1,0:T(8,128)(2,1)S(1)}, bf16[64,768]{1,0:T(8,128)(2,1)S(1)}, u32[]{:S(2)}, u32[]{:S(2)}) %collective-permute-start.8) | collective-permute-done | bytes 98336 | tf_op jit(solution)/shard_map/ppermute | solution.py:85
  22.1 1.7 %collective-permute-done.6 = bf16[64,768]{1,0:T(8,128)(2,1)S(1)} collective-permute-done((bf16[64,768]{1,0:T(8,128)(2,1)S(1)}, bf16[64,768]{1,0:T(8,128)(2,1)S(1)}, u32[]{:S(2)}, u32[]{:S(2)}) %collective-permute-start.6) | collective-permute-done | bytes 98336 | tf_op jit(solution)/shard_map/ppermute | solution.py:85
  23.8 0.5 %collective-permute-done.7 = bf16[64,768]{1,0:T(8,128)(2,1)S(1)} collective-permute-done((bf16[64,768]{1,0:T(8,128)(2,1)S(1)}, bf16[64,768]{1,0:T(8,128)(2,1)S(1)}, u32[]{:S(2)}, u32[]{:S(2)}) %collective-permute-start.7) | collective-permute-done | bytes 98336 | tf_op jit(solution)/shard_map/ppermute | solution.py:85
  24.8 0.5 %collective-permute-start.11 = (bf16[64,640]{1,0:T(8,128)(2,1)S(1)}, bf16[64,640]{1,0:T(8,128)(2,1)S(1)}, u32[]{:S(2)}, u32[]{:S(2)}) collective-permute-start(bf16[64,640]{1,0:T(8,128)(2,1)S(1)} %pad_maximum_fusion.14), channel_id=1, source_target_pairs={{0,1},{1,0},{2,3},{3,2},{4,5},{5,4},{6,7},{7,6},{8,9},{9,8},{10,11... | collective-permute-start | bytes 245768 | tf_op jit(solution)/shard_map/ppermute | solution.py:67
  25.3 0.6 %collective-permute-done.9 = f32[8,128]{1,0:T(8,128)S(1)} collective-permute-done((f32[8,128]{1,0:T(8,128)S(1)}, f32[8,128]{1,0:T(8,128)S(1)}, u32[]{:S(2)}, u32[]{:S(2)}) %collective-permute-start.9) | collective-permute-done | bytes 4128 | tf_op jit(solution)/shard_map/ppermute | solution.py:67
  25.8 1.0 %collective-permute-start.10 = (f32[8,128]{1,0:T(8,128)S(1)}, f32[8,128]{1,0:T(8,128)S(1)}, u32[]{:S(2)}, u32[]{:S(2)}) collective-permute-start(f32[8,128]{1,0:T(8,128)S(1)} %pad_maximum_fusion.16), channel_id=1, source_target_pairs={{18,0},{24,1},{6,30},{12,31},{13,8},{25,9},{4,22},{14,23},{16,2},{... | collective-permute-start | bytes 12296 | tf_op jit(solution)/shard_map/ppermute | solution.py:177
  26.9 0.2 fusion.35
  27.2 0.3 fusion.34
  27.5 0.7 %multiply_convert_fusion.1 = bf16[8,2048]{1,0:T(8,128)(2,1)} fusion(f32[64,2048]{1,0:T(8,128)S(1)} %get-tuple-element.77, s32[]{:T(128)S(6)} %select_n.202, s32[]{:T(128)S(6)} %select_n.203, bf16[64,2048]{1,0:T(8,128)(2,1)S(1)} %get-tuple-element.27, bf16[16,2048]{1,0:T(8,128)(2,1)S(1)} %pad_maximum_fusion.15, f32[2048]{0:T(1024)S(1)} %broadcast_multiply_fusion, ...), kind=kLoop, calls=%fused_computation.56 | loop fusion | flops 196608 | bytes 450569 | tf_op jit(solution)/shard_map/convert_element_type | solution.py:268
  28.1 0.7 %multiply_convert_fusion = bf16[16,1024]{1,0:T(8,128)(2,1)} fusion(f32[64,1024]{1,0:T(8,128)S(1)} %get-tuple-element.78, s32[]{:T(128)S(6)} %select_n.187, s32[]{:T(128)S(6)} %select_n.211, bf16[64,1024]{1,0:T(8,128)(2,1)S(1)} %slice_select_fusion, bf16[16,512]{1,0:T(8,128)(2,1)S(1)} %get-tuple-element.57, bf16[16,512]{1,0:T(8,128)(2,1)S(1)} %get-tuple-element.58, ...), kind=kLoop, calls=%fused_computation.55 | loop fusion | flops 327680 | bytes 307209 | tf_op jit(solution)/shard_map/convert_element_type | solution.py:268
  28.8 0.1 fusion.26
  28.9 1.5 %collective-permute-done.10 = f32[8,128]{1,0:T(8,128)S(1)} collective-permute-done((f32[8,128]{1,0:T(8,128)S(1)}, f32[8,128]{1,0:T(8,128)S(1)}, u32[]{:S(2)}, u32[]{:S(2)}) %collective-permute-start.10) | collective-permute-done | bytes 4128 | tf_op jit(solution)/shard_map/ppermute | solution.py:177
  30.5 1.2 %collective-permute-done.12 = f32[8,128]{1,0:T(8,128)S(1)} collective-permute-done((f32[8,128]{1,0:T(8,128)S(1)}, f32[8,128]{1,0:T(8,128)S(1)}, u32[]{:S(2)}, u32[]{:S(2)}) %collective-permute-start.12) | collective-permute-done | bytes 4128 | tf_op jit(solution)/shard_map/ppermute | solution.py:67
  31.7 0.6 %add_reduce_fusion = f32[]{:T(128)} fusion(f32[128]{0:T(128)S(1)} %pad.4, f32[128]{0:T(128)S(1)} %select_reduce_fusion), kind=kLoop, calls=%fused_computation.117 | loop fusion | flops 383 | bytes 1028 | tf_op jit(solution)/shard_map/reduce_sum | solution.py:284
  (52 shorter events, 1.2 us)
Async XLA Ops:
  0.6 1.6 %collective-permute-start = (bf16[8,2048]{1,0:T(8,128)(2,1)}, bf16[8,2048]{1,0:T(8,128)(2,1)S(1)}, u32[]{:S(2)}, u32[]{:S(2)}) collective-permute-start(bf16[8,2048]{1,0:T(8,128)(2,1)} %param.2), channel_id=1, source_target_pairs={{0,1},{1,0},{2,3},{3,2},{4,5},{5,4},{6,7},{7,6},{8,9},{9,8},{10,11... | collective-permute-start | bytes 98312 | tf_op jit(solution)/shard_map/ppermute | solution.py:67
  1.1 1.4 %collective-permute-start.1 = (bf16[16,1024]{1,0:T(8,128)(2,1)}, bf16[16,1024]{1,0:T(8,128)(2,1)S(1)}, u32[]{:S(2)}, u32[]{:S(2)}) collective-permute-start(bf16[16,1024]{1,0:T(8,128)(2,1)} %param.3), channel_id=1, source_target_pairs={{0,1},{1,0},{2,3},{3,2},{4,5},{5,4},{6,7},{7,6},{8,9},{9,8},{10,11... | collective-permute-start | bytes 98312 | tf_op jit(solution)/shard_map/ppermute | solution.py:67
  1.2 1.3 %copy-start.1 = (bf16[16,1024]{1,0:T(8,128)(2,1)S(1)}, bf16[16,1024]{1,0:T(8,128)(2,1)}, u32[]{:S(2)}) copy-start(bf16[16,1024]{1,0:T(8,128)(2,1)} %param.3) | copy-start | bytes 98308
  1.2 1.3 %copy-start = (bf16[8,2048]{1,0:T(8,128)(2,1)S(1)}, bf16[8,2048]{1,0:T(8,128)(2,1)}, u32[]{:S(2)}) copy-start(bf16[8,2048]{1,0:T(8,128)(2,1)} %param.2) | copy-start | bytes 98308
  2.6 5.4 %collective-permute-start.4 = (bf16[16,2048]{1,0:T(8,128)(2,1)S(1)}, bf16[16,2048]{1,0:T(8,128)(2,1)S(1)}, u32[]{:S(2)}, u32[]{:S(2)}) collective-permute-start(bf16[16,2048]{1,0:T(8,128)(2,1)S(1)} %maximum_select_fusion), channel_id=1, source_target_pairs={{0,2},{1,9},{2,0},{3,11},{4,6},{5,13},{6,4},{7,15},{8,10},{9,1},{1... | collective-permute-start | bytes 196616 | tf_op jit(solution)/shard_map/ppermute | solution.py:76
  5.4 5.9 %collective-permute-start.3 = (bf16[16,2048]{1,0:T(8,128)(2,1)S(1)}, bf16[16,2048]{1,0:T(8,128)(2,1)S(1)}, u32[]{:S(2)}, u32[]{:S(2)}) collective-permute-start(bf16[16,2048]{1,0:T(8,128)(2,1)S(1)} %maximum_select_fusion), channel_id=1, source_target_pairs={{0,4},{1,17},{2,6},{3,19},{4,0},{5,21},{6,2},{7,23},{8,12},{9,25},... | collective-permute-start | bytes 196616 | tf_op jit(solution)/shard_map/ppermute | solution.py:76
  8.0 6.1 %collective-permute-start.2 = (bf16[16,2048]{1,0:T(8,128)(2,1)S(1)}, bf16[16,2048]{1,0:T(8,128)(2,1)S(1)}, u32[]{:S(2)}, u32[]{:S(2)}) collective-permute-start(bf16[16,2048]{1,0:T(8,128)(2,1)S(1)} %maximum_select_fusion), channel_id=1, source_target_pairs={{0,6},{1,25},{2,4},{3,27},{4,2},{5,29},{6,0},{7,31},{8,14},{9,17},... | collective-permute-start | bytes 196616 | tf_op jit(solution)/shard_map/ppermute | solution.py:76
  14.2 1.6 %collective-permute-start.5 = (bf16[64,2048]{1,0:T(8,128)(2,1)S(1)}, bf16[64,2048]{1,0:T(8,128)(2,1)S(1)}, u32[]{:S(2)}, u32[]{:S(2)}) collective-permute-start(bf16[64,2048]{1,0:T(8,128)(2,1)S(1)} %get-tuple-element.30), channel_id=1, source_target_pairs={{0,1},{1,0},{2,3},{3,2},{4,5},{5,4},{6,7},{7,6},{8,9},{9,8},{10,11... | collective-permute-start | bytes 786440 | tf_op jit(solution)/shard_map/ppermute | solution.py:67
  16.6 5.6 %collective-permute-start.8 = (bf16[64,768]{1,0:T(8,128)(2,1)S(1)}, bf16[64,768]{1,0:T(8,128)(2,1)S(1)}, u32[]{:S(2)}, u32[]{:S(2)}) collective-permute-start(bf16[64,768]{1,0:T(8,128)(2,1)S(1)} %fusion.17), channel_id=1, source_target_pairs={{0,24},{1,7},{2,26},{3,5},{4,28},{5,3},{6,30},{7,1},{8,16},{9,15},... | collective-permute-start | bytes 294920 | tf_op jit(solution)/shard_map/ppermute | solution.py:85
  19.2 4.7 %collective-permute-start.6 = (bf16[64,768]{1,0:T(8,128)(2,1)S(1)}, bf16[64,768]{1,0:T(8,128)(2,1)S(1)}, u32[]{:S(2)}, u32[]{:S(2)}) collective-permute-start(bf16[64,768]{1,0:T(8,128)(2,1)S(1)} %get-tuple-element.63), channel_id=1, source_target_pairs={{0,8},{1,3},{2,10},{3,1},{4,12},{5,7},{6,14},{7,5},{8,0},{9,11},{1... | collective-permute-start | bytes 294920 | tf_op jit(solution)/shard_map/ppermute | solution.py:85
  19.8 4.6 %collective-permute-start.7 = (bf16[64,768]{1,0:T(8,128)(2,1)S(1)}, bf16[64,768]{1,0:T(8,128)(2,1)S(1)}, u32[]{:S(2)}, u32[]{:S(2)}) collective-permute-start(bf16[64,768]{1,0:T(8,128)(2,1)S(1)} %get-tuple-element.64), channel_id=1, source_target_pairs={{0,16},{1,5},{2,18},{3,7},{4,20},{5,1},{6,22},{7,3},{8,24},{9,13},... | collective-permute-start | bytes 294920 | tf_op jit(solution)/shard_map/ppermute | solution.py:85
  24.6 1.2 %collective-permute-start.9 = (f32[8,128]{1,0:T(8,128)S(1)}, f32[8,128]{1,0:T(8,128)S(1)}, u32[]{:S(2)}, u32[]{:S(2)}) collective-permute-start(f32[8,128]{1,0:T(8,128)S(1)} %select_select_fusion), channel_id=1, source_target_pairs={{0,1},{1,0},{2,3},{3,2},{4,5},{5,4},{6,7},{7,6},{8,9},{9,8},{10,11... | collective-permute-start | bytes 12296 | tf_op jit(solution)/shard_map/ppermute | solution.py:67
  24.8 2.1 %collective-permute-start.11 = (bf16[64,640]{1,0:T(8,128)(2,1)S(1)}, bf16[64,640]{1,0:T(8,128)(2,1)S(1)}, u32[]{:S(2)}, u32[]{:S(2)}) collective-permute-start(bf16[64,640]{1,0:T(8,128)(2,1)S(1)} %pad_maximum_fusion.14), channel_id=1, source_target_pairs={{0,1},{1,0},{2,3},{3,2},{4,5},{5,4},{6,7},{7,6},{8,9},{9,8},{10,11... | collective-permute-start | bytes 245768 | tf_op jit(solution)/shard_map/ppermute | solution.py:67
  25.8 4.6 %collective-permute-start.10 = (f32[8,128]{1,0:T(8,128)S(1)}, f32[8,128]{1,0:T(8,128)S(1)}, u32[]{:S(2)}, u32[]{:S(2)}) collective-permute-start(f32[8,128]{1,0:T(8,128)S(1)} %pad_maximum_fusion.16), channel_id=1, source_target_pairs={{18,0},{24,1},{6,30},{12,31},{13,8},{25,9},{4,22},{14,23},{16,2},{... | collective-permute-start | bytes 12296 | tf_op jit(solution)/shard_map/ppermute | solution.py:177
  30.4 1.2 %collective-permute-start.12 = (f32[8,128]{1,0:T(8,128)S(1)}, f32[8,128]{1,0:T(8,128)S(1)}, u32[]{:S(2)}, u32[]{:S(2)}) collective-permute-start(f32[8,128]{1,0:T(8,128)S(1)} %pad_maximum_fusion.17), channel_id=1, source_target_pairs={{0,1},{1,0},{2,3},{3,2},{4,5},{5,4},{6,7},{7,6},{8,9},{9,8},{10,11... | collective-permute-start | bytes 12296 | tf_op jit(solution)/shard_map/ppermute | solution.py:67

commit v7 on v6

--- a/solution.py
+++ b/solution.py
@@ -76,12 +76,13 @@
     return lax.ppermute(value, BOTH, pairs)
 
 
-def across(value, side, step):
+def across(value, side, step, along_z=1):
     pairs = []
     for row in range(side):
         for z in range(side):
-            pairs.append(((row * side + z) * 2, ((row ^ step) * side + z) * 2))
-            pairs.append(((row * side + z) * 2 + 1, (row * side + (z ^ step)) * 2 + 1))
+            for core in range(2):
+                to = (row, z ^ step) if core == along_z else (row ^ step, z)
+                pairs.append(((row * side + z) * 2 + core, (to[0] * side + to[1]) * 2 + core))
     return lax.ppermute(value, BOTH, pairs)
 
 
@@ -210,6 +211,10 @@
     corr = jnp.mean(normed_f * other_f, 0)
     slope = jnp.where(diagonal, rounded(2.0 * (corr - 1.0)) - 2.0 * off_weight * corr, 0.0)
     extra = (slope * (normed_f - jnp.mean(normed_f, 0) - other_f * corr)).astype(jnp.bfloat16)
+    other_extra = (slope * (other_f - jnp.mean(other_f, 0) - normed_f * corr)).astype(jnp.bfloat16)
+    other_gram = lax.dot_general(
+        other_normed, other_normed, (((1,), (1,)), ((), ())), preferred_element_type=jnp.float32
+    )
     part = jnp.square(1.0 - corr) - off_weight * jnp.square(corr)
     part = jnp.sum(jnp.where(diagonal, part, 0.0).reshape(-1, 128), 0, keepdims=True)
 
@@ -220,25 +225,50 @@
         part = [jnp.broadcast_to(x, (count // 2, 128)) for x in split(part)]
         return jnp.concatenate([jnp.concatenate(images, 0), *split(gram), jnp.concatenate(part, 0)], 1)
 
-    def images_of(step):
+    def images_of(extra, step):
         return lax.dynamic_slice_in_dim(extra, (row ^ step) * pair, pair, 0)
 
-    landed = {step: across(payload(images_of(step), gram, part), side, step) for step in range(1, side)}
-    landed[0] = payload(images_of(0), gram, part)
-    summed = total([landed[step].astype(jnp.float32) for step in range(side)])
-    gram = summed[:, lanes : lanes + count] + summed[:, lanes + count : lanes + 2 * count]
-    part = summed[:1, lanes + 2 * count :] + summed[count // 2 : count // 2 + 1, lanes + 2 * count :]
-
-    sent = jnp.concatenate([summed[:, :lanes].astype(jnp.bfloat16), *split(gram)], 1)
-    came = sibling(sent, n_col)
-    for_a = jnp.where(is_a, came, sent)
-    for_b = jnp.where(is_a, sent, came)
+    changed = 3
+    landed = {}
+    for step in [1, 2, 3]:
+        if step == changed:
+            lone = across(payload(images_of(other_extra, step), other_gram, part), side, step, 0)
+        else:
+            landed[step] = across(payload(images_of(extra, step), gram, part), side, step, 1)
+    landed[0] = payload(images_of(extra, 0), gram, part)
+
+    def section(value, i):
+        first = (0, lanes, lanes + 2 * count, lanes + 2 * count + 128)
+        return value[:, first[i] : first[i + 1]].astype(jnp.float32)
+
+    def whole(halves):
+        return halves[:, :count] + halves[:, count:]
+
+    def part_of(value):
+        value = section(value, 2)
+        return value[:1] + value[count // 2 : count // 2 + 1]
 
     slots = lax.broadcasted_iota(jnp.int32, (2 * side, 128), 0)
-    known = jnp.where(slots < side, part, 1.0)
-    known = jnp.where((slots & (side - 1)) == jnp.where(is_a, z, row), known, 0.0)
+    at = jnp.where(jnp.logical_xor(is_a, (row ^ z) == changed), z, row)
+    known = jnp.where(slots < side, part_of(lone) + sum(part_of(landed[i]) for i in landed), 1.0)
+    known = jnp.where((slots & (side - 1)) == at, known, 0.0)
     known = joined(known, sibling(known, n_col))
     heard = hear(known, side)
+
+    near = landed[changed ^ 1]
+    far = total([whole(section(landed[i], 1)) for i in landed if i != changed ^ 1])
+    images = sum(section(landed[i], 0) for i in landed).astype(jnp.bfloat16)
+    sent = jnp.concatenate([images, near[:, lanes : lanes + 2 * count], *split(far)], 1)
+    came = sibling(sent, n_col)
+    lone_came = sibling(lone[:, : lanes + 2 * count], n_col)
+
+    def sums_of(most, lone):
+        gram = whole(section(most, 1)) + whole(section(lone, 1)) + whole(section(most, 2))
+        images = (section(most, 0) + section(lone, 0)).astype(jnp.bfloat16)
+        return jnp.concatenate([images, *split(gram)], 1)
+
+    for_a = sums_of(jnp.where(is_a, came, sent), jnp.where(is_a, lone[:, : lanes + 2 * count], lone_came))
+    for_b = sums_of(jnp.where(is_a, sent, came), jnp.where(is_a, lone_came, lone[:, : lanes + 2 * count]))
 
     twice = [jnp.where(is_a, normed, other_normed)] * 2
     all_a = jnp.concatenate(twice, 0)
@@ -269,11 +299,8 @@
             jnp.bfloat16
         )
 
-    def whole(sums):
-        sums = sums.astype(jnp.float32)
-        return sums[:, lanes : lanes + count] + sums[:, lanes + count : lanes + 2 * count]
-
-    everywhere = whole(for_a) * whole(for_b) * (off_weight / (count * count * width * side))
+    everywhere = whole(section(for_a, 1)) * whole(section(for_b, 1))
+    everywhere = everywhere * (off_weight / (count * count * width * side))
     everywhere = jnp.pad(jnp.sum(everywhere, 0), (0, 128 - count))
     grad_a = gradient(terms(for_a, all_a), all_a, scaled_a, extra_a, col * share, share)
     grad_b = gradient(terms(for_b, all_b), all_b, scaled_b, extra_b, row * pair, pair)

time: 32.4 us -> 31.3 us (0.966)
  waiting for transfers between devices: 15.8 us -> 11.8 us
  starting transfers between devices: 11.2 us -> 13 us
  other arithmetic: 3.52 us -> 4.15 us
  matrix products: 0.67 us -> 1 us
    ppermute x3, waiting for transfers between devices: 6.05 us -> 4.52 us  [flip(): return lax.ppermute(value, BOTH, pairs)]
    ppermute x3, waiting for transfers between devices: 4.1 us -> 2.78 us  [across(): return lax.ppermute(value, BOTH, pairs)]
    ppermute x1, waiting for transfers between devices: 1.52 us -> 0.33 us  [hear(): return lax.ppermute(known, BOTH, pairs)]
    ppermute x3, starting transfers between devices: 3.61 us -> 4.76 us  [across(): return lax.ppermute(value, BOTH, pairs)]
    ppermute x1, starting transfers between devices: 0.96 us -> 1.48 us  [hear(): return lax.ppermute(known, BOTH, pairs)]
    convert_element_type x1 -> x17, other arithmetic: 0.08 us -> 0.44 us  [the longest x9 0.28 us: section(): return value[:, first[i]:first[i + 1]].astype(jnp.float32)]
    ppermute x6 -> x7, starting transfers between devices: 1.25 us -> 1.33 us  [sibling(): return lax.ppermute(value, 'col', [(c, c ^ 1) for c in range(n_col)])]
    ppermute x6 -> x7, waiting for transfers between devices: 4.14 us -> 4.15 us  [sibling(): return lax.ppermute(value, 'col', [(c, c ^ 1) for c in range(n_col)])]
  transfers between devices with their start and end apart: 13 -> 14, of which waited for: 11 -> 10; matrix products, arithmetic and copies ran while one was open for 8% -> 12% of each run, Pallas kernels for 0% -> 0%
where the time goes in v7:
time: 31.3 us; the launch traced here: 31.1 us
  starting transfers between devices  13 us (42%)
  waiting for transfers between devices  11.8 us (38%)
  other arithmetic  4.15 us (13%)
  between operations  1.07 us (3%)
  matrix products  1 us (3%)
    ppermute x3, starting transfers between devices, flip(): return lax.ppermute(value, BOTH, pairs)  5.47 us
    ppermute x3, starting transfers between devices, across(): return lax.ppermute(value, BOTH, pairs)  4.76 us
    ppermute x3, waiting for transfers between devices, flip(): return lax.ppermute(value, BOTH, pairs)  4.52 us
    ppermute x7, waiting for transfers between devices, sibling(): return lax.ppermute(value, 'col', [(c, c ^ 1) for c in range(n_col)])  4.15 us
    ppermute x3, waiting for transfers between devices, across(): return lax.ppermute(value, BOTH, pairs)  2.78 us
    ppermute x1, starting transfers between devices, hear(): return lax.ppermute(known, BOTH, pairs)  1.48 us
    ppermute x7, starting transfers between devices, sibling(): return lax.ppermute(value, 'col', [(c, c ^ 1) for c in range(n_col)])  1.33 us
    convert_element_type x2, other arithmetic, gradient(): (scaled * (term - first - normed * second + extra.astype(jnp.float32))).a...  1.32 us
  transfers between devices with their start and end apart: 14, of which 10 were waited for; matrix products, arithmetic and copies ran while one was open for 12% of the time, Pallas kernels for 0%

profile of v7, /device:TPU:0, one launch (start us, length us, event | category | flops | bytes accessed | tf_op | source)
XLA Modules:
  0.0 31.1 jit_solution(421539824746441377)
XLA Ops:
  0.6 0.5 %collective-permute-start = (bf16[8,2048]{1,0:T(8,128)(2,1)}, bf16[8,2048]{1,0:T(8,128)(2,1)S(1)}, u32[]{:S(2)}, u32[]{:S(2)}) collective-permute-start(bf16[8,2048]{1,0:T(8,128)(2,1)} %param.2), channel_id=1, source_target_pairs={{0,1},{1,0},{2,3},{3,2},{4,5},{5,4},{6,7},{7,6},{8,9},{9,8},{10,11... | collective-permute-start | bytes 98312 | tf_op jit(solution)/shard_map/ppermute | solution.py:67
  1.2 1.0 %collective-permute-done = bf16[8,2048]{1,0:T(8,128)(2,1)S(1)} collective-permute-done((bf16[8,2048]{1,0:T(8,128)(2,1)}, bf16[8,2048]{1,0:T(8,128)(2,1)S(1)}, u32[]{:S(2)}, u32[]{:S(2)}) %collective-permute-start) | collective-permute-done | bytes 32800 | tf_op jit(solution)/shard_map/ppermute | solution.py:67
  2.2 0.3 %collective-permute-done.1 = bf16[16,1024]{1,0:T(8,128)(2,1)S(1)} collective-permute-done((bf16[16,1024]{1,0:T(8,128)(2,1)}, bf16[16,1024]{1,0:T(8,128)(2,1)S(1)}, u32[]{:S(2)}, u32[]{:S(2)}) %collective-permute-start.1) | collective-permute-done | bytes 32800 | tf_op jit(solution)/shard_map/ppermute | solution.py:67
  2.6 4.8 %collective-permute-start.2 = (bf16[16,2048]{1,0:T(8,128)(2,1)S(1)}, bf16[16,2048]{1,0:T(8,128)(2,1)S(1)}, u32[]{:S(2)}, u32[]{:S(2)}) collective-permute-start(bf16[16,2048]{1,0:T(8,128)(2,1)S(1)} %maximum_select_fusion), channel_id=1, source_target_pairs={{0,6},{1,25},{2,4},{3,27},{4,2},{5,29},{6,0},{7,31},{8,14},{9,17},... | collective-permute-start | bytes 196616 | tf_op jit(solution)/shard_map/ppermute | solution.py:76
  7.4 0.6 %collective-permute-start.4 = (bf16[16,2048]{1,0:T(8,128)(2,1)S(1)}, bf16[16,2048]{1,0:T(8,128)(2,1)S(1)}, u32[]{:S(2)}, u32[]{:S(2)}) collective-permute-start(bf16[16,2048]{1,0:T(8,128)(2,1)S(1)} %maximum_select_fusion), channel_id=1, source_target_pairs={{0,2},{1,9},{2,0},{3,11},{4,6},{5,13},{6,4},{7,15},{8,10},{9,1},{1... | collective-permute-start | bytes 196616 | tf_op jit(solution)/shard_map/ppermute | solution.py:76
  8.1 1.7 %collective-permute-done.2 = bf16[16,2048]{1,0:T(8,128)(2,1)S(1)} collective-permute-done((bf16[16,2048]{1,0:T(8,128)(2,1)S(1)}, bf16[16,2048]{1,0:T(8,128)(2,1)S(1)}, u32[]{:S(2)}, u32[]{:S(2)}) %collective-permute-start.2) | collective-permute-done | bytes 65568 | tf_op jit(solution)/shard_map/ppermute | solution.py:76
  9.8 2.8 %collective-permute-done.3 = bf16[16,2048]{1,0:T(8,128)(2,1)S(1)} collective-permute-done((bf16[16,2048]{1,0:T(8,128)(2,1)S(1)}, bf16[16,2048]{1,0:T(8,128)(2,1)S(1)}, u32[]{:S(2)}, u32[]{:S(2)}) %collective-permute-start.3) | collective-permute-done | bytes 65568 | tf_op jit(solution)/shard_map/ppermute | solution.py:76
  13.0 0.2 fusion.58
  13.2 1.1 %collective-permute-done.5 = bf16[64,2048]{1,0:T(8,128)(2,1)S(1)} collective-permute-done((bf16[64,2048]{1,0:T(8,128)(2,1)S(1)}, bf16[64,2048]{1,0:T(8,128)(2,1)S(1)}, u32[]{:S(2)}, u32[]{:S(2)}) %collective-permute-start.5) | collective-permute-done | bytes 262176 | tf_op jit(solution)/shard_map/ppermute | solution.py:67
  14.5 0.1 broadcast_select_fusion
  14.6 0.1 convert_reduce_fusion.2
  14.8 0.2 reduce-precision_convert_fusion.4
  15.3 1.7 %collective-permute-start.6 = (bf16[64,768]{1,0:T(8,128)(2,1)S(1)}, bf16[64,768]{1,0:T(8,128)(2,1)S(1)}, u32[]{:S(2)}, u32[]{:S(2)}) collective-permute-start(bf16[64,768]{1,0:T(8,128)(2,1)S(1)} %fusion.15), channel_id=1, source_target_pairs={{0,6},{1,25},{2,4},{3,27},{4,2},{5,29},{6,0},{7,31},{8,14},{9,17},... | collective-permute-start | bytes 294920 | tf_op jit(solution)/shard_map/ppermute | solution.py:86
  16.9 0.1 multiply_convert_fusion
  17.2 1.6 %collective-permute-start.7 = (bf16[64,768]{1,0:T(8,128)(2,1)S(1)}, bf16[64,768]{1,0:T(8,128)(2,1)S(1)}, u32[]{:S(2)}, u32[]{:S(2)}) collective-permute-start(bf16[64,768]{1,0:T(8,128)(2,1)S(1)} %get-tuple-element.75), channel_id=1, source_target_pairs={{0,8},{1,3},{2,10},{3,1},{4,12},{5,7},{6,14},{7,5},{8,0},{9,11},{1... | collective-permute-start | bytes 294920 | tf_op jit(solution)/shard_map/ppermute | solution.py:86
  18.8 1.5 %collective-permute-start.8 = (bf16[64,768]{1,0:T(8,128)(2,1)S(1)}, bf16[64,768]{1,0:T(8,128)(2,1)S(1)}, u32[]{:S(2)}, u32[]{:S(2)}) collective-permute-start(bf16[64,768]{1,0:T(8,128)(2,1)S(1)} %get-tuple-element.76), channel_id=1, source_target_pairs={{0,16},{1,5},{2,18},{3,7},{4,20},{5,1},{6,22},{7,3},{8,24},{9,13},... | collective-permute-start | bytes 294920 | tf_op jit(solution)/shard_map/ppermute | solution.py:86
  20.4 1.5 %collective-permute-done.6 = bf16[64,768]{1,0:T(8,128)(2,1)S(1)} collective-permute-done((bf16[64,768]{1,0:T(8,128)(2,1)S(1)}, bf16[64,768]{1,0:T(8,128)(2,1)S(1)}, u32[]{:S(2)}, u32[]{:S(2)}) %collective-permute-start.6) | collective-permute-done | bytes 98336 | tf_op jit(solution)/shard_map/ppermute | solution.py:86
  22.1 1.3 %collective-permute-done.8 = bf16[64,768]{1,0:T(8,128)(2,1)S(1)} collective-permute-done((bf16[64,768]{1,0:T(8,128)(2,1)S(1)}, bf16[64,768]{1,0:T(8,128)(2,1)S(1)}, u32[]{:S(2)}, u32[]{:S(2)}) %collective-permute-start.8) | collective-permute-done | bytes 98336 | tf_op jit(solution)/shard_map/ppermute | solution.py:86
  23.5 0.3 collective-permute-start.9
  23.9 0.2 collective-permute-start.11
  24.1 0.5 %collective-permute-done.9 = f32[8,128]{1,0:T(8,128)S(1)} collective-permute-done((f32[8,128]{1,0:T(8,128)S(1)}, f32[8,128]{1,0:T(8,128)S(1)}, u32[]{:S(2)}, u32[]{:S(2)}) %collective-permute-start.9) | collective-permute-done | bytes 4128 | tf_op jit(solution)/shard_map/ppermute | solution.py:67
  24.7 1.5 %collective-permute-start.10 = (f32[8,128]{1,0:T(8,128)S(1)}, f32[8,128]{1,0:T(8,128)S(1)}, u32[]{:S(2)}, u32[]{:S(2)}) collective-permute-start(f32[8,128]{1,0:T(8,128)S(1)} %pad_maximum_fusion.14), channel_id=1, source_target_pairs={{18,0},{24,1},{6,30},{12,31},{13,8},{25,9},{4,22},{14,23},{16,2},{... | collective-permute-start | bytes 12296 | tf_op jit(solution)/shard_map/ppermute | solution.py:178
  26.4 0.1 reduce-precision_convert_fusion.1
  26.5 0.1 reduce-precision_convert_fusion
  26.8 0.3 fusion.49
  27.1 0.3 %fusion.48 = (f32[2048]{0:T(1024)S(1)}, f32[2048]{0:T(1024)S(1)}, f32[64,2048]{1,0:T(8,128)S(1)}) fusion(bf16[64,2048]{1,0:T(8,128)(2,1)S(1)} %get-tuple-element.30, bf16[64,64]{1,0:T(8,128)(2,1)S(1)} %fusion.25, bf16[64,64]{1,0:T(8,128)(2,1)S(1)} %get-tuple-element.26), kind=kOutput, calls=%fused_computation.166 | convolution fusion | flops 35287040 | bytes 819200 | tf_op jit(solution)/shard_map/dot_general | solution.py:290
  27.5 0.7 %multiply_convert_fusion.2 = bf16[8,2048]{1,0:T(8,128)(2,1)} fusion(f32[64,2048]{1,0:T(8,128)S(1)} %get-tuple-element.91, s32[]{:T(128)S(6)} %select_n.219, s32[]{:T(128)S(6)} %select_n.220, bf16[64,2048]{1,0:T(8,128)(2,1)S(1)} %get-tuple-element.30, bf16[16,2048]{1,0:T(8,128)(2,1)S(1)} %pad_maximum_fusion.11, f32[2048]{0:T(1024)S(1)} %broadcast_multiply_fusion, ...), kind=kLoop, calls=%fused_computation.55 | loop fusion | flops 196608 | bytes 450569 | tf_op jit(solution)/shard_map/convert_element_type | solution.py:298
  28.2 0.7 %multiply_convert_fusion.1 = bf16[16,1024]{1,0:T(8,128)(2,1)} fusion(f32[64,1024]{1,0:T(8,128)S(1)} %get-tuple-element.92, s32[]{:T(128)S(6)} %select_n.213, s32[]{:T(128)S(6)} %select_n.229, bf16[64,1024]{1,0:T(8,128)(2,1)S(1)} %slice_select_fusion, bf16[16,512]{1,0:T(8,128)(2,1)S(1)} %get-tuple-element.65, bf16[16,512]{1,0:T(8,128)(2,1)S(1)} %get-tuple-element.66, ...), kind=kLoop, calls=%fused_computation.54 | loop fusion | flops 327680 | bytes 307209 | tf_op jit(solution)/shard_map/convert_element_type | solution.py:298
  28.8 0.1 fusion.30
  28.9 0.3 %collective-permute-done.10 = f32[8,128]{1,0:T(8,128)S(1)} collective-permute-done((f32[8,128]{1,0:T(8,128)S(1)}, f32[8,128]{1,0:T(8,128)S(1)}, u32[]{:S(2)}, u32[]{:S(2)}) %collective-permute-start.10) | collective-permute-done | bytes 4128 | tf_op jit(solution)/shard_map/ppermute | solution.py:178
  29.4 1.2 %collective-permute-done.13 = f32[8,128]{1,0:T(8,128)S(1)} collective-permute-done((f32[8,128]{1,0:T(8,128)S(1)}, f32[8,128]{1,0:T(8,128)S(1)}, u32[]{:S(2)}, u32[]{:S(2)}) %collective-permute-start.13) | collective-permute-done | bytes 4128 | tf_op jit(solution)/shard_map/ppermute | solution.py:67
  30.5 0.6 %add_reduce_fusion = f32[]{:T(128)} fusion(f32[128]{0:T(128)S(1)} %pad.4, f32[128]{0:T(128)S(1)} %select_reduce_fusion), kind=kLoop, calls=%fused_computation.160 | loop fusion | flops 383 | bytes 1028 | tf_op jit(solution)/shard_map/reduce_sum | solution.py:311
  (76 shorter events, 1.9 us)
Async XLA Ops:
  0.6 1.6 %collective-permute-start = (bf16[8,2048]{1,0:T(8,128)(2,1)}, bf16[8,2048]{1,0:T(8,128)(2,1)S(1)}, u32[]{:S(2)}, u32[]{:S(2)}) collective-permute-start(bf16[8,2048]{1,0:T(8,128)(2,1)} %param.2), channel_id=1, source_target_pairs={{0,1},{1,0},{2,3},{3,2},{4,5},{5,4},{6,7},{7,6},{8,9},{9,8},{10,11... | collective-permute-start | bytes 98312 | tf_op jit(solution)/shard_map/ppermute | solution.py:67
  1.1 1.4 %collective-permute-start.1 = (bf16[16,1024]{1,0:T(8,128)(2,1)}, bf16[16,1024]{1,0:T(8,128)(2,1)S(1)}, u32[]{:S(2)}, u32[]{:S(2)}) collective-permute-start(bf16[16,1024]{1,0:T(8,128)(2,1)} %param.3), channel_id=1, source_target_pairs={{0,1},{1,0},{2,3},{3,2},{4,5},{5,4},{6,7},{7,6},{8,9},{9,8},{10,11... | collective-permute-start | bytes 98312 | tf_op jit(solution)/shard_map/ppermute | solution.py:67
  1.2 1.3 %copy-start.1 = (bf16[16,1024]{1,0:T(8,128)(2,1)S(1)}, bf16[16,1024]{1,0:T(8,128)(2,1)}, u32[]{:S(2)}) copy-start(bf16[16,1024]{1,0:T(8,128)(2,1)} %param.3) | copy-start | bytes 98308
  1.2 1.3 %copy-start = (bf16[8,2048]{1,0:T(8,128)(2,1)S(1)}, bf16[8,2048]{1,0:T(8,128)(2,1)}, u32[]{:S(2)}) copy-start(bf16[8,2048]{1,0:T(8,128)(2,1)} %param.2) | copy-start | bytes 98308
  2.6 7.2 %collective-permute-start.2 = (bf16[16,2048]{1,0:T(8,128)(2,1)S(1)}, bf16[16,2048]{1,0:T(8,128)(2,1)S(1)}, u32[]{:S(2)}, u32[]{:S(2)}) collective-permute-start(bf16[16,2048]{1,0:T(8,128)(2,1)S(1)} %maximum_select_fusion), channel_id=1, source_target_pairs={{0,6},{1,25},{2,4},{3,27},{4,2},{5,29},{6,0},{7,31},{8,14},{9,17},... | collective-permute-start | bytes 196616 | tf_op jit(solution)/shard_map/ppermute | solution.py:76
  7.4 5.2 %collective-permute-start.3 = (bf16[16,2048]{1,0:T(8,128)(2,1)S(1)}, bf16[16,2048]{1,0:T(8,128)(2,1)S(1)}, u32[]{:S(2)}, u32[]{:S(2)}) collective-permute-start(bf16[16,2048]{1,0:T(8,128)(2,1)S(1)} %maximum_select_fusion), channel_id=1, source_target_pairs={{0,4},{1,17},{2,6},{3,19},{4,0},{5,21},{6,2},{7,23},{8,12},{9,25},... | collective-permute-start | bytes 196616 | tf_op jit(solution)/shard_map/ppermute | solution.py:76
  7.4 5.2 %collective-permute-start.4 = (bf16[16,2048]{1,0:T(8,128)(2,1)S(1)}, bf16[16,2048]{1,0:T(8,128)(2,1)S(1)}, u32[]{:S(2)}, u32[]{:S(2)}) collective-permute-start(bf16[16,2048]{1,0:T(8,128)(2,1)S(1)} %maximum_select_fusion), channel_id=1, source_target_pairs={{0,2},{1,9},{2,0},{3,11},{4,6},{5,13},{6,4},{7,15},{8,10},{9,1},{1... | collective-permute-start | bytes 196616 | tf_op jit(solution)/shard_map/ppermute | solution.py:76
  12.7 1.6 %collective-permute-start.5 = (bf16[64,2048]{1,0:T(8,128)(2,1)S(1)}, bf16[64,2048]{1,0:T(8,128)(2,1)S(1)}, u32[]{:S(2)}, u32[]{:S(2)}) collective-permute-start(bf16[64,2048]{1,0:T(8,128)(2,1)S(1)} %get-tuple-element.33), channel_id=1, source_target_pairs={{0,1},{1,0},{2,3},{3,2},{4,5},{5,4},{6,7},{7,6},{8,9},{9,8},{10,11... | collective-permute-start | bytes 786440 | tf_op jit(solution)/shard_map/ppermute | solution.py:67
  15.3 6.6 %collective-permute-start.6 = (bf16[64,768]{1,0:T(8,128)(2,1)S(1)}, bf16[64,768]{1,0:T(8,128)(2,1)S(1)}, u32[]{:S(2)}, u32[]{:S(2)}) collective-permute-start(bf16[64,768]{1,0:T(8,128)(2,1)S(1)} %fusion.15), channel_id=1, source_target_pairs={{0,6},{1,25},{2,4},{3,27},{4,2},{5,29},{6,0},{7,31},{8,14},{9,17},... | collective-permute-start | bytes 294920 | tf_op jit(solution)/shard_map/ppermute | solution.py:86
  17.2 4.7 %collective-permute-start.7 = (bf16[64,768]{1,0:T(8,128)(2,1)S(1)}, bf16[64,768]{1,0:T(8,128)(2,1)S(1)}, u32[]{:S(2)}, u32[]{:S(2)}) collective-permute-start(bf16[64,768]{1,0:T(8,128)(2,1)S(1)} %get-tuple-element.75), channel_id=1, source_target_pairs={{0,8},{1,3},{2,10},{3,1},{4,12},{5,7},{6,14},{7,5},{8,0},{9,11},{1... | collective-permute-start | bytes 294920 | tf_op jit(solution)/shard_map/ppermute | solution.py:86
  18.8 4.6 %collective-permute-start.8 = (bf16[64,768]{1,0:T(8,128)(2,1)S(1)}, bf16[64,768]{1,0:T(8,128)(2,1)S(1)}, u32[]{:S(2)}, u32[]{:S(2)}) collective-permute-start(bf16[64,768]{1,0:T(8,128)(2,1)S(1)} %get-tuple-element.76), channel_id=1, source_target_pairs={{0,16},{1,5},{2,18},{3,7},{4,20},{5,1},{6,22},{7,3},{8,24},{9,13},... | collective-permute-start | bytes 294920 | tf_op jit(solution)/shard_map/ppermute | solution.py:86
  21.9 4.3 %collective-permute-start.12 = (bf16[64,640]{1,0:T(8,128)(2,1)S(1)}, bf16[64,640]{1,0:T(8,128)(2,1)S(1)}, u32[]{:S(2)}, u32[]{:S(2)}) collective-permute-start(bf16[64,640]{1,0:T(8,128)(2,1)S(1)} %slice.369), channel_id=1, source_target_pairs={{0,1},{1,0},{2,3},{3,2},{4,5},{5,4},{6,7},{7,6},{8,9},{9,8},{10,11... | collective-permute-start | bytes 245768 | tf_op jit(solution)/shard_map/ppermute | solution.py:67
  23.5 1.2 %collective-permute-start.9 = (f32[8,128]{1,0:T(8,128)S(1)}, f32[8,128]{1,0:T(8,128)S(1)}, u32[]{:S(2)}, u32[]{:S(2)}) collective-permute-start(f32[8,128]{1,0:T(8,128)S(1)} %select_select_fusion), channel_id=1, source_target_pairs={{0,1},{1,0},{2,3},{3,2},{4,5},{5,4},{6,7},{7,6},{8,9},{9,8},{10,11... | collective-permute-start | bytes 12296 | tf_op jit(solution)/shard_map/ppermute | solution.py:67
  23.9 2.3 %collective-permute-start.11 = (bf16[64,768]{1,0:T(8,128)(2,1)S(1)}, bf16[64,768]{1,0:T(8,128)(2,1)S(1)}, u32[]{:S(2)}, u32[]{:S(2)}) collective-permute-start(bf16[64,768]{1,0:T(8,128)(2,1)S(1)} %pad_maximum_fusion.10), channel_id=1, source_target_pairs={{0,1},{1,0},{2,3},{3,2},{4,5},{5,4},{6,7},{7,6},{8,9},{9,8},{10,11... | collective-permute-start | bytes 294920 | tf_op jit(solution)/shard_map/ppermute | solution.py:67
  24.7 4.6 %collective-permute-start.10 = (f32[8,128]{1,0:T(8,128)S(1)}, f32[8,128]{1,0:T(8,128)S(1)}, u32[]{:S(2)}, u32[]{:S(2)}) collective-permute-start(f32[8,128]{1,0:T(8,128)S(1)} %pad_maximum_fusion.14), channel_id=1, source_target_pairs={{18,0},{24,1},{6,30},{12,31},{13,8},{25,9},{4,22},{14,23},{16,2},{... | collective-permute-start | bytes 12296 | tf_op jit(solution)/shard_map/ppermute | solution.py:178
  29.3 1.2 %collective-permute-start.13 = (f32[8,128]{1,0:T(8,128)S(1)}, f32[8,128]{1,0:T(8,128)S(1)}, u32[]{:S(2)}, u32[]{:S(2)}) collective-permute-start(f32[8,128]{1,0:T(8,128)S(1)} %pad_maximum_fusion.15), channel_id=1, source_target_pairs={{0,1},{1,0},{2,3},{3,2},{4,5},{5,4},{6,7},{7,6},{8,9},{9,8},{10,11... | collective-permute-start | bytes 12296 | tf_op jit(solution)/shard_map/ppermute | solution.py:67

commit v8 on v6

--- a/solution.py
+++ b/solution.py
@@ -193,7 +193,10 @@
         is_a, jnp.concatenate([view_a, got_a], 0), jnp.concatenate([got_b, view_b], 1)
     )
 
-    pieces = {step: flip(own, side, step) for step in range(1, side)}
+    pieces, late = {}, own
+    for step in range(1, side):
+        pieces[step] = flip(late, side, step)
+        late = jnp.where(row < (step + 1) * side, late, 0)
     pieces = [own] + [pieces[step] for step in range(1, side)]
     mine = jnp.concatenate(in_order(pieces, jnp.where(is_a, z, row)), 0)
     other = sibling(mine, n_col)

time: 32.4 us -> 31 us (0.957)
  waiting for transfers between devices: 15.8 us -> 13.8 us
  starting transfers between devices: 11.2 us -> 11.8 us
    ppermute x3, waiting for transfers between devices: 6.05 us -> 4.52 us  [flip(): return lax.ppermute(value, BOTH, pairs)]
    ppermute x1, starting transfers between devices: 0.96 us -> 1.49 us  [hear(): return lax.ppermute(known, BOTH, pairs)]
    ppermute x1, waiting for transfers between devices: 1.52 us -> 1.03 us  [hear(): return lax.ppermute(known, BOTH, pairs)]
where the time goes in v8:
time: 31 us; the launch traced here: 30.9 us
  waiting for transfers between devices  13.8 us (45%)
  starting transfers between devices  11.8 us (38%)
  other arithmetic  3.54 us (11%)
  between operations  0.95 us (3%)
  matrix products  0.67 us (2%)
    ppermute x3, starting transfers between devices, flip(): return lax.ppermute(value, BOTH, pairs)  5.47 us
    ppermute x3, waiting for transfers between devices, flip(): return lax.ppermute(value, BOTH, pairs)  4.52 us
    ppermute x6, waiting for transfers between devices, sibling(): return lax.ppermute(value, 'col', [(c, c ^ 1) for c in range(n_col)])  4.15 us
    ppermute x3, waiting for transfers between devices, across(): return lax.ppermute(value, BOTH, pairs)  4.1 us
    ppermute x3, starting transfers between devices, across(): return lax.ppermute(value, BOTH, pairs)  3.61 us
    ppermute x1, starting transfers between devices, hear(): return lax.ppermute(known, BOTH, pairs)  1.49 us
    convert_element_type x2, other arithmetic, gradient(): (scaled * (term - first - normed * second + extra.astype(jnp.float32))).a...  1.32 us
    ppermute x6, starting transfers between devices, sibling(): return lax.ppermute(value, 'col', [(c, c ^ 1) for c in range(n_col)])  1.25 us
  transfers between devices with their start and end apart: 13, of which 11 were waited for; matrix products, arithmetic and copies ran while one was open for 8% of the time, Pallas kernels for 0%

profile of v8, /device:TPU:0, one launch (start us, length us, event | category | flops | bytes accessed | tf_op | source)
XLA Modules:
  0.0 30.9 jit_solution(464652236097329661)
XLA Ops:
  0.6 0.5 %collective-permute-start = (bf16[8,2048]{1,0:T(8,128)(2,1)}, bf16[8,2048]{1,0:T(8,128)(2,1)S(1)}, u32[]{:S(2)}, u32[]{:S(2)}) collective-permute-start(bf16[8,2048]{1,0:T(8,128)(2,1)} %param.2), channel_id=1, source_target_pairs={{0,1},{1,0},{2,3},{3,2},{4,5},{5,4},{6,7},{7,6},{8,9},{9,8},{10,11... | collective-permute-start | bytes 98312 | tf_op jit(solution)/shard_map/ppermute | solution.py:67
  1.3 1.0 %collective-permute-done = bf16[8,2048]{1,0:T(8,128)(2,1)S(1)} collective-permute-done((bf16[8,2048]{1,0:T(8,128)(2,1)}, bf16[8,2048]{1,0:T(8,128)(2,1)S(1)}, u32[]{:S(2)}, u32[]{:S(2)}) %collective-permute-start) | collective-permute-done | bytes 32800 | tf_op jit(solution)/shard_map/ppermute | solution.py:67
  2.2 0.3 %collective-permute-done.1 = bf16[16,1024]{1,0:T(8,128)(2,1)S(1)} collective-permute-done((bf16[16,1024]{1,0:T(8,128)(2,1)}, bf16[16,1024]{1,0:T(8,128)(2,1)S(1)}, u32[]{:S(2)}, u32[]{:S(2)}) %collective-permute-start.1) | collective-permute-done | bytes 32800 | tf_op jit(solution)/shard_map/ppermute | solution.py:67
  2.6 4.8 %collective-permute-start.2 = (bf16[16,2048]{1,0:T(8,128)(2,1)S(1)}, bf16[16,2048]{1,0:T(8,128)(2,1)S(1)}, u32[]{:S(2)}, u32[]{:S(2)}) collective-permute-start(bf16[16,2048]{1,0:T(8,128)(2,1)S(1)} %get-tuple-element.31), channel_id=1, source_target_pairs={{0,6},{1,25},{2,4},{3,27},{4,2},{5,29},{6,0},{7,31},{8,14},{9,17},... | collective-permute-start | bytes 196616 | tf_op jit(solution)/shard_map/ppermute | solution.py:76
  7.4 0.6 %collective-permute-start.4 = (bf16[16,2048]{1,0:T(8,128)(2,1)S(1)}, bf16[16,2048]{1,0:T(8,128)(2,1)S(1)}, u32[]{:S(2)}, u32[]{:S(2)}) collective-permute-start(bf16[16,2048]{1,0:T(8,128)(2,1)S(1)} %get-tuple-element.33), channel_id=1, source_target_pairs={{0,2},{1,9},{2,0},{3,11},{4,6},{5,13},{6,4},{7,15},{8,10},{9,1},{1... | collective-permute-start | bytes 196616 | tf_op jit(solution)/shard_map/ppermute | solution.py:76
  8.1 1.7 %collective-permute-done.2 = bf16[16,2048]{1,0:T(8,128)(2,1)S(1)} collective-permute-done((bf16[16,2048]{1,0:T(8,128)(2,1)S(1)}, bf16[16,2048]{1,0:T(8,128)(2,1)S(1)}, u32[]{:S(2)}, u32[]{:S(2)}) %collective-permute-start.2) | collective-permute-done | bytes 65568 | tf_op jit(solution)/shard_map/ppermute | solution.py:76
  9.8 2.8 %collective-permute-done.3 = bf16[16,2048]{1,0:T(8,128)(2,1)S(1)} collective-permute-done((bf16[16,2048]{1,0:T(8,128)(2,1)S(1)}, bf16[16,2048]{1,0:T(8,128)(2,1)S(1)}, u32[]{:S(2)}, u32[]{:S(2)}) %collective-permute-start.3) | collective-permute-done | bytes 65568 | tf_op jit(solution)/shard_map/ppermute | solution.py:76
  12.8 0.1 fusion.7
  13.0 0.2 fusion.41
  13.2 1.1 %collective-permute-done.5 = bf16[64,2048]{1,0:T(8,128)(2,1)S(1)} collective-permute-done((bf16[64,2048]{1,0:T(8,128)(2,1)S(1)}, bf16[64,2048]{1,0:T(8,128)(2,1)S(1)}, u32[]{:S(2)}, u32[]{:S(2)}) %collective-permute-start.5) | collective-permute-done | bytes 262176 | tf_op jit(solution)/shard_map/ppermute | solution.py:67
  14.4 0.1 fusion.4
  14.5 0.1 broadcast_select_fusion
  14.6 0.1 convert_reduce_fusion
  14.8 0.1 fusion.12
  15.0 0.1 fusion.17
  15.1 2.5 %collective-permute-start.8 = (bf16[64,768]{1,0:T(8,128)(2,1)S(1)}, bf16[64,768]{1,0:T(8,128)(2,1)S(1)}, u32[]{:S(2)}, u32[]{:S(2)}) collective-permute-start(bf16[64,768]{1,0:T(8,128)(2,1)S(1)} %fusion.17), channel_id=1, source_target_pairs={{0,24},{1,7},{2,26},{3,5},{4,28},{5,3},{6,30},{7,1},{8,16},{9,15},... | collective-permute-start | bytes 294920 | tf_op jit(solution)/shard_map/ppermute | solution.py:85
  17.7 0.6 %collective-permute-start.6 = (bf16[64,768]{1,0:T(8,128)(2,1)S(1)}, bf16[64,768]{1,0:T(8,128)(2,1)S(1)}, u32[]{:S(2)}, u32[]{:S(2)}) collective-permute-start(bf16[64,768]{1,0:T(8,128)(2,1)S(1)} %get-tuple-element.66), channel_id=1, source_target_pairs={{0,8},{1,3},{2,10},{3,1},{4,12},{5,7},{6,14},{7,5},{8,0},{9,11},{1... | collective-permute-start | bytes 294920 | tf_op jit(solution)/shard_map/ppermute | solution.py:85
  18.3 0.5 %collective-permute-start.7 = (bf16[64,768]{1,0:T(8,128)(2,1)S(1)}, bf16[64,768]{1,0:T(8,128)(2,1)S(1)}, u32[]{:S(2)}, u32[]{:S(2)}) collective-permute-start(bf16[64,768]{1,0:T(8,128)(2,1)S(1)} %get-tuple-element.67), channel_id=1, source_target_pairs={{0,16},{1,5},{2,18},{3,7},{4,20},{5,1},{6,22},{7,3},{8,24},{9,13},... | collective-permute-start | bytes 294920 | tf_op jit(solution)/shard_map/ppermute | solution.py:85
  18.8 1.9 %collective-permute-done.8 = bf16[64,768]{1,0:T(8,128)(2,1)S(1)} collective-permute-done((bf16[64,768]{1,0:T(8,128)(2,1)S(1)}, bf16[64,768]{1,0:T(8,128)(2,1)S(1)}, u32[]{:S(2)}, u32[]{:S(2)}) %collective-permute-start.8) | collective-permute-done | bytes 98336 | tf_op jit(solution)/shard_map/ppermute | solution.py:85
  20.7 1.7 %collective-permute-done.6 = bf16[64,768]{1,0:T(8,128)(2,1)S(1)} collective-permute-done((bf16[64,768]{1,0:T(8,128)(2,1)S(1)}, bf16[64,768]{1,0:T(8,128)(2,1)S(1)}, u32[]{:S(2)}, u32[]{:S(2)}) %collective-permute-start.6) | collective-permute-done | bytes 98336 | tf_op jit(solution)/shard_map/ppermute | solution.py:85
  22.4 0.5 %collective-permute-done.7 = bf16[64,768]{1,0:T(8,128)(2,1)S(1)} collective-permute-done((bf16[64,768]{1,0:T(8,128)(2,1)S(1)}, bf16[64,768]{1,0:T(8,128)(2,1)S(1)}, u32[]{:S(2)}, u32[]{:S(2)}) %collective-permute-start.7) | collective-permute-done | bytes 98336 | tf_op jit(solution)/shard_map/ppermute | solution.py:85
  23.3 0.5 %collective-permute-start.11 = (bf16[64,640]{1,0:T(8,128)(2,1)S(1)}, bf16[64,640]{1,0:T(8,128)(2,1)S(1)}, u32[]{:S(2)}, u32[]{:S(2)}) collective-permute-start(bf16[64,640]{1,0:T(8,128)(2,1)S(1)} %pad_maximum_fusion.14), channel_id=1, source_target_pairs={{0,1},{1,0},{2,3},{3,2},{4,5},{5,4},{6,7},{7,6},{8,9},{9,8},{10,11... | collective-permute-start | bytes 245768 | tf_op jit(solution)/shard_map/ppermute | solution.py:67
  23.8 0.6 %collective-permute-done.9 = f32[8,128]{1,0:T(8,128)S(1)} collective-permute-done((f32[8,128]{1,0:T(8,128)S(1)}, f32[8,128]{1,0:T(8,128)S(1)}, u32[]{:S(2)}, u32[]{:S(2)}) %collective-permute-start.9) | collective-permute-done | bytes 4128 | tf_op jit(solution)/shard_map/ppermute | solution.py:67
  24.4 1.5 %collective-permute-start.10 = (f32[8,128]{1,0:T(8,128)S(1)}, f32[8,128]{1,0:T(8,128)S(1)}, u32[]{:S(2)}, u32[]{:S(2)}) collective-permute-start(f32[8,128]{1,0:T(8,128)S(1)} %pad_maximum_fusion.16), channel_id=1, source_target_pairs={{18,0},{24,1},{6,30},{12,31},{13,8},{25,9},{4,22},{14,23},{16,2},{... | collective-permute-start | bytes 12296 | tf_op jit(solution)/shard_map/ppermute | solution.py:177
  26.0 0.2 fusion.35
  26.2 0.3 fusion.34
  26.5 0.7 %multiply_convert_fusion.1 = bf16[8,2048]{1,0:T(8,128)(2,1)} fusion(f32[64,2048]{1,0:T(8,128)S(1)} %get-tuple-element.80, s32[]{:T(128)S(6)} %select_n.220, s32[]{:T(128)S(6)} %select_n.221, bf16[64,2048]{1,0:T(8,128)(2,1)S(1)} %get-tuple-element.27, bf16[16,2048]{1,0:T(8,128)(2,1)S(1)} %pad_maximum_fusion.15, f32[2048]{0:T(1024)S(1)} %broadcast_multiply_fusion, ...), kind=kLoop, calls=%fused_computation.56 | loop fusion | flops 196608 | bytes 450569 | tf_op jit(solution)/shard_map/convert_element_type | solution.py:271
  27.2 0.7 %multiply_convert_fusion = bf16[16,1024]{1,0:T(8,128)(2,1)} fusion(f32[64,1024]{1,0:T(8,128)S(1)} %get-tuple-element.81, s32[]{:T(128)S(6)} %select_n.205, s32[]{:T(128)S(6)} %select_n.229, bf16[64,1024]{1,0:T(8,128)(2,1)S(1)} %slice_select_fusion, bf16[16,512]{1,0:T(8,128)(2,1)S(1)} %get-tuple-element.60, bf16[16,512]{1,0:T(8,128)(2,1)S(1)} %get-tuple-element.61, ...), kind=kLoop, calls=%fused_computation.55 | loop fusion | flops 327680 | bytes 307209 | tf_op jit(solution)/shard_map/convert_element_type | solution.py:271
  27.9 0.1 fusion.26
  28.0 1.0 %collective-permute-done.10 = f32[8,128]{1,0:T(8,128)S(1)} collective-permute-done((f32[8,128]{1,0:T(8,128)S(1)}, f32[8,128]{1,0:T(8,128)S(1)}, u32[]{:S(2)}, u32[]{:S(2)}) %collective-permute-start.10) | collective-permute-done | bytes 4128 | tf_op jit(solution)/shard_map/ppermute | solution.py:177
  29.1 1.2 %collective-permute-done.12 = f32[8,128]{1,0:T(8,128)S(1)} collective-permute-done((f32[8,128]{1,0:T(8,128)S(1)}, f32[8,128]{1,0:T(8,128)S(1)}, u32[]{:S(2)}, u32[]{:S(2)}) %collective-permute-start.12) | collective-permute-done | bytes 4128 | tf_op jit(solution)/shard_map/ppermute | solution.py:67
  30.3 0.6 %add_reduce_fusion = f32[]{:T(128)} fusion(f32[128]{0:T(128)S(1)} %pad.4, f32[128]{0:T(128)S(1)} %select_reduce_fusion), kind=kLoop, calls=%fused_computation.119 | loop fusion | flops 383 | bytes 1028 | tf_op jit(solution)/shard_map/reduce_sum | solution.py:287
  (52 shorter events, 1.2 us)
Async XLA Ops:
  0.6 1.6 %collective-permute-start = (bf16[8,2048]{1,0:T(8,128)(2,1)}, bf16[8,2048]{1,0:T(8,128)(2,1)S(1)}, u32[]{:S(2)}, u32[]{:S(2)}) collective-permute-start(bf16[8,2048]{1,0:T(8,128)(2,1)} %param.2), channel_id=1, source_target_pairs={{0,1},{1,0},{2,3},{3,2},{4,5},{5,4},{6,7},{7,6},{8,9},{9,8},{10,11... | collective-permute-start | bytes 98312 | tf_op jit(solution)/shard_map/ppermute | solution.py:67
  1.1 1.4 %collective-permute-start.1 = (bf16[16,1024]{1,0:T(8,128)(2,1)}, bf16[16,1024]{1,0:T(8,128)(2,1)S(1)}, u32[]{:S(2)}, u32[]{:S(2)}) collective-permute-start(bf16[16,1024]{1,0:T(8,128)(2,1)} %param.3), channel_id=1, source_target_pairs={{0,1},{1,0},{2,3},{3,2},{4,5},{5,4},{6,7},{7,6},{8,9},{9,8},{10,11... | collective-permute-start | bytes 98312 | tf_op jit(solution)/shard_map/ppermute | solution.py:67
  1.2 1.3 %copy-start.1 = (bf16[8,2048]{1,0:T(8,128)(2,1)S(1)}, bf16[8,2048]{1,0:T(8,128)(2,1)}, u32[]{:S(2)}) copy-start(bf16[8,2048]{1,0:T(8,128)(2,1)} %param.2) | copy-start | bytes 98308
  1.2 1.3 %copy-start = (bf16[16,1024]{1,0:T(8,128)(2,1)S(1)}, bf16[16,1024]{1,0:T(8,128)(2,1)}, u32[]{:S(2)}) copy-start(bf16[16,1024]{1,0:T(8,128)(2,1)} %param.3) | copy-start | bytes 98308
  2.6 7.2 %collective-permute-start.2 = (bf16[16,2048]{1,0:T(8,128)(2,1)S(1)}, bf16[16,2048]{1,0:T(8,128)(2,1)S(1)}, u32[]{:S(2)}, u32[]{:S(2)}) collective-permute-start(bf16[16,2048]{1,0:T(8,128)(2,1)S(1)} %get-tuple-element.31), channel_id=1, source_target_pairs={{0,6},{1,25},{2,4},{3,27},{4,2},{5,29},{6,0},{7,31},{8,14},{9,17},... | collective-permute-start | bytes 196616 | tf_op jit(solution)/shard_map/ppermute | solution.py:76
  7.4 5.2 %collective-permute-start.3 = (bf16[16,2048]{1,0:T(8,128)(2,1)S(1)}, bf16[16,2048]{1,0:T(8,128)(2,1)S(1)}, u32[]{:S(2)}, u32[]{:S(2)}) collective-permute-start(bf16[16,2048]{1,0:T(8,128)(2,1)S(1)} %get-tuple-element.32), channel_id=1, source_target_pairs={{0,4},{1,17},{2,6},{3,19},{4,0},{5,21},{6,2},{7,23},{8,12},{9,25},... | collective-permute-start | bytes 196616 | tf_op jit(solution)/shard_map/ppermute | solution.py:76
  7.4 5.2 %collective-permute-start.4 = (bf16[16,2048]{1,0:T(8,128)(2,1)S(1)}, bf16[16,2048]{1,0:T(8,128)(2,1)S(1)}, u32[]{:S(2)}, u32[]{:S(2)}) collective-permute-start(bf16[16,2048]{1,0:T(8,128)(2,1)S(1)} %get-tuple-element.33), channel_id=1, source_target_pairs={{0,2},{1,9},{2,0},{3,11},{4,6},{5,13},{6,4},{7,15},{8,10},{9,1},{1... | collective-permute-start | bytes 196616 | tf_op jit(solution)/shard_map/ppermute | solution.py:76
  12.7 1.6 %collective-permute-start.5 = (bf16[64,2048]{1,0:T(8,128)(2,1)S(1)}, bf16[64,2048]{1,0:T(8,128)(2,1)S(1)}, u32[]{:S(2)}, u32[]{:S(2)}) collective-permute-start(bf16[64,2048]{1,0:T(8,128)(2,1)S(1)} %get-tuple-element.30), channel_id=1, source_target_pairs={{0,1},{1,0},{2,3},{3,2},{4,5},{5,4},{6,7},{7,6},{8,9},{9,8},{10,11... | collective-permute-start | bytes 786440 | tf_op jit(solution)/shard_map/ppermute | solution.py:67
  15.1 5.6 %collective-permute-start.8 = (bf16[64,768]{1,0:T(8,128)(2,1)S(1)}, bf16[64,768]{1,0:T(8,128)(2,1)S(1)}, u32[]{:S(2)}, u32[]{:S(2)}) collective-permute-start(bf16[64,768]{1,0:T(8,128)(2,1)S(1)} %fusion.17), channel_id=1, source_target_pairs={{0,24},{1,7},{2,26},{3,5},{4,28},{5,3},{6,30},{7,1},{8,16},{9,15},... | collective-permute-start | bytes 294920 | tf_op jit(solution)/shard_map/ppermute | solution.py:85
  17.7 4.7 %collective-permute-start.6 = (bf16[64,768]{1,0:T(8,128)(2,1)S(1)}, bf16[64,768]{1,0:T(8,128)(2,1)S(1)}, u32[]{:S(2)}, u32[]{:S(2)}) collective-permute-start(bf16[64,768]{1,0:T(8,128)(2,1)S(1)} %get-tuple-element.66), channel_id=1, source_target_pairs={{0,8},{1,3},{2,10},{3,1},{4,12},{5,7},{6,14},{7,5},{8,0},{9,11},{1... | collective-permute-start | bytes 294920 | tf_op jit(solution)/shard_map/ppermute | solution.py:85
  18.3 4.6 %collective-permute-start.7 = (bf16[64,768]{1,0:T(8,128)(2,1)S(1)}, bf16[64,768]{1,0:T(8,128)(2,1)S(1)}, u32[]{:S(2)}, u32[]{:S(2)}) collective-permute-start(bf16[64,768]{1,0:T(8,128)(2,1)S(1)} %get-tuple-element.67), channel_id=1, source_target_pairs={{0,16},{1,5},{2,18},{3,7},{4,20},{5,1},{6,22},{7,3},{8,24},{9,13},... | collective-permute-start | bytes 294920 | tf_op jit(solution)/shard_map/ppermute | solution.py:85
  23.2 1.2 %collective-permute-start.9 = (f32[8,128]{1,0:T(8,128)S(1)}, f32[8,128]{1,0:T(8,128)S(1)}, u32[]{:S(2)}, u32[]{:S(2)}) collective-permute-start(f32[8,128]{1,0:T(8,128)S(1)} %select_select_fusion), channel_id=1, source_target_pairs={{0,1},{1,0},{2,3},{3,2},{4,5},{5,4},{6,7},{7,6},{8,9},{9,8},{10,11... | collective-permute-start | bytes 12296 | tf_op jit(solution)/shard_map/ppermute | solution.py:67
  23.3 2.6 %collective-permute-start.11 = (bf16[64,640]{1,0:T(8,128)(2,1)S(1)}, bf16[64,640]{1,0:T(8,128)(2,1)S(1)}, u32[]{:S(2)}, u32[]{:S(2)}) collective-permute-start(bf16[64,640]{1,0:T(8,128)(2,1)S(1)} %pad_maximum_fusion.14), channel_id=1, source_target_pairs={{0,1},{1,0},{2,3},{3,2},{4,5},{5,4},{6,7},{7,6},{8,9},{9,8},{10,11... | collective-permute-start | bytes 245768 | tf_op jit(solution)/shard_map/ppermute | solution.py:67
  24.4 4.6 %collective-permute-start.10 = (f32[8,128]{1,0:T(8,128)S(1)}, f32[8,128]{1,0:T(8,128)S(1)}, u32[]{:S(2)}, u32[]{:S(2)}) collective-permute-start(f32[8,128]{1,0:T(8,128)S(1)} %pad_maximum_fusion.16), channel_id=1, source_target_pairs={{18,0},{24,1},{6,30},{12,31},{13,8},{25,9},{4,22},{14,23},{16,2},{... | collective-permute-start | bytes 12296 | tf_op jit(solution)/shard_map/ppermute | solution.py:177
  29.0 1.2 %collective-permute-start.12 = (f32[8,128]{1,0:T(8,128)S(1)}, f32[8,128]{1,0:T(8,128)S(1)}, u32[]{:S(2)}, u32[]{:S(2)}) collective-permute-start(f32[8,128]{1,0:T(8,128)S(1)} %pad_maximum_fusion.17), channel_id=1, source_target_pairs={{0,1},{1,0},{2,3},{3,2},{4,5},{5,4},{6,7},{7,6},{8,9},{9,8},{10,11... | collective-permute-start | bytes 12296 | tf_op jit(solution)/shard_map/ppermute | solution.py:67

commit v9 on v8

--- a/solution.py
+++ b/solution.py
@@ -136,12 +136,15 @@
         return None
     for limit in range(1, 3 * side):
         choices = {
-            p: [
-                (q, t)
-                for i, q in enumerate(chips)
-                for t in chips[i + 1 :]
-                if max(hops(p, q), hops(p, t)) <= limit and len({*p, *q, *t}) == side
-            ]
+            p: sorted(
+                (
+                    (q, t)
+                    for i, q in enumerate(chips)
+                    for t in chips[i + 1 :]
+                    if max(hops(p, q), hops(p, t)) <= limit and len({*p, *q, *t}) == side
+                ),
+                key=lambda pair, p=p: hops(p, pair[0]) + hops(p, pair[1]),
+            )
             for p in chips
         }
         if all(choices.values()):
@@ -171,8 +174,8 @@
     used, pairs = {}, []
     for (row, z), pair in plan.items():
         for core, chip in enumerate(pair):
-            from_core = used.get(chip, 0)
-            used[chip] = from_core + 1
+            from_core = used.get(chip, 1)
+            used[chip] = from_core - 1
             pairs.append(((chip[0] * side + chip[1]) * 2 + from_core, (row * side + z) * 2 + core))
     return lax.ppermute(known, BOTH, pairs)
 

time: 31 us -> 30.4 us (0.981)
  starting transfers between devices: 11.8 us -> 11.4 us
    ppermute x1, starting transfers between devices: 1.49 us -> 1.09 us  [hear(): return lax.ppermute(known, BOTH, pairs)]
where the time goes in v9:
time: 30.4 us; the launch traced here: 30.3 us
  waiting for transfers between devices  13.6 us (45%)
  starting transfers between devices  11.4 us (38%)
  other arithmetic  3.54 us (12%)
  between operations  0.95 us (3%)
  matrix products  0.67 us (2%)
    ppermute x3, starting transfers between devices, flip(): return lax.ppermute(value, BOTH, pairs)  5.47 us
    ppermute x3, waiting for transfers between devices, flip(): return lax.ppermute(value, BOTH, pairs)  4.52 us
    ppermute x6, waiting for transfers between devices, sibling(): return lax.ppermute(value, 'col', [(c, c ^ 1) for c in range(n_col)])  4.15 us
    ppermute x3, waiting for transfers between devices, across(): return lax.ppermute(value, BOTH, pairs)  4.1 us
    ppermute x3, starting transfers between devices, across(): return lax.ppermute(value, BOTH, pairs)  3.61 us
    convert_element_type x2, other arithmetic, gradient(): (scaled * (term - first - normed * second + extra.astype(jnp.float32))).a...  1.32 us
    ppermute x6, starting transfers between devices, sibling(): return lax.ppermute(value, 'col', [(c, c ^ 1) for c in range(n_col)])  1.25 us
    ppermute x1, starting transfers between devices, hear(): return lax.ppermute(known, BOTH, pairs)  1.09 us
  transfers between devices with their start and end apart: 13, of which 11 were waited for; matrix products, arithmetic and copies ran while one was open for 8% of the time, Pallas kernels for 0%

profile of v9, /device:TPU:0, one launch (start us, length us, event | category | flops | bytes accessed | tf_op | source)
XLA Modules:
  0.0 30.3 jit_solution(15595521312784619087)
XLA Ops:
  0.6 0.5 %collective-permute-start = (bf16[8,2048]{1,0:T(8,128)(2,1)}, bf16[8,2048]{1,0:T(8,128)(2,1)S(1)}, u32[]{:S(2)}, u32[]{:S(2)}) collective-permute-start(bf16[8,2048]{1,0:T(8,128)(2,1)} %param.2), channel_id=1, source_target_pairs={{0,1},{1,0},{2,3},{3,2},{4,5},{5,4},{6,7},{7,6},{8,9},{9,8},{10,11... | collective-permute-start | bytes 98312 | tf_op jit(solution)/shard_map/ppermute | solution.py:67
  1.3 1.0 %collective-permute-done = bf16[8,2048]{1,0:T(8,128)(2,1)S(1)} collective-permute-done((bf16[8,2048]{1,0:T(8,128)(2,1)}, bf16[8,2048]{1,0:T(8,128)(2,1)S(1)}, u32[]{:S(2)}, u32[]{:S(2)}) %collective-permute-start) | collective-permute-done | bytes 32800 | tf_op jit(solution)/shard_map/ppermute | solution.py:67
  2.2 0.3 %collective-permute-done.1 = bf16[16,1024]{1,0:T(8,128)(2,1)S(1)} collective-permute-done((bf16[16,1024]{1,0:T(8,128)(2,1)}, bf16[16,1024]{1,0:T(8,128)(2,1)S(1)}, u32[]{:S(2)}, u32[]{:S(2)}) %collective-permute-start.1) | collective-permute-done | bytes 32800 | tf_op jit(solution)/shard_map/ppermute | solution.py:67
  2.6 4.8 %collective-permute-start.2 = (bf16[16,2048]{1,0:T(8,128)(2,1)S(1)}, bf16[16,2048]{1,0:T(8,128)(2,1)S(1)}, u32[]{:S(2)}, u32[]{:S(2)}) collective-permute-start(bf16[16,2048]{1,0:T(8,128)(2,1)S(1)} %get-tuple-element.31), channel_id=1, source_target_pairs={{0,6},{1,25},{2,4},{3,27},{4,2},{5,29},{6,0},{7,31},{8,14},{9,17},... | collective-permute-start | bytes 196616 | tf_op jit(solution)/shard_map/ppermute | solution.py:76
  7.4 0.6 %collective-permute-start.4 = (bf16[16,2048]{1,0:T(8,128)(2,1)S(1)}, bf16[16,2048]{1,0:T(8,128)(2,1)S(1)}, u32[]{:S(2)}, u32[]{:S(2)}) collective-permute-start(bf16[16,2048]{1,0:T(8,128)(2,1)S(1)} %get-tuple-element.33), channel_id=1, source_target_pairs={{0,2},{1,9},{2,0},{3,11},{4,6},{5,13},{6,4},{7,15},{8,10},{9,1},{1... | collective-permute-start | bytes 196616 | tf_op jit(solution)/shard_map/ppermute | solution.py:76
  8.1 1.7 %collective-permute-done.2 = bf16[16,2048]{1,0:T(8,128)(2,1)S(1)} collective-permute-done((bf16[16,2048]{1,0:T(8,128)(2,1)S(1)}, bf16[16,2048]{1,0:T(8,128)(2,1)S(1)}, u32[]{:S(2)}, u32[]{:S(2)}) %collective-permute-start.2) | collective-permute-done | bytes 65568 | tf_op jit(solution)/shard_map/ppermute | solution.py:76
  9.8 2.8 %collective-permute-done.3 = bf16[16,2048]{1,0:T(8,128)(2,1)S(1)} collective-permute-done((bf16[16,2048]{1,0:T(8,128)(2,1)S(1)}, bf16[16,2048]{1,0:T(8,128)(2,1)S(1)}, u32[]{:S(2)}, u32[]{:S(2)}) %collective-permute-start.3) | collective-permute-done | bytes 65568 | tf_op jit(solution)/shard_map/ppermute | solution.py:76
  12.8 0.1 fusion.7
  13.0 0.2 fusion.41
  13.2 1.1 %collective-permute-done.5 = bf16[64,2048]{1,0:T(8,128)(2,1)S(1)} collective-permute-done((bf16[64,2048]{1,0:T(8,128)(2,1)S(1)}, bf16[64,2048]{1,0:T(8,128)(2,1)S(1)}, u32[]{:S(2)}, u32[]{:S(2)}) %collective-permute-start.5) | collective-permute-done | bytes 262176 | tf_op jit(solution)/shard_map/ppermute | solution.py:67
  14.4 0.1 fusion.4
  14.5 0.1 broadcast_select_fusion
  14.6 0.1 convert_reduce_fusion
  14.8 0.1 fusion.12
  15.1 2.5 %collective-permute-start.8 = (bf16[64,768]{1,0:T(8,128)(2,1)S(1)}, bf16[64,768]{1,0:T(8,128)(2,1)S(1)}, u32[]{:S(2)}, u32[]{:S(2)}) collective-permute-start(bf16[64,768]{1,0:T(8,128)(2,1)S(1)} %fusion.17), channel_id=1, source_target_pairs={{0,24},{1,7},{2,26},{3,5},{4,28},{5,3},{6,30},{7,1},{8,16},{9,15},... | collective-permute-start | bytes 294920 | tf_op jit(solution)/shard_map/ppermute | solution.py:85
  17.6 0.1 fusion.15
  17.7 0.6 %collective-permute-start.6 = (bf16[64,768]{1,0:T(8,128)(2,1)S(1)}, bf16[64,768]{1,0:T(8,128)(2,1)S(1)}, u32[]{:S(2)}, u32[]{:S(2)}) collective-permute-start(bf16[64,768]{1,0:T(8,128)(2,1)S(1)} %get-tuple-element.66), channel_id=1, source_target_pairs={{0,8},{1,3},{2,10},{3,1},{4,12},{5,7},{6,14},{7,5},{8,0},{9,11},{1... | collective-permute-start | bytes 294920 | tf_op jit(solution)/shard_map/ppermute | solution.py:85
  18.3 0.5 %collective-permute-start.7 = (bf16[64,768]{1,0:T(8,128)(2,1)S(1)}, bf16[64,768]{1,0:T(8,128)(2,1)S(1)}, u32[]{:S(2)}, u32[]{:S(2)}) collective-permute-start(bf16[64,768]{1,0:T(8,128)(2,1)S(1)} %get-tuple-element.67), channel_id=1, source_target_pairs={{0,16},{1,5},{2,18},{3,7},{4,20},{5,1},{6,22},{7,3},{8,24},{9,13},... | collective-permute-start | bytes 294920 | tf_op jit(solution)/shard_map/ppermute | solution.py:85
  18.8 1.9 %collective-permute-done.8 = bf16[64,768]{1,0:T(8,128)(2,1)S(1)} collective-permute-done((bf16[64,768]{1,0:T(8,128)(2,1)S(1)}, bf16[64,768]{1,0:T(8,128)(2,1)S(1)}, u32[]{:S(2)}, u32[]{:S(2)}) %collective-permute-start.8) | collective-permute-done | bytes 98336 | tf_op jit(solution)/shard_map/ppermute | solution.py:85
  20.7 1.7 %collective-permute-done.6 = bf16[64,768]{1,0:T(8,128)(2,1)S(1)} collective-permute-done((bf16[64,768]{1,0:T(8,128)(2,1)S(1)}, bf16[64,768]{1,0:T(8,128)(2,1)S(1)}, u32[]{:S(2)}, u32[]{:S(2)}) %collective-permute-start.6) | collective-permute-done | bytes 98336 | tf_op jit(solution)/shard_map/ppermute | solution.py:85
  22.4 0.5 %collective-permute-done.7 = bf16[64,768]{1,0:T(8,128)(2,1)S(1)} collective-permute-done((bf16[64,768]{1,0:T(8,128)(2,1)S(1)}, bf16[64,768]{1,0:T(8,128)(2,1)S(1)}, u32[]{:S(2)}, u32[]{:S(2)}) %collective-permute-start.7) | collective-permute-done | bytes 98336 | tf_op jit(solution)/shard_map/ppermute | solution.py:85
  23.3 0.5 %collective-permute-start.11 = (bf16[64,640]{1,0:T(8,128)(2,1)S(1)}, bf16[64,640]{1,0:T(8,128)(2,1)S(1)}, u32[]{:S(2)}, u32[]{:S(2)}) collective-permute-start(bf16[64,640]{1,0:T(8,128)(2,1)S(1)} %pad_maximum_fusion.14), channel_id=1, source_target_pairs={{0,1},{1,0},{2,3},{3,2},{4,5},{5,4},{6,7},{7,6},{8,9},{9,8},{10,11... | collective-permute-start | bytes 245768 | tf_op jit(solution)/shard_map/ppermute | solution.py:67
  23.8 0.6 %collective-permute-done.9 = f32[8,128]{1,0:T(8,128)S(1)} collective-permute-done((f32[8,128]{1,0:T(8,128)S(1)}, f32[8,128]{1,0:T(8,128)S(1)}, u32[]{:S(2)}, u32[]{:S(2)}) %collective-permute-start.9) | collective-permute-done | bytes 4128 | tf_op jit(solution)/shard_map/ppermute | solution.py:67
  24.4 1.1 %collective-permute-start.10 = (f32[8,128]{1,0:T(8,128)S(1)}, f32[8,128]{1,0:T(8,128)S(1)}, u32[]{:S(2)}, u32[]{:S(2)}) collective-permute-start(f32[8,128]{1,0:T(8,128)S(1)} %pad_maximum_fusion.16), channel_id=1, source_target_pairs={{19,0},{25,1},{7,30},{13,31},{12,8},{24,9},{6,22},{15,23},{18,2},{... | collective-permute-start | bytes 12296 | tf_op jit(solution)/shard_map/ppermute | solution.py:180
  25.6 0.2 fusion.35
  25.8 0.3 fusion.34
  26.1 0.7 %multiply_convert_fusion.1 = bf16[8,2048]{1,0:T(8,128)(2,1)} fusion(f32[64,2048]{1,0:T(8,128)S(1)} %get-tuple-element.80, s32[]{:T(128)S(6)} %select_n.220, s32[]{:T(128)S(6)} %select_n.221, bf16[64,2048]{1,0:T(8,128)(2,1)S(1)} %get-tuple-element.27, bf16[16,2048]{1,0:T(8,128)(2,1)S(1)} %pad_maximum_fusion.15, f32[2048]{0:T(1024)S(1)} %broadcast_multiply_fusion, ...), kind=kLoop, calls=%fused_computation.56 | loop fusion | flops 196608 | bytes 450569 | tf_op jit(solution)/shard_map/convert_element_type | solution.py:274
  26.8 0.7 %multiply_convert_fusion = bf16[16,1024]{1,0:T(8,128)(2,1)} fusion(f32[64,1024]{1,0:T(8,128)S(1)} %get-tuple-element.81, s32[]{:T(128)S(6)} %select_n.205, s32[]{:T(128)S(6)} %select_n.229, bf16[64,1024]{1,0:T(8,128)(2,1)S(1)} %slice_select_fusion, bf16[16,512]{1,0:T(8,128)(2,1)S(1)} %get-tuple-element.60, bf16[16,512]{1,0:T(8,128)(2,1)S(1)} %get-tuple-element.61, ...), kind=kLoop, calls=%fused_computation.55 | loop fusion | flops 327680 | bytes 307209 | tf_op jit(solution)/shard_map/convert_element_type | solution.py:274
  27.5 0.1 fusion.26
  27.6 0.8 %collective-permute-done.10 = f32[8,128]{1,0:T(8,128)S(1)} collective-permute-done((f32[8,128]{1,0:T(8,128)S(1)}, f32[8,128]{1,0:T(8,128)S(1)}, u32[]{:S(2)}, u32[]{:S(2)}) %collective-permute-start.10) | collective-permute-done | bytes 4128 | tf_op jit(solution)/shard_map/ppermute | solution.py:180
  28.5 1.2 %collective-permute-done.12 = f32[8,128]{1,0:T(8,128)S(1)} collective-permute-done((f32[8,128]{1,0:T(8,128)S(1)}, f32[8,128]{1,0:T(8,128)S(1)}, u32[]{:S(2)}, u32[]{:S(2)}) %collective-permute-start.12) | collective-permute-done | bytes 4128 | tf_op jit(solution)/shard_map/ppermute | solution.py:67
  29.6 0.6 %add_reduce_fusion = f32[]{:T(128)} fusion(f32[128]{0:T(128)S(1)} %pad.4, f32[128]{0:T(128)S(1)} %select_reduce_fusion), kind=kLoop, calls=%fused_computation.119 | loop fusion | flops 383 | bytes 1028 | tf_op jit(solution)/shard_map/reduce_sum | solution.py:290
  (52 shorter events, 1.2 us)
Async XLA Ops:
  0.6 1.6 %collective-permute-start = (bf16[8,2048]{1,0:T(8,128)(2,1)}, bf16[8,2048]{1,0:T(8,128)(2,1)S(1)}, u32[]{:S(2)}, u32[]{:S(2)}) collective-permute-start(bf16[8,2048]{1,0:T(8,128)(2,1)} %param.2), channel_id=1, source_target_pairs={{0,1},{1,0},{2,3},{3,2},{4,5},{5,4},{6,7},{7,6},{8,9},{9,8},{10,11... | collective-permute-start | bytes 98312 | tf_op jit(solution)/shard_map/ppermute | solution.py:67
  1.1 1.4 %collective-permute-start.1 = (bf16[16,1024]{1,0:T(8,128)(2,1)}, bf16[16,1024]{1,0:T(8,128)(2,1)S(1)}, u32[]{:S(2)}, u32[]{:S(2)}) collective-permute-start(bf16[16,1024]{1,0:T(8,128)(2,1)} %param.3), channel_id=1, source_target_pairs={{0,1},{1,0},{2,3},{3,2},{4,5},{5,4},{6,7},{7,6},{8,9},{9,8},{10,11... | collective-permute-start | bytes 98312 | tf_op jit(solution)/shard_map/ppermute | solution.py:67
  1.2 1.3 %copy-start.1 = (bf16[8,2048]{1,0:T(8,128)(2,1)S(1)}, bf16[8,2048]{1,0:T(8,128)(2,1)}, u32[]{:S(2)}) copy-start(bf16[8,2048]{1,0:T(8,128)(2,1)} %param.2) | copy-start | bytes 98308
  1.2 1.3 %copy-start = (bf16[16,1024]{1,0:T(8,128)(2,1)S(1)}, bf16[16,1024]{1,0:T(8,128)(2,1)}, u32[]{:S(2)}) copy-start(bf16[16,1024]{1,0:T(8,128)(2,1)} %param.3) | copy-start | bytes 98308
  2.6 7.2 %collective-permute-start.2 = (bf16[16,2048]{1,0:T(8,128)(2,1)S(1)}, bf16[16,2048]{1,0:T(8,128)(2,1)S(1)}, u32[]{:S(2)}, u32[]{:S(2)}) collective-permute-start(bf16[16,2048]{1,0:T(8,128)(2,1)S(1)} %get-tuple-element.31), channel_id=1, source_target_pairs={{0,6},{1,25},{2,4},{3,27},{4,2},{5,29},{6,0},{7,31},{8,14},{9,17},... | collective-permute-start | bytes 196616 | tf_op jit(solution)/shard_map/ppermute | solution.py:76
  7.4 5.2 %collective-permute-start.3 = (bf16[16,2048]{1,0:T(8,128)(2,1)S(1)}, bf16[16,2048]{1,0:T(8,128)(2,1)S(1)}, u32[]{:S(2)}, u32[]{:S(2)}) collective-permute-start(bf16[16,2048]{1,0:T(8,128)(2,1)S(1)} %get-tuple-element.32), channel_id=1, source_target_pairs={{0,4},{1,17},{2,6},{3,19},{4,0},{5,21},{6,2},{7,23},{8,12},{9,25},... | collective-permute-start | bytes 196616 | tf_op jit(solution)/shard_map/ppermute | solution.py:76
  7.4 5.2 %collective-permute-start.4 = (bf16[16,2048]{1,0:T(8,128)(2,1)S(1)}, bf16[16,2048]{1,0:T(8,128)(2,1)S(1)}, u32[]{:S(2)}, u32[]{:S(2)}) collective-permute-start(bf16[16,2048]{1,0:T(8,128)(2,1)S(1)} %get-tuple-element.33), channel_id=1, source_target_pairs={{0,2},{1,9},{2,0},{3,11},{4,6},{5,13},{6,4},{7,15},{8,10},{9,1},{1... | collective-permute-start | bytes 196616 | tf_op jit(solution)/shard_map/ppermute | solution.py:76
  12.7 1.6 %collective-permute-start.5 = (bf16[64,2048]{1,0:T(8,128)(2,1)S(1)}, bf16[64,2048]{1,0:T(8,128)(2,1)S(1)}, u32[]{:S(2)}, u32[]{:S(2)}) collective-permute-start(bf16[64,2048]{1,0:T(8,128)(2,1)S(1)} %get-tuple-element.30), channel_id=1, source_target_pairs={{0,1},{1,0},{2,3},{3,2},{4,5},{5,4},{6,7},{7,6},{8,9},{9,8},{10,11... | collective-permute-start | bytes 786440 | tf_op jit(solution)/shard_map/ppermute | solution.py:67
  15.1 5.6 %collective-permute-start.8 = (bf16[64,768]{1,0:T(8,128)(2,1)S(1)}, bf16[64,768]{1,0:T(8,128)(2,1)S(1)}, u32[]{:S(2)}, u32[]{:S(2)}) collective-permute-start(bf16[64,768]{1,0:T(8,128)(2,1)S(1)} %fusion.17), channel_id=1, source_target_pairs={{0,24},{1,7},{2,26},{3,5},{4,28},{5,3},{6,30},{7,1},{8,16},{9,15},... | collective-permute-start | bytes 294920 | tf_op jit(solution)/shard_map/ppermute | solution.py:85
  17.7 4.7 %collective-permute-start.6 = (bf16[64,768]{1,0:T(8,128)(2,1)S(1)}, bf16[64,768]{1,0:T(8,128)(2,1)S(1)}, u32[]{:S(2)}, u32[]{:S(2)}) collective-permute-start(bf16[64,768]{1,0:T(8,128)(2,1)S(1)} %get-tuple-element.66), channel_id=1, source_target_pairs={{0,8},{1,3},{2,10},{3,1},{4,12},{5,7},{6,14},{7,5},{8,0},{9,11},{1... | collective-permute-start | bytes 294920 | tf_op jit(solution)/shard_map/ppermute | solution.py:85
  18.3 4.6 %collective-permute-start.7 = (bf16[64,768]{1,0:T(8,128)(2,1)S(1)}, bf16[64,768]{1,0:T(8,128)(2,1)S(1)}, u32[]{:S(2)}, u32[]{:S(2)}) collective-permute-start(bf16[64,768]{1,0:T(8,128)(2,1)S(1)} %get-tuple-element.67), channel_id=1, source_target_pairs={{0,16},{1,5},{2,18},{3,7},{4,20},{5,1},{6,22},{7,3},{8,24},{9,13},... | collective-permute-start | bytes 294920 | tf_op jit(solution)/shard_map/ppermute | solution.py:85
  23.2 1.2 %collective-permute-start.9 = (f32[8,128]{1,0:T(8,128)S(1)}, f32[8,128]{1,0:T(8,128)S(1)}, u32[]{:S(2)}, u32[]{:S(2)}) collective-permute-start(f32[8,128]{1,0:T(8,128)S(1)} %select_select_fusion), channel_id=1, source_target_pairs={{0,1},{1,0},{2,3},{3,2},{4,5},{5,4},{6,7},{7,6},{8,9},{9,8},{10,11... | collective-permute-start | bytes 12296 | tf_op jit(solution)/shard_map/ppermute | solution.py:67
  23.3 2.2 %collective-permute-start.11 = (bf16[64,640]{1,0:T(8,128)(2,1)S(1)}, bf16[64,640]{1,0:T(8,128)(2,1)S(1)}, u32[]{:S(2)}, u32[]{:S(2)}) collective-permute-start(bf16[64,640]{1,0:T(8,128)(2,1)S(1)} %pad_maximum_fusion.14), channel_id=1, source_target_pairs={{0,1},{1,0},{2,3},{3,2},{4,5},{5,4},{6,7},{7,6},{8,9},{9,8},{10,11... | collective-permute-start | bytes 245768 | tf_op jit(solution)/shard_map/ppermute | solution.py:67
  24.4 4.0 %collective-permute-start.10 = (f32[8,128]{1,0:T(8,128)S(1)}, f32[8,128]{1,0:T(8,128)S(1)}, u32[]{:S(2)}, u32[]{:S(2)}) collective-permute-start(f32[8,128]{1,0:T(8,128)S(1)} %pad_maximum_fusion.16), channel_id=1, source_target_pairs={{19,0},{25,1},{7,30},{13,31},{12,8},{24,9},{6,22},{15,23},{18,2},{... | collective-permute-start | bytes 12296 | tf_op jit(solution)/shard_map/ppermute | solution.py:180
  28.4 1.2 %collective-permute-start.12 = (f32[8,128]{1,0:T(8,128)S(1)}, f32[8,128]{1,0:T(8,128)S(1)}, u32[]{:S(2)}, u32[]{:S(2)}) collective-permute-start(f32[8,128]{1,0:T(8,128)S(1)} %pad_maximum_fusion.17), channel_id=1, source_target_pairs={{0,1},{1,0},{2,3},{3,2},{4,5},{5,4},{6,7},{7,6},{8,9},{9,8},{10,11... | collective-permute-start | bytes 12296 | tf_op jit(solution)/shard_map/ppermute | solution.py:67

commit v10 on v9

--- a/solution.py
+++ b/solution.py
@@ -177,7 +177,10 @@
             from_core = used.get(chip, 1)
             used[chip] = from_core - 1
             pairs.append(((chip[0] * side + chip[1]) * 2 + from_core, (row * side + z) * 2 + core))
-    return lax.ppermute(known, BOTH, pairs)
+    return [
+        lax.ppermute(known, BOTH, pairs),
+        lax.ppermute(known, BOTH, [(teller, hearer ^ 1) for teller, hearer in pairs]),
+    ]
 
 
 def gram_body(side, view_a, view_b):
@@ -219,21 +222,36 @@
     part = jnp.square(1.0 - corr) - off_weight * jnp.square(corr)
     part = jnp.sum(jnp.where(diagonal, part, 0.0).reshape(-1, 128), 0, keepdims=True)
 
-    lanes = width // side
+    lanes, few = width // side, 32
+    i, j = (lax.broadcasted_iota(jnp.int32, (count, count), d) for d in range(2))
+
+    def with_loss(low, part):
+        part = sum(part[:, k : k + few] for k in range(0, 128, few))
+        for line, half in enumerate(split(part)):
+            half = jnp.pad(half, ((0, 0), (0, count - few)))
+            low = jnp.where((i == count - 1 - line) & (j < few), half, low)
+        return low
 
     def payload(images, gram, part):
         images = [images[:, i * lanes : (i + 1) * lanes] for i in range(side)]
-        part = [jnp.broadcast_to(x, (count // 2, 128)) for x in split(part)]
-        return jnp.concatenate([jnp.concatenate(images, 0), *split(gram), jnp.concatenate(part, 0)], 1)
-
-    def images_of(step):
+        high, low = split(gram)
+        return jnp.concatenate([jnp.concatenate(images, 0), high, with_loss(low, part)], 1)
+
+    def images_of(step, extra):
         return lax.dynamic_slice_in_dim(extra, (row ^ step) * pair, pair, 0)
 
-    landed = {step: across(payload(images_of(step), gram, part), side, step) for step in range(1, side)}
-    landed[0] = payload(images_of(0), gram, part)
+    landed = {}
+    for step in (2, 1, *range(3, side)):
+        ready = payload(images_of(step, extra), gram, part)
+        ready, extra = lax.optimization_barrier((ready, extra))
+        landed[step] = across(ready, side, step)
+    landed[0] = payload(images_of(0, extra), gram, part)
     summed = total([landed[step].astype(jnp.float32) for step in range(side)])
-    gram = summed[:, lanes : lanes + count] + summed[:, lanes + count : lanes + 2 * count]
-    part = summed[:1, lanes + 2 * count :] + summed[count // 2 : count // 2 + 1, lanes + 2 * count :]
+    high, low = summed[:, lanes : lanes + count], summed[:, lanes + count :]
+    part = low[count - 1 :, :few] + low[count - 2 : count - 1, :few]
+    part = jnp.pad(part, ((0, 0), (0, 128 - few)))
+    gram = high + low
+    gram = jnp.where((i >= count - 2) & (j < few), gram.T, gram)
 
     sent = jnp.concatenate([summed[:, :lanes].astype(jnp.bfloat16), *split(gram)], 1)
     came = sibling(sent, n_col)
@@ -285,8 +303,7 @@
     grad_b = gradient(terms(for_b, all_b), all_b, scaled_b, extra_b, row * pair, pair)
 
     heard, grad_a, grad_b, everywhere = lax.optimization_barrier((heard, grad_a, grad_b, everywhere))
-    known = joined(known, heard)
-    known = joined(known, sibling(known, n_col))
+    known = joined(joined(known, heard[0]), heard[1])
     loss = jnp.sum(everywhere + jnp.sum(known[:side], 0) * (1.0 / (width * side)))
     return (loss, grad_a, grad_b)
 

time: 30.4 us -> 30.1 us (level)
  waiting for transfers between devices: 13.6 us -> 12.1 us
  starting transfers between devices: 11.4 us -> 11.9 us
  other arithmetic: 3.54 us -> 3.94 us
    ppermute x6 -> x5, waiting for transfers between devices: 4.15 us -> 2.73 us  [sibling(): return lax.ppermute(value, 'col', [(c, c ^ 1) for c in range(n_col)])]
    ppermute x1 -> x2, starting transfers between devices: 1.09 us -> 1.79 us  [the longest x1 0.95 us: hear(): lax.ppermute(known, BOTH, pairs)]
    ppermute x1 -> x2, waiting for transfers between devices: 0.81 us -> 0.89 us  [the longest x1 0.78 us: hear(): lax.ppermute(known, BOTH, pairs)]
    ppermute x6 -> x5, starting transfers between devices: 1.25 us -> 1.19 us  [sibling(): return lax.ppermute(value, 'col', [(c, c ^ 1) for c in range(n_col)])]
  transfers between devices with their start and end apart: 13 -> 13, of which waited for: 11 -> 11; matrix products, arithmetic and copies ran while one was open for 8% -> 9% of each run, Pallas kernels for 0% -> 0%
where the time goes in v10:
time: 30.1 us; the launch traced here: 29.8 us
  waiting for transfers between devices  12.1 us (40%)
  starting transfers between devices  11.9 us (40%)
  other arithmetic  3.94 us (13%)
  between operations  1 us (3%)
  matrix products  0.68 us (2%)
    ppermute x3, starting transfers between devices, flip(): return lax.ppermute(value, BOTH, pairs)  5.47 us
    ppermute x3, waiting for transfers between devices, flip(): return lax.ppermute(value, BOTH, pairs)  4.52 us
    ppermute x3, waiting for transfers between devices, across(): return lax.ppermute(value, BOTH, pairs)  3.93 us
    ppermute x3, starting transfers between devices, across(): return lax.ppermute(value, BOTH, pairs)  3.5 us
    ppermute x5, waiting for transfers between devices, sibling(): return lax.ppermute(value, 'col', [(c, c ^ 1) for c in range(n_col)])  2.73 us
    convert_element_type x2, other arithmetic, gradient(): (scaled * (term - first - normed * second + extra.astype(jnp.float32))).a...  1.32 us
    ppermute x5, starting transfers between devices, sibling(): return lax.ppermute(value, 'col', [(c, c ^ 1) for c in range(n_col)])  1.19 us
    ppermute x1, starting transfers between devices, hear(): lax.ppermute(known, BOTH, pairs)  0.95 us
  transfers between devices with their start and end apart: 13, of which 11 were waited for; matrix products, arithmetic and copies ran while one was open for 9% of the time, Pallas kernels for 0%

profile of v10, /device:TPU:0, one launch (start us, length us, event | category | flops | bytes accessed | tf_op | source)
XLA Modules:
  0.0 29.8 jit_solution(6807377858551333860)
XLA Ops:
  0.6 0.5 %collective-permute-start = (bf16[8,2048]{1,0:T(8,128)(2,1)}, bf16[8,2048]{1,0:T(8,128)(2,1)S(1)}, u32[]{:S(2)}, u32[]{:S(2)}) collective-permute-start(bf16[8,2048]{1,0:T(8,128)(2,1)} %param.2), channel_id=1, source_target_pairs={{0,1},{1,0},{2,3},{3,2},{4,5},{5,4},{6,7},{7,6},{8,9},{9,8},{10,11... | collective-permute-start | bytes 98312 | tf_op jit(solution)/shard_map/ppermute | solution.py:67
  1.3 0.9 %collective-permute-done = bf16[8,2048]{1,0:T(8,128)(2,1)S(1)} collective-permute-done((bf16[8,2048]{1,0:T(8,128)(2,1)}, bf16[8,2048]{1,0:T(8,128)(2,1)S(1)}, u32[]{:S(2)}, u32[]{:S(2)}) %collective-permute-start) | collective-permute-done | bytes 32800 | tf_op jit(solution)/shard_map/ppermute | solution.py:67
  2.2 0.3 %collective-permute-done.1 = bf16[16,1024]{1,0:T(8,128)(2,1)S(1)} collective-permute-done((bf16[16,1024]{1,0:T(8,128)(2,1)}, bf16[16,1024]{1,0:T(8,128)(2,1)S(1)}, u32[]{:S(2)}, u32[]{:S(2)}) %collective-permute-start.1) | collective-permute-done | bytes 32800 | tf_op jit(solution)/shard_map/ppermute | solution.py:67
  2.6 4.8 %collective-permute-start.2 = (bf16[16,2048]{1,0:T(8,128)(2,1)S(1)}, bf16[16,2048]{1,0:T(8,128)(2,1)S(1)}, u32[]{:S(2)}, u32[]{:S(2)}) collective-permute-start(bf16[16,2048]{1,0:T(8,128)(2,1)S(1)} %get-tuple-element.49), channel_id=1, source_target_pairs={{0,6},{1,25},{2,4},{3,27},{4,2},{5,29},{6,0},{7,31},{8,14},{9,17},... | collective-permute-start | bytes 196616 | tf_op jit(solution)/shard_map/ppermute | solution.py:76
  7.4 0.6 %collective-permute-start.4 = (bf16[16,2048]{1,0:T(8,128)(2,1)S(1)}, bf16[16,2048]{1,0:T(8,128)(2,1)S(1)}, u32[]{:S(2)}, u32[]{:S(2)}) collective-permute-start(bf16[16,2048]{1,0:T(8,128)(2,1)S(1)} %get-tuple-element.51), channel_id=1, source_target_pairs={{0,2},{1,9},{2,0},{3,11},{4,6},{5,13},{6,4},{7,15},{8,10},{9,1},{1... | collective-permute-start | bytes 196616 | tf_op jit(solution)/shard_map/ppermute | solution.py:76
  8.1 1.7 %collective-permute-done.2 = bf16[16,2048]{1,0:T(8,128)(2,1)S(1)} collective-permute-done((bf16[16,2048]{1,0:T(8,128)(2,1)S(1)}, bf16[16,2048]{1,0:T(8,128)(2,1)S(1)}, u32[]{:S(2)}, u32[]{:S(2)}) %collective-permute-start.2) | collective-permute-done | bytes 65568 | tf_op jit(solution)/shard_map/ppermute | solution.py:76
  9.8 2.8 %collective-permute-done.3 = bf16[16,2048]{1,0:T(8,128)(2,1)S(1)} collective-permute-done((bf16[16,2048]{1,0:T(8,128)(2,1)S(1)}, bf16[16,2048]{1,0:T(8,128)(2,1)S(1)}, u32[]{:S(2)}, u32[]{:S(2)}) %collective-permute-start.3) | collective-permute-done | bytes 65568 | tf_op jit(solution)/shard_map/ppermute | solution.py:76
  13.0 0.2 fusion.37
  13.2 1.1 %collective-permute-done.5 = bf16[64,2048]{1,0:T(8,128)(2,1)S(1)} collective-permute-done((bf16[64,2048]{1,0:T(8,128)(2,1)S(1)}, bf16[64,2048]{1,0:T(8,128)(2,1)S(1)}, u32[]{:S(2)}, u32[]{:S(2)}) %collective-permute-start.5) | collective-permute-done | bytes 262176 | tf_op jit(solution)/shard_map/ppermute | solution.py:67
  14.4 0.1 fusion.4
  14.5 0.1 broadcast_select_fusion
  14.6 0.1 convert_reduce_fusion
  14.9 0.1 fusion.12
  15.4 2.5 %collective-permute-start.8 = (bf16[64,640]{1,0:T(8,128)(2,1)S(1)}, bf16[64,640]{1,0:T(8,128)(2,1)S(1)}, u32[]{:S(2)}, u32[]{:S(2)}) collective-permute-start(bf16[64,640]{1,0:T(8,128)(2,1)S(1)} %pad_maximum_fusion.6), channel_id=1, source_target_pairs={{0,24},{1,7},{2,26},{3,5},{4,28},{5,3},{6,30},{7,1},{8,16},{9,15},... | collective-permute-start | bytes 245768 | tf_op jit(solution)/shard_map/ppermute | solution.py:85
  17.9 0.5 %collective-permute-start.6 = (bf16[64,640]{1,0:T(8,128)(2,1)S(1)}, bf16[64,640]{1,0:T(8,128)(2,1)S(1)}, u32[]{:S(2)}, u32[]{:S(2)}) collective-permute-start(bf16[64,640]{1,0:T(8,128)(2,1)S(1)} %pad_maximum_fusion.7), channel_id=1, source_target_pairs={{0,8},{1,3},{2,10},{3,1},{4,12},{5,7},{6,14},{7,5},{8,0},{9,11},{1... | collective-permute-start | bytes 245768 | tf_op jit(solution)/shard_map/ppermute | solution.py:85
  18.4 0.5 %collective-permute-start.7 = (bf16[64,640]{1,0:T(8,128)(2,1)S(1)}, bf16[64,640]{1,0:T(8,128)(2,1)S(1)}, u32[]{:S(2)}, u32[]{:S(2)}) collective-permute-start(bf16[64,640]{1,0:T(8,128)(2,1)S(1)} %pad_maximum_fusion.8), channel_id=1, source_target_pairs={{0,16},{1,5},{2,18},{3,7},{4,20},{5,1},{6,22},{7,3},{8,24},{9,13},... | collective-permute-start | bytes 245768 | tf_op jit(solution)/shard_map/ppermute | solution.py:85
  18.9 1.8 %collective-permute-done.8 = bf16[64,640]{1,0:T(8,128)(2,1)S(1)} collective-permute-done((bf16[64,640]{1,0:T(8,128)(2,1)S(1)}, bf16[64,640]{1,0:T(8,128)(2,1)S(1)}, u32[]{:S(2)}, u32[]{:S(2)}) %collective-permute-start.8) | collective-permute-done | bytes 81952 | tf_op jit(solution)/shard_map/ppermute | solution.py:85
  20.8 1.5 %collective-permute-done.6 = bf16[64,640]{1,0:T(8,128)(2,1)S(1)} collective-permute-done((bf16[64,640]{1,0:T(8,128)(2,1)S(1)}, bf16[64,640]{1,0:T(8,128)(2,1)S(1)}, u32[]{:S(2)}, u32[]{:S(2)}) %collective-permute-start.6) | collective-permute-done | bytes 81952 | tf_op jit(solution)/shard_map/ppermute | solution.py:85
  22.3 0.5 %collective-permute-done.7 = bf16[64,640]{1,0:T(8,128)(2,1)S(1)} collective-permute-done((bf16[64,640]{1,0:T(8,128)(2,1)S(1)}, bf16[64,640]{1,0:T(8,128)(2,1)S(1)}, u32[]{:S(2)}, u32[]{:S(2)}) %collective-permute-start.7) | collective-permute-done | bytes 81952 | tf_op jit(solution)/shard_map/ppermute | solution.py:85
  23.3 0.1 reduce-precision_convert_fusion
  23.5 0.5 %collective-permute-start.12 = (bf16[64,640]{1,0:T(8,128)(2,1)S(1)}, bf16[64,640]{1,0:T(8,128)(2,1)S(1)}, u32[]{:S(2)}, u32[]{:S(2)}) collective-permute-start(bf16[64,640]{1,0:T(8,128)(2,1)S(1)} %pad_maximum_fusion.13), channel_id=1, source_target_pairs={{0,1},{1,0},{2,3},{3,2},{4,5},{5,4},{6,7},{7,6},{8,9},{9,8},{10,11... | collective-permute-start | bytes 245768 | tf_op jit(solution)/shard_map/ppermute | solution.py:67
  24.0 0.4 %collective-permute-done.9 = f32[8,128]{1,0:T(8,128)S(1)} collective-permute-done((f32[8,128]{1,0:T(8,128)S(1)}, f32[8,128]{1,0:T(8,128)S(1)}, u32[]{:S(2)}, u32[]{:S(2)}) %collective-permute-start.9) | collective-permute-done | bytes 4128 | tf_op jit(solution)/shard_map/ppermute | solution.py:67
  24.4 0.8 %collective-permute-start.11 = (f32[8,128]{1,0:T(8,128)S(1)}, f32[8,128]{1,0:T(8,128)S(1)}, u32[]{:S(2)}, u32[]{:S(2)}) collective-permute-start(f32[8,128]{1,0:T(8,128)S(1)} %pad_maximum_fusion.15), channel_id=1, source_target_pairs={{19,1},{25,0},{7,31},{13,30},{12,9},{24,8},{6,23},{15,22},{18,3},{... | collective-permute-start | bytes 12296 | tf_op jit(solution)/shard_map/ppermute | solution.py:182
  25.2 1.0 %collective-permute-start.10 = (f32[8,128]{1,0:T(8,128)S(1)}, f32[8,128]{1,0:T(8,128)S(1)}, u32[]{:S(2)}, u32[]{:S(2)}) collective-permute-start(f32[8,128]{1,0:T(8,128)S(1)} %pad_maximum_fusion.15), channel_id=1, source_target_pairs={{19,0},{25,1},{7,30},{13,31},{12,8},{24,9},{6,22},{15,23},{18,2},{... | collective-permute-start | bytes 12296 | tf_op jit(solution)/shard_map/ppermute | solution.py:181
  26.3 0.2 fusion.31
  26.5 0.3 fusion.30
  26.8 0.7 %multiply_convert_fusion.1 = bf16[8,2048]{1,0:T(8,128)(2,1)} fusion(f32[64,2048]{1,0:T(8,128)S(1)} %get-tuple-element.88, s32[]{:T(128)S(6)} %select_n.240, s32[]{:T(128)S(6)} %select_n.241, bf16[64,2048]{1,0:T(8,128)(2,1)S(1)} %get-tuple-element.43, bf16[16,2048]{1,0:T(8,128)(2,1)S(1)} %pad_maximum_fusion.14, f32[2048]{0:T(1024)S(1)} %broadcast_multiply_fusion, ...), kind=kLoop, calls=%fused_computation.51 | loop fusion | flops 196608 | bytes 450569 | tf_op jit(solution)/shard_map/convert_element_type | solution.py:292
  27.5 0.7 %multiply_convert_fusion = bf16[16,1024]{1,0:T(8,128)(2,1)} fusion(f32[64,1024]{1,0:T(8,128)S(1)} %get-tuple-element.89, s32[]{:T(128)S(6)} %select_n.229, s32[]{:T(128)S(6)} %select_n.249, bf16[64,1024]{1,0:T(8,128)(2,1)S(1)} %slice_select_fusion, bf16[16,512]{1,0:T(8,128)(2,1)S(1)} %get-tuple-element.76, bf16[16,512]{1,0:T(8,128)(2,1)S(1)} %get-tuple-element.77, ...), kind=kLoop, calls=%fused_computation.50 | loop fusion | flops 327680 | bytes 307209 | tf_op jit(solution)/shard_map/convert_element_type | solution.py:292
  28.2 0.1 fusion.22
  28.3 0.1 collective-permute-done.11
  28.4 0.8 %collective-permute-done.10 = f32[8,128]{1,0:T(8,128)S(1)} collective-permute-done((f32[8,128]{1,0:T(8,128)S(1)}, f32[8,128]{1,0:T(8,128)S(1)}, u32[]{:S(2)}, u32[]{:S(2)}) %collective-permute-start.10) | collective-permute-done | bytes 4128 | tf_op jit(solution)/shard_map/ppermute | solution.py:181
  29.2 0.6 %add_reduce_fusion = f32[]{:T(128)} fusion(f32[128]{0:T(128)S(1)} %pad.24, f32[128]{0:T(128)S(1)} %select_reduce_fusion), kind=kLoop, calls=%fused_computation.115 | loop fusion | flops 383 | bytes 1028 | tf_op jit(solution)/shard_map/reduce_sum | solution.py:307
  (62 shorter events, 1.7 us)
Async XLA Ops:
  0.6 1.6 %collective-permute-start = (bf16[8,2048]{1,0:T(8,128)(2,1)}, bf16[8,2048]{1,0:T(8,128)(2,1)S(1)}, u32[]{:S(2)}, u32[]{:S(2)}) collective-permute-start(bf16[8,2048]{1,0:T(8,128)(2,1)} %param.2), channel_id=1, source_target_pairs={{0,1},{1,0},{2,3},{3,2},{4,5},{5,4},{6,7},{7,6},{8,9},{9,8},{10,11... | collective-permute-start | bytes 98312 | tf_op jit(solution)/shard_map/ppermute | solution.py:67
  1.1 1.4 %collective-permute-start.1 = (bf16[16,1024]{1,0:T(8,128)(2,1)}, bf16[16,1024]{1,0:T(8,128)(2,1)S(1)}, u32[]{:S(2)}, u32[]{:S(2)}) collective-permute-start(bf16[16,1024]{1,0:T(8,128)(2,1)} %param.3), channel_id=1, source_target_pairs={{0,1},{1,0},{2,3},{3,2},{4,5},{5,4},{6,7},{7,6},{8,9},{9,8},{10,11... | collective-permute-start | bytes 98312 | tf_op jit(solution)/shard_map/ppermute | solution.py:67
  1.3 1.3 %copy-start.1 = (bf16[8,2048]{1,0:T(8,128)(2,1)S(1)}, bf16[8,2048]{1,0:T(8,128)(2,1)}, u32[]{:S(2)}) copy-start(bf16[8,2048]{1,0:T(8,128)(2,1)} %param.2) | copy-start | bytes 98308
  1.3 1.3 %copy-start = (bf16[16,1024]{1,0:T(8,128)(2,1)S(1)}, bf16[16,1024]{1,0:T(8,128)(2,1)}, u32[]{:S(2)}) copy-start(bf16[16,1024]{1,0:T(8,128)(2,1)} %param.3) | copy-start | bytes 98308
  2.6 7.2 %collective-permute-start.2 = (bf16[16,2048]{1,0:T(8,128)(2,1)S(1)}, bf16[16,2048]{1,0:T(8,128)(2,1)S(1)}, u32[]{:S(2)}, u32[]{:S(2)}) collective-permute-start(bf16[16,2048]{1,0:T(8,128)(2,1)S(1)} %get-tuple-element.49), channel_id=1, source_target_pairs={{0,6},{1,25},{2,4},{3,27},{4,2},{5,29},{6,0},{7,31},{8,14},{9,17},... | collective-permute-start | bytes 196616 | tf_op jit(solution)/shard_map/ppermute | solution.py:76
  7.4 5.2 %collective-permute-start.3 = (bf16[16,2048]{1,0:T(8,128)(2,1)S(1)}, bf16[16,2048]{1,0:T(8,128)(2,1)S(1)}, u32[]{:S(2)}, u32[]{:S(2)}) collective-permute-start(bf16[16,2048]{1,0:T(8,128)(2,1)S(1)} %get-tuple-element.50), channel_id=1, source_target_pairs={{0,4},{1,17},{2,6},{3,19},{4,0},{5,21},{6,2},{7,23},{8,12},{9,25},... | collective-permute-start | bytes 196616 | tf_op jit(solution)/shard_map/ppermute | solution.py:76
  7.4 5.2 %collective-permute-start.4 = (bf16[16,2048]{1,0:T(8,128)(2,1)S(1)}, bf16[16,2048]{1,0:T(8,128)(2,1)S(1)}, u32[]{:S(2)}, u32[]{:S(2)}) collective-permute-start(bf16[16,2048]{1,0:T(8,128)(2,1)S(1)} %get-tuple-element.51), channel_id=1, source_target_pairs={{0,2},{1,9},{2,0},{3,11},{4,6},{5,13},{6,4},{7,15},{8,10},{9,1},{1... | collective-permute-start | bytes 196616 | tf_op jit(solution)/shard_map/ppermute | solution.py:76
  12.7 1.6 %collective-permute-start.5 = (bf16[64,2048]{1,0:T(8,128)(2,1)S(1)}, bf16[64,2048]{1,0:T(8,128)(2,1)S(1)}, u32[]{:S(2)}, u32[]{:S(2)}) collective-permute-start(bf16[64,2048]{1,0:T(8,128)(2,1)S(1)} %get-tuple-element.48), channel_id=1, source_target_pairs={{0,1},{1,0},{2,3},{3,2},{4,5},{5,4},{6,7},{7,6},{8,9},{9,8},{10,11... | collective-permute-start | bytes 786440 | tf_op jit(solution)/shard_map/ppermute | solution.py:67
  15.4 5.3 %collective-permute-start.8 = (bf16[64,640]{1,0:T(8,128)(2,1)S(1)}, bf16[64,640]{1,0:T(8,128)(2,1)S(1)}, u32[]{:S(2)}, u32[]{:S(2)}) collective-permute-start(bf16[64,640]{1,0:T(8,128)(2,1)S(1)} %pad_maximum_fusion.6), channel_id=1, source_target_pairs={{0,24},{1,7},{2,26},{3,5},{4,28},{5,3},{6,30},{7,1},{8,16},{9,15},... | collective-permute-start | bytes 245768 | tf_op jit(solution)/shard_map/ppermute | solution.py:85
  17.9 4.4 %collective-permute-start.6 = (bf16[64,640]{1,0:T(8,128)(2,1)S(1)}, bf16[64,640]{1,0:T(8,128)(2,1)S(1)}, u32[]{:S(2)}, u32[]{:S(2)}) collective-permute-start(bf16[64,640]{1,0:T(8,128)(2,1)S(1)} %pad_maximum_fusion.7), channel_id=1, source_target_pairs={{0,8},{1,3},{2,10},{3,1},{4,12},{5,7},{6,14},{7,5},{8,0},{9,11},{1... | collective-permute-start | bytes 245768 | tf_op jit(solution)/shard_map/ppermute | solution.py:85
  18.4 4.4 %collective-permute-start.7 = (bf16[64,640]{1,0:T(8,128)(2,1)S(1)}, bf16[64,640]{1,0:T(8,128)(2,1)S(1)}, u32[]{:S(2)}, u32[]{:S(2)}) collective-permute-start(bf16[64,640]{1,0:T(8,128)(2,1)S(1)} %pad_maximum_fusion.8), channel_id=1, source_target_pairs={{0,16},{1,5},{2,18},{3,7},{4,20},{5,1},{6,22},{7,3},{8,24},{9,13},... | collective-permute-start | bytes 245768 | tf_op jit(solution)/shard_map/ppermute | solution.py:85
  23.2 1.2 %collective-permute-start.9 = (f32[8,128]{1,0:T(8,128)S(1)}, f32[8,128]{1,0:T(8,128)S(1)}, u32[]{:S(2)}, u32[]{:S(2)}) collective-permute-start(f32[8,128]{1,0:T(8,128)S(1)} %select_select_fusion), channel_id=1, source_target_pairs={{0,1},{1,0},{2,3},{3,2},{4,5},{5,4},{6,7},{7,6},{8,9},{9,8},{10,11... | collective-permute-start | bytes 12296 | tf_op jit(solution)/shard_map/ppermute | solution.py:67
  23.5 2.7 %collective-permute-start.12 = (bf16[64,640]{1,0:T(8,128)(2,1)S(1)}, bf16[64,640]{1,0:T(8,128)(2,1)S(1)}, u32[]{:S(2)}, u32[]{:S(2)}) collective-permute-start(bf16[64,640]{1,0:T(8,128)(2,1)S(1)} %pad_maximum_fusion.13), channel_id=1, source_target_pairs={{0,1},{1,0},{2,3},{3,2},{4,5},{5,4},{6,7},{7,6},{8,9},{9,8},{10,11... | collective-permute-start | bytes 245768 | tf_op jit(solution)/shard_map/ppermute | solution.py:67
  24.4 4.0 %collective-permute-start.11 = (f32[8,128]{1,0:T(8,128)S(1)}, f32[8,128]{1,0:T(8,128)S(1)}, u32[]{:S(2)}, u32[]{:S(2)}) collective-permute-start(f32[8,128]{1,0:T(8,128)S(1)} %pad_maximum_fusion.15), channel_id=1, source_target_pairs={{19,1},{25,0},{7,31},{13,30},{12,9},{24,8},{6,23},{15,22},{18,3},{... | collective-permute-start | bytes 12296 | tf_op jit(solution)/shard_map/ppermute | solution.py:182
  25.2 3.9 %collective-permute-start.10 = (f32[8,128]{1,0:T(8,128)S(1)}, f32[8,128]{1,0:T(8,128)S(1)}, u32[]{:S(2)}, u32[]{:S(2)}) collective-permute-start(f32[8,128]{1,0:T(8,128)S(1)} %pad_maximum_fusion.15), channel_id=1, source_target_pairs={{19,0},{25,1},{7,30},{13,31},{12,8},{24,9},{6,22},{15,23},{18,2},{... | collective-permute-start | bytes 12296 | tf_op jit(solution)/shard_map/ppermute | solution.py:181

commit v11 on v10

--- a/solution.py
+++ b/solution.py
@@ -178,8 +178,8 @@
             used[chip] = from_core - 1
             pairs.append(((chip[0] * side + chip[1]) * 2 + from_core, (row * side + z) * 2 + core))
     return [
+        lax.ppermute(known, BOTH, [(teller, hearer ^ 1) for teller, hearer in pairs]),
         lax.ppermute(known, BOTH, pairs),
-        lax.ppermute(known, BOTH, [(teller, hearer ^ 1) for teller, hearer in pairs]),
     ]
 
 

time: 30.1 us -> 30 us (level)
  starting transfers between devices: 11.9 us -> 12.8 us
  waiting for transfers between devices: 12.1 us -> 11.2 us
    ppermute x1, starting transfers between devices: 0.84 us -> 1.81 us  [hear(): lax.ppermute(known, BOTH, [(teller, hearer ^ 1) for teller, hearer in pai...]
    ppermute x1, waiting for transfers between devices: 0.78 us -> 0.01 us  [hear(): lax.ppermute(known, BOTH, pairs)]
  transfers between devices with their start and end apart: 13 -> 13, of which waited for: 11 -> 9; matrix products, arithmetic and copies ran while one was open for 9% -> 9% of each run, Pallas kernels for 0% -> 0%
where the time goes in v11:
time: 30 us; the launch traced here: 29.8 us
  starting transfers between devices  12.8 us (43%)
  waiting for transfers between devices  11.2 us (37%)
  other arithmetic  3.94 us (13%)
  between operations  1.01 us (3%)
  matrix products  0.68 us (2%)
    ppermute x3, starting transfers between devices, flip(): return lax.ppermute(value, BOTH, pairs)  5.47 us
    ppermute x3, waiting for transfers between devices, flip(): return lax.ppermute(value, BOTH, pairs)  4.52 us
    ppermute x3, waiting for transfers between devices, across(): return lax.ppermute(value, BOTH, pairs)  3.93 us
    ppermute x3, starting transfers between devices, across(): return lax.ppermute(value, BOTH, pairs)  3.5 us
    ppermute x5, waiting for transfers between devices, sibling(): return lax.ppermute(value, 'col', [(c, c ^ 1) for c in range(n_col)])  2.73 us
    ppermute x1, starting transfers between devices, hear(): lax.ppermute(known, BOTH, [(teller, hearer ^ 1) for teller, hearer in pai...  1.81 us
    convert_element_type x2, other arithmetic, gradient(): (scaled * (term - first - normed * second + extra.astype(jnp.float32))).a...  1.32 us
    ppermute x5, starting transfers between devices, sibling(): return lax.ppermute(value, 'col', [(c, c ^ 1) for c in range(n_col)])  1.19 us
  transfers between devices with their start and end apart: 13, of which 9 were waited for; matrix products, arithmetic and copies ran while one was open for 9% of the time, Pallas kernels for 0%

profile of v11, /device:TPU:0, one launch (start us, length us, event | category | flops | bytes accessed | tf_op | source)
XLA Modules:
  0.0 29.8 jit_solution(8434458612161544522)
XLA Ops:
  0.6 0.5 %collective-permute-start = (bf16[8,2048]{1,0:T(8,128)(2,1)}, bf16[8,2048]{1,0:T(8,128)(2,1)S(1)}, u32[]{:S(2)}, u32[]{:S(2)}) collective-permute-start(bf16[8,2048]{1,0:T(8,128)(2,1)} %param.2), channel_id=1, source_target_pairs={{0,1},{1,0},{2,3},{3,2},{4,5},{5,4},{6,7},{7,6},{8,9},{9,8},{10,11... | collective-permute-start | bytes 98312 | tf_op jit(solution)/shard_map/ppermute | solution.py:67
  1.3 0.9 %collective-permute-done = bf16[8,2048]{1,0:T(8,128)(2,1)S(1)} collective-permute-done((bf16[8,2048]{1,0:T(8,128)(2,1)}, bf16[8,2048]{1,0:T(8,128)(2,1)S(1)}, u32[]{:S(2)}, u32[]{:S(2)}) %collective-permute-start) | collective-permute-done | bytes 32800 | tf_op jit(solution)/shard_map/ppermute | solution.py:67
  2.2 0.3 %collective-permute-done.1 = bf16[16,1024]{1,0:T(8,128)(2,1)S(1)} collective-permute-done((bf16[16,1024]{1,0:T(8,128)(2,1)}, bf16[16,1024]{1,0:T(8,128)(2,1)S(1)}, u32[]{:S(2)}, u32[]{:S(2)}) %collective-permute-start.1) | collective-permute-done | bytes 32800 | tf_op jit(solution)/shard_map/ppermute | solution.py:67
  2.6 4.8 %collective-permute-start.2 = (bf16[16,2048]{1,0:T(8,128)(2,1)S(1)}, bf16[16,2048]{1,0:T(8,128)(2,1)S(1)}, u32[]{:S(2)}, u32[]{:S(2)}) collective-permute-start(bf16[16,2048]{1,0:T(8,128)(2,1)S(1)} %get-tuple-element.49), channel_id=1, source_target_pairs={{0,6},{1,25},{2,4},{3,27},{4,2},{5,29},{6,0},{7,31},{8,14},{9,17},... | collective-permute-start | bytes 196616 | tf_op jit(solution)/shard_map/ppermute | solution.py:76
  7.4 0.6 %collective-permute-start.4 = (bf16[16,2048]{1,0:T(8,128)(2,1)S(1)}, bf16[16,2048]{1,0:T(8,128)(2,1)S(1)}, u32[]{:S(2)}, u32[]{:S(2)}) collective-permute-start(bf16[16,2048]{1,0:T(8,128)(2,1)S(1)} %get-tuple-element.51), channel_id=1, source_target_pairs={{0,2},{1,9},{2,0},{3,11},{4,6},{5,13},{6,4},{7,15},{8,10},{9,1},{1... | collective-permute-start | bytes 196616 | tf_op jit(solution)/shard_map/ppermute | solution.py:76
  8.1 1.7 %collective-permute-done.2 = bf16[16,2048]{1,0:T(8,128)(2,1)S(1)} collective-permute-done((bf16[16,2048]{1,0:T(8,128)(2,1)S(1)}, bf16[16,2048]{1,0:T(8,128)(2,1)S(1)}, u32[]{:S(2)}, u32[]{:S(2)}) %collective-permute-start.2) | collective-permute-done | bytes 65568 | tf_op jit(solution)/shard_map/ppermute | solution.py:76
  9.8 2.8 %collective-permute-done.3 = bf16[16,2048]{1,0:T(8,128)(2,1)S(1)} collective-permute-done((bf16[16,2048]{1,0:T(8,128)(2,1)S(1)}, bf16[16,2048]{1,0:T(8,128)(2,1)S(1)}, u32[]{:S(2)}, u32[]{:S(2)}) %collective-permute-start.3) | collective-permute-done | bytes 65568 | tf_op jit(solution)/shard_map/ppermute | solution.py:76
  12.8 0.1 fusion.7
  13.0 0.2 fusion.37
  13.2 1.1 %collective-permute-done.5 = bf16[64,2048]{1,0:T(8,128)(2,1)S(1)} collective-permute-done((bf16[64,2048]{1,0:T(8,128)(2,1)S(1)}, bf16[64,2048]{1,0:T(8,128)(2,1)S(1)}, u32[]{:S(2)}, u32[]{:S(2)}) %collective-permute-start.5) | collective-permute-done | bytes 262176 | tf_op jit(solution)/shard_map/ppermute | solution.py:67
  14.4 0.1 fusion.4
  14.5 0.1 broadcast_select_fusion
  14.6 0.1 convert_reduce_fusion
  14.9 0.1 fusion.12
  15.4 2.5 %collective-permute-start.8 = (bf16[64,640]{1,0:T(8,128)(2,1)S(1)}, bf16[64,640]{1,0:T(8,128)(2,1)S(1)}, u32[]{:S(2)}, u32[]{:S(2)}) collective-permute-start(bf16[64,640]{1,0:T(8,128)(2,1)S(1)} %pad_maximum_fusion.6), channel_id=1, source_target_pairs={{0,24},{1,7},{2,26},{3,5},{4,28},{5,3},{6,30},{7,1},{8,16},{9,15},... | collective-permute-start | bytes 245768 | tf_op jit(solution)/shard_map/ppermute | solution.py:85
  17.9 0.5 %collective-permute-start.6 = (bf16[64,640]{1,0:T(8,128)(2,1)S(1)}, bf16[64,640]{1,0:T(8,128)(2,1)S(1)}, u32[]{:S(2)}, u32[]{:S(2)}) collective-permute-start(bf16[64,640]{1,0:T(8,128)(2,1)S(1)} %pad_maximum_fusion.7), channel_id=1, source_target_pairs={{0,8},{1,3},{2,10},{3,1},{4,12},{5,7},{6,14},{7,5},{8,0},{9,11},{1... | collective-permute-start | bytes 245768 | tf_op jit(solution)/shard_map/ppermute | solution.py:85
  18.4 0.5 %collective-permute-start.7 = (bf16[64,640]{1,0:T(8,128)(2,1)S(1)}, bf16[64,640]{1,0:T(8,128)(2,1)S(1)}, u32[]{:S(2)}, u32[]{:S(2)}) collective-permute-start(bf16[64,640]{1,0:T(8,128)(2,1)S(1)} %pad_maximum_fusion.8), channel_id=1, source_target_pairs={{0,16},{1,5},{2,18},{3,7},{4,20},{5,1},{6,22},{7,3},{8,24},{9,13},... | collective-permute-start | bytes 245768 | tf_op jit(solution)/shard_map/ppermute | solution.py:85
  18.9 1.8 %collective-permute-done.8 = bf16[64,640]{1,0:T(8,128)(2,1)S(1)} collective-permute-done((bf16[64,640]{1,0:T(8,128)(2,1)S(1)}, bf16[64,640]{1,0:T(8,128)(2,1)S(1)}, u32[]{:S(2)}, u32[]{:S(2)}) %collective-permute-start.8) | collective-permute-done | bytes 81952 | tf_op jit(solution)/shard_map/ppermute | solution.py:85
  20.8 1.5 %collective-permute-done.6 = bf16[64,640]{1,0:T(8,128)(2,1)S(1)} collective-permute-done((bf16[64,640]{1,0:T(8,128)(2,1)S(1)}, bf16[64,640]{1,0:T(8,128)(2,1)S(1)}, u32[]{:S(2)}, u32[]{:S(2)}) %collective-permute-start.6) | collective-permute-done | bytes 81952 | tf_op jit(solution)/shard_map/ppermute | solution.py:85
  22.3 0.5 %collective-permute-done.7 = bf16[64,640]{1,0:T(8,128)(2,1)S(1)} collective-permute-done((bf16[64,640]{1,0:T(8,128)(2,1)S(1)}, bf16[64,640]{1,0:T(8,128)(2,1)S(1)}, u32[]{:S(2)}, u32[]{:S(2)}) %collective-permute-start.7) | collective-permute-done | bytes 81952 | tf_op jit(solution)/shard_map/ppermute | solution.py:85
  23.3 0.1 reduce-precision_convert_fusion
  23.5 0.5 %collective-permute-start.12 = (bf16[64,640]{1,0:T(8,128)(2,1)S(1)}, bf16[64,640]{1,0:T(8,128)(2,1)S(1)}, u32[]{:S(2)}, u32[]{:S(2)}) collective-permute-start(bf16[64,640]{1,0:T(8,128)(2,1)S(1)} %pad_maximum_fusion.13), channel_id=1, source_target_pairs={{0,1},{1,0},{2,3},{3,2},{4,5},{5,4},{6,7},{7,6},{8,9},{9,8},{10,11... | collective-permute-start | bytes 245768 | tf_op jit(solution)/shard_map/ppermute | solution.py:67
  24.0 0.4 %collective-permute-done.9 = f32[8,128]{1,0:T(8,128)S(1)} collective-permute-done((f32[8,128]{1,0:T(8,128)S(1)}, f32[8,128]{1,0:T(8,128)S(1)}, u32[]{:S(2)}, u32[]{:S(2)}) %collective-permute-start.9) | collective-permute-done | bytes 4128 | tf_op jit(solution)/shard_map/ppermute | solution.py:67
  24.4 0.9 %collective-permute-start.11 = (f32[8,128]{1,0:T(8,128)S(1)}, f32[8,128]{1,0:T(8,128)S(1)}, u32[]{:S(2)}, u32[]{:S(2)}) collective-permute-start(f32[8,128]{1,0:T(8,128)S(1)} %pad_maximum_fusion.15), channel_id=1, source_target_pairs={{19,0},{25,1},{7,30},{13,31},{12,8},{24,9},{6,22},{15,23},{18,2},{... | collective-permute-start | bytes 12296 | tf_op jit(solution)/shard_map/ppermute | solution.py:182
  25.3 1.8 %collective-permute-start.10 = (f32[8,128]{1,0:T(8,128)S(1)}, f32[8,128]{1,0:T(8,128)S(1)}, u32[]{:S(2)}, u32[]{:S(2)}) collective-permute-start(f32[8,128]{1,0:T(8,128)S(1)} %pad_maximum_fusion.15), channel_id=1, source_target_pairs={{19,1},{25,0},{7,31},{13,30},{12,9},{24,8},{6,23},{15,22},{18,3},{... | collective-permute-start | bytes 12296 | tf_op jit(solution)/shard_map/ppermute | solution.py:181
  27.1 0.1 fusion.33
  27.2 0.2 fusion.31
  27.4 0.3 fusion.30
  27.8 0.7 %multiply_convert_fusion.1 = bf16[8,2048]{1,0:T(8,128)(2,1)} fusion(f32[64,2048]{1,0:T(8,128)S(1)} %get-tuple-element.88, s32[]{:T(128)S(6)} %select_n.240, s32[]{:T(128)S(6)} %select_n.241, bf16[64,2048]{1,0:T(8,128)(2,1)S(1)} %get-tuple-element.43, bf16[16,2048]{1,0:T(8,128)(2,1)S(1)} %pad_maximum_fusion.14, f32[2048]{0:T(1024)S(1)} %broadcast_multiply_fusion, ...), kind=kLoop, calls=%fused_computation.51 | loop fusion | flops 196608 | bytes 450569 | tf_op jit(solution)/shard_map/convert_element_type | solution.py:292
  28.4 0.7 %multiply_convert_fusion = bf16[16,1024]{1,0:T(8,128)(2,1)} fusion(f32[64,1024]{1,0:T(8,128)S(1)} %get-tuple-element.89, s32[]{:T(128)S(6)} %select_n.229, s32[]{:T(128)S(6)} %select_n.249, bf16[64,1024]{1,0:T(8,128)(2,1)S(1)} %slice_select_fusion, bf16[16,512]{1,0:T(8,128)(2,1)S(1)} %get-tuple-element.76, bf16[16,512]{1,0:T(8,128)(2,1)S(1)} %get-tuple-element.77, ...), kind=kLoop, calls=%fused_computation.50 | loop fusion | flops 327680 | bytes 307209 | tf_op jit(solution)/shard_map/convert_element_type | solution.py:292
  29.1 0.1 fusion.22
  29.2 0.6 %add_reduce_fusion = f32[]{:T(128)} fusion(f32[128]{0:T(128)S(1)} %pad.24, f32[128]{0:T(128)S(1)} %select_reduce_fusion), kind=kLoop, calls=%fused_computation.115 | loop fusion | flops 383 | bytes 1028 | tf_op jit(solution)/shard_map/reduce_sum | solution.py:307
  (62 shorter events, 1.6 us)
Async XLA Ops:
  0.6 1.6 %collective-permute-start = (bf16[8,2048]{1,0:T(8,128)(2,1)}, bf16[8,2048]{1,0:T(8,128)(2,1)S(1)}, u32[]{:S(2)}, u32[]{:S(2)}) collective-permute-start(bf16[8,2048]{1,0:T(8,128)(2,1)} %param.2), channel_id=1, source_target_pairs={{0,1},{1,0},{2,3},{3,2},{4,5},{5,4},{6,7},{7,6},{8,9},{9,8},{10,11... | collective-permute-start | bytes 98312 | tf_op jit(solution)/shard_map/ppermute | solution.py:67
  1.1 1.4 %collective-permute-start.1 = (bf16[16,1024]{1,0:T(8,128)(2,1)}, bf16[16,1024]{1,0:T(8,128)(2,1)S(1)}, u32[]{:S(2)}, u32[]{:S(2)}) collective-permute-start(bf16[16,1024]{1,0:T(8,128)(2,1)} %param.3), channel_id=1, source_target_pairs={{0,1},{1,0},{2,3},{3,2},{4,5},{5,4},{6,7},{7,6},{8,9},{9,8},{10,11... | collective-permute-start | bytes 98312 | tf_op jit(solution)/shard_map/ppermute | solution.py:67
  1.3 1.3 %copy-start.1 = (bf16[8,2048]{1,0:T(8,128)(2,1)S(1)}, bf16[8,2048]{1,0:T(8,128)(2,1)}, u32[]{:S(2)}) copy-start(bf16[8,2048]{1,0:T(8,128)(2,1)} %param.2) | copy-start | bytes 98308
  1.3 1.3 %copy-start = (bf16[16,1024]{1,0:T(8,128)(2,1)S(1)}, bf16[16,1024]{1,0:T(8,128)(2,1)}, u32[]{:S(2)}) copy-start(bf16[16,1024]{1,0:T(8,128)(2,1)} %param.3) | copy-start | bytes 98308
  2.6 7.2 %collective-permute-start.2 = (bf16[16,2048]{1,0:T(8,128)(2,1)S(1)}, bf16[16,2048]{1,0:T(8,128)(2,1)S(1)}, u32[]{:S(2)}, u32[]{:S(2)}) collective-permute-start(bf16[16,2048]{1,0:T(8,128)(2,1)S(1)} %get-tuple-element.49), channel_id=1, source_target_pairs={{0,6},{1,25},{2,4},{3,27},{4,2},{5,29},{6,0},{7,31},{8,14},{9,17},... | collective-permute-start | bytes 196616 | tf_op jit(solution)/shard_map/ppermute | solution.py:76
  7.4 5.2 %collective-permute-start.3 = (bf16[16,2048]{1,0:T(8,128)(2,1)S(1)}, bf16[16,2048]{1,0:T(8,128)(2,1)S(1)}, u32[]{:S(2)}, u32[]{:S(2)}) collective-permute-start(bf16[16,2048]{1,0:T(8,128)(2,1)S(1)} %get-tuple-element.50), channel_id=1, source_target_pairs={{0,4},{1,17},{2,6},{3,19},{4,0},{5,21},{6,2},{7,23},{8,12},{9,25},... | collective-permute-start | bytes 196616 | tf_op jit(solution)/shard_map/ppermute | solution.py:76
  7.4 5.2 %collective-permute-start.4 = (bf16[16,2048]{1,0:T(8,128)(2,1)S(1)}, bf16[16,2048]{1,0:T(8,128)(2,1)S(1)}, u32[]{:S(2)}, u32[]{:S(2)}) collective-permute-start(bf16[16,2048]{1,0:T(8,128)(2,1)S(1)} %get-tuple-element.51), channel_id=1, source_target_pairs={{0,2},{1,9},{2,0},{3,11},{4,6},{5,13},{6,4},{7,15},{8,10},{9,1},{1... | collective-permute-start | bytes 196616 | tf_op jit(solution)/shard_map/ppermute | solution.py:76
  12.7 1.6 %collective-permute-start.5 = (bf16[64,2048]{1,0:T(8,128)(2,1)S(1)}, bf16[64,2048]{1,0:T(8,128)(2,1)S(1)}, u32[]{:S(2)}, u32[]{:S(2)}) collective-permute-start(bf16[64,2048]{1,0:T(8,128)(2,1)S(1)} %get-tuple-element.48), channel_id=1, source_target_pairs={{0,1},{1,0},{2,3},{3,2},{4,5},{5,4},{6,7},{7,6},{8,9},{9,8},{10,11... | collective-permute-start | bytes 786440 | tf_op jit(solution)/shard_map/ppermute | solution.py:67
  15.4 5.3 %collective-permute-start.8 = (bf16[64,640]{1,0:T(8,128)(2,1)S(1)}, bf16[64,640]{1,0:T(8,128)(2,1)S(1)}, u32[]{:S(2)}, u32[]{:S(2)}) collective-permute-start(bf16[64,640]{1,0:T(8,128)(2,1)S(1)} %pad_maximum_fusion.6), channel_id=1, source_target_pairs={{0,24},{1,7},{2,26},{3,5},{4,28},{5,3},{6,30},{7,1},{8,16},{9,15},... | collective-permute-start | bytes 245768 | tf_op jit(solution)/shard_map/ppermute | solution.py:85
  17.9 4.4 %collective-permute-start.6 = (bf16[64,640]{1,0:T(8,128)(2,1)S(1)}, bf16[64,640]{1,0:T(8,128)(2,1)S(1)}, u32[]{:S(2)}, u32[]{:S(2)}) collective-permute-start(bf16[64,640]{1,0:T(8,128)(2,1)S(1)} %pad_maximum_fusion.7), channel_id=1, source_target_pairs={{0,8},{1,3},{2,10},{3,1},{4,12},{5,7},{6,14},{7,5},{8,0},{9,11},{1... | collective-permute-start | bytes 245768 | tf_op jit(solution)/shard_map/ppermute | solution.py:85
  18.4 4.4 %collective-permute-start.7 = (bf16[64,640]{1,0:T(8,128)(2,1)S(1)}, bf16[64,640]{1,0:T(8,128)(2,1)S(1)}, u32[]{:S(2)}, u32[]{:S(2)}) collective-permute-start(bf16[64,640]{1,0:T(8,128)(2,1)S(1)} %pad_maximum_fusion.8), channel_id=1, source_target_pairs={{0,16},{1,5},{2,18},{3,7},{4,20},{5,1},{6,22},{7,3},{8,24},{9,13},... | collective-permute-start | bytes 245768 | tf_op jit(solution)/shard_map/ppermute | solution.py:85
  23.2 1.2 %collective-permute-start.9 = (f32[8,128]{1,0:T(8,128)S(1)}, f32[8,128]{1,0:T(8,128)S(1)}, u32[]{:S(2)}, u32[]{:S(2)}) collective-permute-start(f32[8,128]{1,0:T(8,128)S(1)} %select_select_fusion), channel_id=1, source_target_pairs={{0,1},{1,0},{2,3},{3,2},{4,5},{5,4},{6,7},{7,6},{8,9},{9,8},{10,11... | collective-permute-start | bytes 12296 | tf_op jit(solution)/shard_map/ppermute | solution.py:67
  23.5 3.6 %collective-permute-start.12 = (bf16[64,640]{1,0:T(8,128)(2,1)S(1)}, bf16[64,640]{1,0:T(8,128)(2,1)S(1)}, u32[]{:S(2)}, u32[]{:S(2)}) collective-permute-start(bf16[64,640]{1,0:T(8,128)(2,1)S(1)} %pad_maximum_fusion.13), channel_id=1, source_target_pairs={{0,1},{1,0},{2,3},{3,2},{4,5},{5,4},{6,7},{7,6},{8,9},{9,8},{10,11... | collective-permute-start | bytes 245768 | tf_op jit(solution)/shard_map/ppermute | solution.py:67
  24.4 4.8 %collective-permute-start.11 = (f32[8,128]{1,0:T(8,128)S(1)}, f32[8,128]{1,0:T(8,128)S(1)}, u32[]{:S(2)}, u32[]{:S(2)}) collective-permute-start(f32[8,128]{1,0:T(8,128)S(1)} %pad_maximum_fusion.15), channel_id=1, source_target_pairs={{19,0},{25,1},{7,30},{13,31},{12,8},{24,9},{6,22},{15,23},{18,2},{... | collective-permute-start | bytes 12296 | tf_op jit(solution)/shard_map/ppermute | solution.py:182
  25.3 3.9 %collective-permute-start.10 = (f32[8,128]{1,0:T(8,128)S(1)}, f32[8,128]{1,0:T(8,128)S(1)}, u32[]{:S(2)}, u32[]{:S(2)}) collective-permute-start(f32[8,128]{1,0:T(8,128)S(1)} %pad_maximum_fusion.15), channel_id=1, source_target_pairs={{19,1},{25,0},{7,31},{13,30},{12,9},{24,8},{6,23},{15,22},{18,3},{... | collective-permute-start | bytes 12296 | tf_op jit(solution)/shard_map/ppermute | solution.py:181
